TPU v7x, 32 devices: a whole 2x2x4 slice. The times are simulated.
32 devices in a mesh: slab: 2 (over x), chan: 16 (over z, y, core).
Axes of the slice: x: 2, y: 2, z: 4, core: 2. Of those that a mesh axis runs over, the one named last changes fastest.
Arguments:
- cube: float32 [128, 128, 256], P(('slab', 'chan')), parts along dimension 0, may hold values from -8 to 8
- multipliers: int32 [6, 4], replicated, may hold values from 1 to 5
- noise_code: int32 [128, 6, 4], P(('slab', 'chan')), parts along dimension 0, may hold values from 16 to 511
Outputs:
- denoised: float32 [128, 128, 256], P(('slab', 'chan')), parts along dimension 0
There are 2 independent parts, one for each index of `slab`. A program takes and returns all parts, laid end to end along the dimension named above; an argument that names none is the same for every part. Nothing has to cross between parts.
All inputs are finite; a program needn't handle non-finite values.
Results may differ from a plain program's by a relative error of at most 0.00002.
Values sent between devices are 32-bit elements; how exact they have to be, the bound alone decides.
No kernel may reach another device: no remote copies, remote signals or barrier semaphores. Data moves between devices by JAX's collectives and lax.ppermute only.
A program may use at most 64 MiB of HBM per device.

v0:
```python
import jax
import jax.numpy as jnp
from jax import lax
from jax.sharding import PartitionSpec as P

SCALES_XY = 5
SCALES_NU = 3


SPLINE = (0.0625, 0.25, 0.375, 0.25, 0.0625)
level_step = 1.0 / 1024.0


def shifted(value, axis, steps):
    count = lax.axis_size(axis)
    leading, last = (max(0, -steps), min(count, count - steps))
    return lax.ppermute(value, axis, [(source, source + steps) for source in range(leading, last)])


def taps(padded, axis, step, length):
    total = jnp.zeros(padded.shape[:axis] + (length,) + padded.shape[axis + 1 :], jnp.float32)
    for place, weight in enumerate(SPLINE):
        total = total + weight * lax.slice_in_dim(
            padded, place * step, place * step + length, axis=axis
        )
    return total


def smooth(field, axis, step):
    widths = [(0, 0)] * field.ndim
    widths[axis] = (2 * step, 2 * step)
    return taps(jnp.pad(field, widths), axis, step, field.shape[axis])


def spread(field, reach):
    local = field.shape[1]
    below = []
    above = []
    distance = 1
    while (distance - 1) * local < reach:
        count = min(local, reach - (distance - 1) * local)
        below.insert(0, shifted(field[:, local - count :], "chan", distance))
        above.append(shifted(field[:, :count], "chan", -distance))
        distance += 1
    return jnp.concatenate(below + [field] + above, axis=1)


def spectral_split(stack):
    parts = []
    current = stack
    for s in range(SCALES_NU):
        step = 2**s
        padded = spread(current, 2 * step)
        coarse = taps(padded, 1, step, current.shape[1])
        parts.append(current - coarse)
        current = coarse
    parts.append(current)
    return parts


def spatial_split(field):
    bands = []
    smoothed = field
    rows_axis = field.ndim - 2
    for j in range(SCALES_XY):
        step = 2**j
        following = smooth(smooth(smoothed, rows_axis, step), rows_axis + 1, step)
        bands.append(smoothed - following)
        smoothed = following
    bands.append(smoothed)
    return bands


def per_device(cube, multipliers, noise_code):
    level = multipliers.astype(jnp.float32)[None] * noise_code.astype(jnp.float32) * level_step
    spatial = jnp.stack(spatial_split(cube))
    spectral = spectral_split(spatial)
    bands = [[spectral[s][j] for s in range(SCALES_NU + 1)] for j in range(SCALES_XY + 1)]
    total = jnp.zeros(cube.shape, jnp.float32)
    for j in range(SCALES_XY + 1):
        for s in range(SCALES_NU + 1):
            value = bands[j][s]
            if j == SCALES_XY and s == SCALES_NU:
                total = total + value
            else:
                limit = level[:, j, s][:, None, None]
                total = total + (value - jnp.clip(value, -limit, limit))
    return total


def solution(mesh):
    placed = (P(("slab", "chan"), None, None), P(), P(("slab", "chan"), None, None))
    return jax.shard_map(
        per_device,
        mesh=mesh,
        in_specs=placed,
        out_specs=P(("slab", "chan"), None, None),
        check_vma=False,
    )
```

profile of v0, /device:TPU:12, one launch (start us, length us, event | category | flops | bytes accessed | tf_op | source)
XLA Modules:
  0.0 372.2 jit_solution(6464806998544068454)
XLA Ops:
  0.0 2.2 multiply_add_fusion.2
  2.2 1.7 bitcast_dynamic-update-slice_fusion.5
  3.9 0.2 multiply_add_fusion.1
  4.1 0.6 bitcast_dynamic-update-slice_fusion.4
  4.8 0.2 fusion.20
  4.9 0.6 bitcast_dynamic-update-slice_fusion.3
  5.7 0.6 bitcast_dynamic-update-slice_fusion.2
  6.3 0.1 fusion.68
  6.4 0.6 bitcast_dynamic-update-slice_fusion.1
  7.0 0.3 fusion.93
  7.4 1.9 collective-permute-start
  9.3 3.6 collective-permute-start.1
  12.9 33.0 %collective-permute-done = f32[6,2,128,256]{3,2,1,0:T(8,128)S(1)} collective-permute-done((f32[6,2,128,256]{3,2,1,0:T(8,128)S(1)}, f32[6,2,128,256]{3,2,1,0:T(8,128)S(1)}, u32[]{:S(2)}, u32[]{:S(2)}) %collective-permute-start) | collective-permute-done | bytes 1572896 | tf_op jit(solution)/shard_map/ppermute | solution.py:17
  45.9 32.6 %collective-permute-done.1 = f32[6,2,128,256]{3,2,1,0:T(8,128)S(1)} collective-permute-done((f32[6,2,128,256]{3,2,1,0:T(8,128)S(1)}, f32[6,2,128,256]{3,2,1,0:T(8,128)S(1)}, u32[]{:S(2)}, u32[]{:S(2)}) %collective-permute-start.1) | collective-permute-done | bytes 1572896 | tf_op jit(solution)/shard_map/ppermute | solution.py:17
  78.6 1.1 fusion.83
  79.7 1.9 collective-permute-start.2
  81.7 3.8 %collective-permute-start.3 = (f32[6,4,128,256]{3,2,1,0:T(8,128)S(1)}, f32[6,4,128,256]{3,2,1,0:T(8,128)S(1)}, u32[]{:S(2)}, u32[]{:S(2)}) collective-permute-start(f32[6,4,128,256]{3,2,1,0:T(8,128)S(1)} %get-tuple-element.52), channel_id=1, source_target_pairs={{1,0},{2,1},{3,2},{4,3},{5,4},{6,5},{7,6},{8,7},{9,8},{10,9},{11,1... | collective-permute-start | bytes 9437192 | tf_op jit(solution)/shard_map/ppermute | solution.py:17
  85.5 66.7 %collective-permute-done.2 = f32[6,4,128,256]{3,2,1,0:T(8,128)S(1)} collective-permute-done((f32[6,4,128,256]{3,2,1,0:T(8,128)S(1)}, f32[6,4,128,256]{3,2,1,0:T(8,128)S(1)}, u32[]{:S(2)}, u32[]{:S(2)}) %collective-permute-start.2) | collective-permute-done | bytes 3145760 | tf_op jit(solution)/shard_map/ppermute | solution.py:17
  152.2 1.3 fusion.85
  153.5 1.9 collective-permute-start.4
  155.4 36.0 %collective-permute-start.5 = (f32[6,4,128,256]{3,2,1,0:T(8,128)S(1)}, f32[6,4,128,256]{3,2,1,0:T(8,128)S(1)}, u32[]{:S(2)}, u32[]{:S(2)}) collective-permute-start(f32[6,4,128,256]{3,2,1,0:T(8,128)S(1)} %get-tuple-element.54), channel_id=1, source_target_pairs={{0,1},{1,2},{2,3},{3,4},{4,5},{5,6},{6,7},{7,8},{8,9},{9,10},{10,1... | collective-permute-start | bytes 9437192 | tf_op jit(solution)/shard_map/ppermute | solution.py:17
  191.4 1.9 collective-permute-start.6
  193.4 1.9 collective-permute-start.7
  195.3 0.2 slice_reduce_fusion.20
  195.5 0.3 slice_reduce_fusion.21
  195.9 0.3 slice_reduce_fusion.22
  196.1 131.4 %collective-permute-done.4 = f32[6,4,128,256]{3,2,1,0:T(8,128)S(1)} collective-permute-done((f32[6,4,128,256]{3,2,1,0:T(8,128)S(1)}, f32[6,4,128,256]{3,2,1,0:T(8,128)S(1)}, u32[]{:S(2)}, u32[]{:S(2)}) %collective-permute-start.4) | collective-permute-done | bytes 3145760 | tf_op jit(solution)/shard_map/ppermute | solution.py:17
  327.6 30.6 %collective-permute-done.5 = f32[6,4,128,256]{3,2,1,0:T(8,128)S(1)} collective-permute-done((f32[6,4,128,256]{3,2,1,0:T(8,128)S(1)}, f32[6,4,128,256]{3,2,1,0:T(8,128)S(1)}, u32[]{:S(2)}, u32[]{:S(2)}) %collective-permute-start.5) | collective-permute-done | bytes 3145760 | tf_op jit(solution)/shard_map/ppermute | solution.py:17
  358.2 1.6 copy-done.2
  359.8 1.7 copy-done.3
  361.5 7.7 %fusion.87 = (f32[6,4,128,256]{3,2,1,0:T(8,128)S(1)}, f32[6,4,128,256]{3,2,1,0:T(8,128)S(1)}) fusion(f32[6,4,128,256]{3,2,1,0:T(8,128)} %copy-done, f32[6,4,128,256]{3,2,1,0:T(8,128)} %collective-permute-done.7, f32[6,4,128,256]{3,2,1,0:T(8,128)} %copy-done.3, f32[6,4,128,256]{3,2,1,0:T(8,128)} %copy-done.2, f32[6,4,128,256]{3,2,1,0:T(8,128)} %copy-done.1), kind=kLoop, calls=%fused_computation.207 | loop fusion | flops 7864320 | bytes 22020096 | tf_op jit(solution)/shard_map/sub | solution.py:55
  369.2 3.0 fusion.80
  (17 shorter events, 0.2 us)
Async XLA Ops:
  7.4 38.6 %collective-permute-start = (f32[6,2,128,256]{3,2,1,0:T(8,128)S(1)}, f32[6,2,128,256]{3,2,1,0:T(8,128)S(1)}, u32[]{:S(2)}, u32[]{:S(2)}) collective-permute-start(f32[6,2,128,256]{3,2,1,0:T(8,128)S(1)} %get-tuple-element.67), channel_id=1, source_target_pairs={{0,1},{1,2},{2,3},{3,4},{4,5},{5,6},{6,7},{7,8},{8,9},{9,10},{10,1... | collective-permute-start | bytes 4718600 | tf_op jit(solution)/shard_map/ppermute | solution.py:17
  9.3 69.3 %collective-permute-start.1 = (f32[6,2,128,256]{3,2,1,0:T(8,128)S(1)}, f32[6,2,128,256]{3,2,1,0:T(8,128)S(1)}, u32[]{:S(2)}, u32[]{:S(2)}) collective-permute-start(f32[6,2,128,256]{3,2,1,0:T(8,128)S(1)} %get-tuple-element.68), channel_id=1, source_target_pairs={{1,0},{2,1},{3,2},{4,3},{5,4},{6,5},{7,6},{8,7},{9,8},{10,9},{11,1... | collective-permute-start | bytes 4718600 | tf_op jit(solution)/shard_map/ppermute | solution.py:17
  79.7 115.6 %copy-start.5 = (s32[6,4]{0,1:T(4,128)S(1)}, s32[6,4]{0,1:T(4,128)}, u32[]{:S(2)}) copy-start(s32[6,4]{0,1:T(4,128)} %param.4) | copy-start | bytes 292
  79.7 115.6 %copy-start.4 = (s32[4,6,4]{1,2,0:T(4,128)S(1)}, s32[4,6,4]{1,2,0:T(4,128)}, u32[]{:S(2)}) copy-start(s32[4,6,4]{1,2,0:T(4,128)} %param.5) | copy-start | bytes 1156
  79.7 72.5 %collective-permute-start.2 = (f32[6,4,128,256]{3,2,1,0:T(8,128)S(1)}, f32[6,4,128,256]{3,2,1,0:T(8,128)S(1)}, u32[]{:S(2)}, u32[]{:S(2)}) collective-permute-start(f32[6,4,128,256]{3,2,1,0:T(8,128)S(1)} %get-tuple-element.52), channel_id=1, source_target_pairs={{0,1},{1,2},{2,3},{3,4},{4,5},{5,6},{6,7},{7,8},{8,9},{9,10},{10,1... | collective-permute-start | bytes 9437192 | tf_op jit(solution)/shard_map/ppermute | solution.py:17
  81.7 70.5 %collective-permute-start.3 = (f32[6,4,128,256]{3,2,1,0:T(8,128)S(1)}, f32[6,4,128,256]{3,2,1,0:T(8,128)S(1)}, u32[]{:S(2)}, u32[]{:S(2)}) collective-permute-start(f32[6,4,128,256]{3,2,1,0:T(8,128)S(1)} %get-tuple-element.52), channel_id=1, source_target_pairs={{1,0},{2,1},{3,2},{4,3},{5,4},{6,5},{7,6},{8,7},{9,8},{10,9},{11,1... | collective-permute-start | bytes 9437192 | tf_op jit(solution)/shard_map/ppermute | solution.py:17
  153.5 204.7 %copy-start = (f32[6,4,128,256]{3,2,1,0:T(8,128)}, f32[6,4,128,256]{3,2,1,0:T(8,128)S(1)}, u32[]{:S(2)}) copy-start(f32[6,4,128,256]{3,2,1,0:T(8,128)S(1)} %get-tuple-element.54) | copy-start | bytes 9437188
  153.5 174.1 %collective-permute-start.4 = (f32[6,4,128,256]{3,2,1,0:T(8,128)S(1)}, f32[6,4,128,256]{3,2,1,0:T(8,128)S(1)}, u32[]{:S(2)}, u32[]{:S(2)}) collective-permute-start(f32[6,4,128,256]{3,2,1,0:T(8,128)S(1)} %get-tuple-element.54), channel_id=1, source_target_pairs={{0,2},{1,3},{2,4},{3,5},{4,6},{5,7},{6,8},{7,9},{8,10},{9,11},{10,... | collective-permute-start | bytes 9437192 | tf_op jit(solution)/shard_map/ppermute | solution.py:17
  155.4 202.7 %collective-permute-start.5 = (f32[6,4,128,256]{3,2,1,0:T(8,128)S(1)}, f32[6,4,128,256]{3,2,1,0:T(8,128)S(1)}, u32[]{:S(2)}, u32[]{:S(2)}) collective-permute-start(f32[6,4,128,256]{3,2,1,0:T(8,128)S(1)} %get-tuple-element.54), channel_id=1, source_target_pairs={{0,1},{1,2},{2,3},{3,4},{4,5},{5,6},{6,7},{7,8},{8,9},{9,10},{10,1... | collective-permute-start | bytes 9437192 | tf_op jit(solution)/shard_map/ppermute | solution.py:17
  191.4 166.7 %collective-permute-start.6 = (f32[6,4,128,256]{3,2,1,0:T(8,128)S(1)}, f32[6,4,128,256]{3,2,1,0:T(8,128)S(1)}, u32[]{:S(2)}, u32[]{:S(2)}) collective-permute-start(f32[6,4,128,256]{3,2,1,0:T(8,128)S(1)} %get-tuple-element.54), channel_id=1, source_target_pairs={{1,0},{2,1},{3,2},{4,3},{5,4},{6,5},{7,6},{8,7},{9,8},{10,9},{11,1... | collective-permute-start | bytes 9437192 | tf_op jit(solution)/shard_map/ppermute | solution.py:17
  193.4 168.1 %collective-permute-start.7 = (f32[6,4,128,256]{3,2,1,0:T(8,128)S(1)}, f32[6,4,128,256]{3,2,1,0:T(8,128)}, u32[]{:S(2)}, u32[]{:S(2)}) collective-permute-start(f32[6,4,128,256]{3,2,1,0:T(8,128)S(1)} %get-tuple-element.54), channel_id=1, source_target_pairs={{2,0},{3,1},{4,2},{5,3},{6,4},{7,5},{8,6},{9,7},{10,8},{11,9},{12,... | collective-permute-start | bytes 9437192 | tf_op jit(solution)/shard_map/ppermute | solution.py:17
  327.6 30.6 %copy-start.1 = (f32[6,4,128,256]{3,2,1,0:T(8,128)}, f32[6,4,128,256]{3,2,1,0:T(8,128)S(1)}, u32[]{:S(2)}) copy-start(f32[6,4,128,256]{3,2,1,0:T(8,128)S(1)} %collective-permute-done.4) | copy-start | bytes 9437188
  358.2 1.6 copy-start.2
  359.8 1.7 copy-start.3
where the time goes:
time: 373 us; the launch traced here: 372 us
  waiting for transfers between devices  294 us (79%)
  starting transfers between devices  53.1 us (14%)
  other arithmetic  20.7 us (6%)
  local copies, waits for them, and re-layouts  3.85 us (1%)
    ppermute x8, waiting for transfers between devices, shifted(): lax.ppermute(value, axis, [(source, source + steps) for source in range(l...  294 us
    ppermute x8, starting transfers between devices, shifted(): lax.ppermute(value, axis, [(source, source + steps) for source in range(l...  53.1 us
    sub x3, other arithmetic, spectral_split(): parts.append(current - coarse)  10.2 us
  transfers between devices with their start and end apart: 8, of which 5 were waited for; matrix products, arithmetic and copies ran while one was open for 0% of the time, Pallas kernels for 0%

commit v1 on v0

v1 whole, which is shorter than its diff:
```python
import functools

import jax
import jax.numpy as jnp
import numpy as np
from jax import lax
from jax.experimental import pallas as pl
from jax.experimental.pallas import tpu as pltpu
from jax.sharding import PartitionSpec as P

SCALES_XY = 5
SCALES_NU = 3
TAPS = (1, 4, 6, 4, 1)
REACH = 14
F32 = jnp.float32
BF16 = jnp.bfloat16


def pairs(count, distance, phase):
    out = []
    for i in range(count):
        j = i + distance if (i // distance) % 2 == phase else i - distance
        if 0 <= j < count:
            out.append((i, j))
    return out


def column_matrices(cols):
    place = np.arange(cols)
    offset = place[None, :] - place[:, None]
    mats = []
    for j in range(SCALES_XY):
        m = np.zeros((cols, cols), np.float32)
        for k, w in enumerate(TAPS):
            m += np.where(offset == (k - 2) * 2**j, np.float32(w / 256.0), np.float32(0))
        mats.append(m)
    return jnp.asarray(np.stack(mats), BF16)


def prep_kernel(half, core_ref, cube, got, v8, za, zb, sem):
    core = core_ref[0]
    mine = cube.at[:, pl.ds(pl.multiple_of(core * half, half), half)]

    def move(dst, k, which):
        block = k // 2
        part = pl.ds((k % 2) * 2, 2)

        @pl.when(core == block)
        def _():
            pltpu.make_async_copy(mine.at[part], dst, sem.at[which]).start()

        @pl.when(core != block)
        def _():
            pltpu.make_async_copy(got.at[part], dst, sem.at[which]).start()

    n = 0
    ends = []
    for k in range(4):
        move(v8.at[pl.ds(2 * k, 2)], k, n)
        ends.append((v8.at[pl.ds(2 * k, 2)], n))
        n += 1
    for z, first in ((za, core_ref[1]), (zb, core_ref[2])):
        for k in range(3):
            dst = z.at[pl.ds(2 * k, 2)]
            move(dst, first + k, n)
            ends.append((dst, n))
            n += 1
    for dst, which in ends:
        pltpu.make_async_copy(got.at[pl.ds(0, 2)], dst, sem.at[which]).wait()


def b3(a, b, c, d, e):
    return 0.375 * c + 0.25 * (b + d) + 0.0625 * (a + e)


def spectral_kernel(half, cols, place_ref, v8, e2, o2, e4, o4, own, other, ext, sem):
    chip = 8
    copies = [
        pltpu.make_async_copy(v8, ext.at[pl.ds(REACH, chip)], sem.at[0]),
        pltpu.make_async_copy(e2, ext.at[pl.ds(place_ref[1], chip)], sem.at[1]),
        pltpu.make_async_copy(o2, ext.at[pl.ds(place_ref[2], chip)], sem.at[2]),
        pltpu.make_async_copy(e4, ext.at[pl.ds(place_ref[3], 6)], sem.at[3]),
        pltpu.make_async_copy(o4, ext.at[pl.ds(place_ref[4], 6)], sem.at[4]),
    ]
    for c in copies:
        c.start()
    for c in copies:
        c.wait()
    core = place_ref[0]
    first = place_ref[5]
    channels = place_ref[6]
    inside = {}
    for k in range(-12, 20):
        if k < 0 or k >= chip:
            at = first + k
            inside[k] = jnp.where((at >= 0) & (at < channels), 1.0, 0.0).astype(F32)

    def body(r, carry):
        rows = pl.ds(pl.multiple_of(r * 8, 8), 8)
        for half_cols in range(cols // 128):
            lanes = pl.ds(half_cols * 128, 128)
            x = {k: ext[k + REACH, rows, lanes] for k in range(-14, 22)}

            def smooth(v, lo, hi, step):
                out = {}
                for k in range(lo, hi):
                    y = b3(*(v[k + o * step] for o in (-2, -1, 0, 1, 2)))
                    out[k] = y * inside[k] if k in inside else y
                return out

            c1 = smooth(x, -12, 20, 1)
            c2 = smooth(c1, -8, 16, 2)
            c3 = smooth(c2, 0, 8, 4)
            for s, c in enumerate((c1, c2, c3)):
                for k in range(4):
                    a, b = c[k], c[k + 4]
                    own[s, k, rows, lanes] = jnp.where(core == 0, a, b)
                    other[s, k, rows, lanes] = jnp.where(core == 0, b, a)
        return carry

    lax.fori_loop(0, half // 8, body, 0)


def spatial_kernel(rows, cols, core_ref, mult, noise, cube, own, got, mats, out, a, p, acc):
    i = pl.program_id(0)
    half = rows // 2
    pad = 2 ** SCALES_XY
    core = core_ref[0]
    mine_at = pl.multiple_of(core * half, half)
    got_at = pl.multiple_of((1 - core) * half, half)

    @pl.when(i == 0)
    def _():
        p[:, :pad] = jnp.zeros((4, pad, cols), F32)
        p[:, pad + rows :] = jnp.zeros((4, pad, cols), F32)

    a[3, pl.ds(mine_at, half)] = own[2, 0]
    a[3, pl.ds(got_at, half)] = got[2, 0]
    for s in (1, 2):
        a[s, pl.ds(mine_at, half)] = own[s - 1, 0] - own[s, 0]
        a[s, pl.ds(got_at, half)] = got[s - 1, 0] - got[s, 0]
    a[0, pl.ds(mine_at, half)] = cube[0, pl.ds(mine_at, half)] - own[0, 0]
    a[0, pl.ds(got_at, half)] = cube[0, pl.ds(got_at, half)] - got[0, 0]

    chunk = 32

    def limit(j, s):
        return (mult[j, s] * noise[i, j, s]).astype(F32) * (1.0 / 1024.0)

    for j in range(SCALES_XY):
        d = 2**j
        w = mats[j]
        for s in range(4):
            x = a[s]
            hi = x.astype(BF16)
            lo = (x - hi.astype(F32)).astype(BF16)
            p[s, pl.ds(pad, rows)] = jnp.dot(hi, w, preferred_element_type=F32) + jnp.dot(lo, w, preferred_element_type=F32)
        for r in range(0, rows, chunk):
            total = None
            for s in range(4):
                at = pad + r
                c0 = p[s, pl.ds(at, chunk)]
                c1 = p[s, pl.ds(at - d, chunk)] + p[s, pl.ds(at + d, chunk)]
                c2 = p[s, pl.ds(at - 2 * d, chunk)] + p[s, pl.ds(at + 2 * d, chunk)]
                nxt = 6.0 * c0 + 4.0 * c1 + c2
                b = a[s, pl.ds(r, chunk)] - nxt
                a[s, pl.ds(r, chunk)] = nxt
                lim = limit(j, s)
                v = b - jnp.clip(b, -lim, lim)
                total = v if total is None else total + v
            if j == 0:
                acc[pl.ds(r, chunk)] = total
            else:
                acc[pl.ds(r, chunk)] += total
    for r in range(0, rows, chunk):
        total = acc[pl.ds(r, chunk)] + a[3, pl.ds(r, chunk)]
        for s in range(3):
            b = a[s, pl.ds(r, chunk)]
            lim = limit(SCALES_XY, s)
            total = total + (b - jnp.clip(b, -lim, lim))
        out[0, pl.ds(r, chunk)] = total


def per_device(count, cube, multipliers, noise_code):
    local, rows, cols = cube.shape
    assert local == 4 and count % 2 == 0 and rows % 128 == 0
    half = rows // 2
    chip = 2 * local
    me = lax.axis_index("chan").astype(jnp.int32)
    core = me % 2
    g2 = (me // 2) % 2
    g4 = (me // 4) % 2

    def permute(v, distance, phase):
        return lax.ppermute(v, "chan", pairs(count, distance, phase))

    smem = pl.BlockSpec(memory_space=pltpu.SMEM)
    anyspace = pl.BlockSpec(memory_space=pl.ANY)
    vmem = pl.BlockSpec(memory_space=pltpu.VMEM)
    got = permute(lax.dynamic_slice_in_dim(cube, (1 - core) * half, half, 1), 1, 0)
    prep_at = jnp.stack([core, 1 - g4, g4])
    v8, za, zb = pl.pallas_call(
        functools.partial(prep_kernel, half),
        in_specs=[smem, anyspace, anyspace],
        out_specs=[anyspace] * 3,
        out_shape=[jax.ShapeDtypeStruct((n, half, cols), F32) for n in (chip, 6, 6)],
        scratch_shapes=[pltpu.SemaphoreType.DMA((10,))],
        name="prep",
    )(prep_at, cube, got)
    e2 = permute(v8, 2, 0)
    o2 = permute(v8, 2, 1)
    e4 = permute(za, 4, 0)
    o4 = permute(zb, 4, 1)
    place = jnp.stack(
        [
            core,
            jnp.where(g2 == 0, 22, 6),
            jnp.where(g2 == 0, 6, 22),
            jnp.where(g4 == 0, 30, 0),
            jnp.where(g4 == 0, 0, 30),
            (me // 2) * chip,
            jnp.int32(count * local),
        ]
    ).astype(jnp.int32)
    own, other = pl.pallas_call(
        functools.partial(spectral_kernel, half, cols),
        in_specs=[smem] + [anyspace] * 5,
        out_specs=[vmem] * 2,
        out_shape=[jax.ShapeDtypeStruct((3, local, half, cols), F32)] * 2,
        scratch_shapes=[pltpu.VMEM((chip + 2 * REACH, half, cols), F32), pltpu.SemaphoreType.DMA((5,))],
        compiler_params=pltpu.CompilerParams(vmem_limit_bytes=32 * 2**20),
        name="spectral",
    )(place, v8, e2, o2, e4, o4)
    back = permute(other, 1, 0)
    pad = 2**SCALES_XY
    plane = pl.BlockSpec((1, rows, cols), lambda i: (i, 0, 0))
    third = pl.BlockSpec((3, 1, half, cols), lambda i: (0, i, 0, 0))
    return pl.pallas_call(
        functools.partial(spatial_kernel, rows, cols),
        grid=(local,),
        in_specs=[smem, smem, smem, plane, third, third, pl.BlockSpec((SCALES_XY, cols, cols), lambda i: (0, 0, 0))],
        out_specs=plane,
        out_shape=jax.ShapeDtypeStruct(cube.shape, F32),
        scratch_shapes=[
            pltpu.VMEM((4, rows, cols), F32),
            pltpu.VMEM((4, rows + 2 * pad, cols), F32),
            pltpu.VMEM((rows, cols), F32),
        ],
        compiler_params=pltpu.CompilerParams(vmem_limit_bytes=32 * 2**20),
        name="spatial",
    )(core[None], multipliers, noise_code, cube, own, back, column_matrices(cols))


def solution(mesh):
    placed = (P(("slab", "chan"), None, None), P(), P(("slab", "chan"), None, None))
    return jax.shard_map(
        functools.partial(per_device, mesh.shape["chan"]),
        mesh=mesh,
        in_specs=placed,
        out_specs=P(("slab", "chan"), None, None),
        check_vma=False,
    )
```

time: 373 us -> 92.8 us (0.25)
  the two profiles are of different devices: /device:TPU:12 before, /device:TPU:0 now
where the time goes in v1:
time: 92.8 us; the launch traced here: 92.5 us
  Pallas kernels  54.9 us (59%)
  waiting for transfers between devices  22.1 us (24%)
  starting transfers between devices  7.76 us (8%)
  local copies, waits for them, and re-layouts  6.99 us (8%)
    pallas_call x1, Pallas kernels, per_device(): pl.pallas_call(functools.partial(prep_kernel, half), in_specs=[smem, anys...  41.6 us
    ppermute x6, waiting for transfers between devices, permute(): return lax.ppermute(v, 'chan', pairs(count, distance, phase))  22.1 us
    pallas_call x1, Pallas kernels, per_device(): pl.pallas_call(functools.partial(spatial_kernel, rows, cols), grid=(local...  10.2 us
    ppermute x6, starting transfers between devices, permute(): return lax.ppermute(v, 'chan', pairs(count, distance, phase))  7.76 us
    unnamed x22, local copies, waits for them, and re-layouts  5.94 us
    pallas_call x1, Pallas kernels, per_device(): pl.pallas_call(functools.partial(spectral_kernel, half, cols), in_specs=[...  3.19 us
  transfers between devices with their start and end apart: 6, of which 3 were waited for; matrix products, arithmetic and copies ran while one was open for 1% of the time, Pallas kernels for 0%

profile of v1, /device:TPU:0, one launch (start us, length us, event | category | flops | bytes accessed | tf_op | source)
XLA Modules:
  0.0 92.5 jit_solution(4962481257844304401)
XLA Ops:
  0.0 1.0 %constant_dynamic-slice_fusion = f32[4,64,256]{2,1,0:T(8,128)S(1)} fusion(f32[4,128,256]{2,1,0:T(8,128)} %cube.3, s32[]{:T(128)S(6)} %select_n.48), kind=kLoop, calls=%fused_computation.1 | loop fusion | bytes 524292 | tf_op jit(solution)/shard_map/dynamic_slice | solution.py:200
  1.0 0.5 collective-permute-start
  1.5 0.6 pad_add_fusion.core_ref
  2.1 0.5 collective-permute-done.got
  2.7 0.0 copy-start.7
  2.7 0.7 copy-done.7
  3.4 41.6 %prep.1 = (f32[8,64,256]{2,1,0:T(8,128)}, f32[6,64,256]{2,1,0:T(8,128)}, f32[6,64,256]{2,1,0:T(8,128)}) custom-call(s32[3]{0:T(128)} %pad_add_fusion.core_ref, f32[4,128,256]{2,1,0:T(8,128)} %cube.3, f32[4,64,256]{2,1,0:T(8,128)} %copy-done.7), custom_call_target="tpu_custom_call" | custom-call | tf_op jit(solution)/shard_map/prep/pallas_call | solution.py:202
  44.9 3.0 %collective-permute-start.1 = (f32[8,64,256]{2,1,0:T(8,128)}, f32[8,64,256]{2,1,0:T(8,128)S(1)}, u32[]{:S(2)}, u32[]{:S(2)}) collective-permute-start(f32[8,64,256]{2,1,0:T(8,128)} %get-tuple-element.10.v8), channel_id=1, source_target_pairs={{0,2},{1,3},{2,0},{3,1},{4,6},{5,7},{6,4},{7,5},{8,10},{9,11},{10,... | collective-permute-start | bytes 1572872 | tf_op jit(solution)/shard_map/ppermute | solution.py:195
  47.9 0.7 collective-permute-start.2
  48.6 2.9 %collective-permute-start.3 = (f32[6,64,256]{2,1,0:T(8,128)}, f32[6,64,256]{2,1,0:T(8,128)S(1)}, u32[]{:S(2)}, u32[]{:S(2)}) collective-permute-start(f32[6,64,256]{2,1,0:T(8,128)} %get-tuple-element.11), channel_id=1, source_target_pairs={{0,4},{1,5},{2,6},{3,7},{4,0},{5,1},{6,2},{7,3},{8,12},{9,13},{10,... | collective-permute-start | bytes 1179656 | tf_op jit(solution)/shard_map/ppermute | solution.py:195
  51.5 0.7 collective-permute-start.4
  52.2 0.1 stack.34.place_ref
  52.3 19.7 %collective-permute-done.3.e4 = f32[6,64,256]{2,1,0:T(8,128)S(1)} collective-permute-done((f32[6,64,256]{2,1,0:T(8,128)}, f32[6,64,256]{2,1,0:T(8,128)S(1)}, u32[]{:S(2)}, u32[]{:S(2)}) %collective-permute-start.3) | collective-permute-done | bytes 393248 | tf_op jit(solution)/shard_map/ppermute | solution.py:195
  72.0 0.7 copy-done.3
  72.7 0.0 collective-permute-done.4.o4
  72.7 0.8 copy-done.5
  73.5 0.0 collective-permute-done.1.e2
  73.5 0.0 collective-permute-done.2.o2
  73.5 1.0 %copy-done.2 = f32[8,64,256]{2,1,0:T(8,128)S(1)} copy-done((f32[8,64,256]{2,1,0:T(8,128)S(1)}, f32[8,64,256]{2,1,0:T(8,128)}, u32[]{:S(2)}) %copy-start.2) | copy-done | bytes 524312
  74.5 1.0 %copy-done.4 = f32[6,64,256]{2,1,0:T(8,128)S(1)} copy-done((f32[6,64,256]{2,1,0:T(8,128)S(1)}, f32[6,64,256]{2,1,0:T(8,128)}, u32[]{:S(2)}) %copy-start.4) | copy-done | bytes 393240
  75.5 1.0 %copy-done.6 = f32[6,64,256]{2,1,0:T(8,128)S(1)} copy-done((f32[6,64,256]{2,1,0:T(8,128)S(1)}, f32[6,64,256]{2,1,0:T(8,128)}, u32[]{:S(2)}) %copy-start.6) | copy-done | bytes 393240
  76.5 3.2 %spectral.1 = (f32[3,4,64,256]{3,2,1,0:T(8,128)S(1)}, f32[3,4,64,256]{3,2,1,0:T(8,128)}) custom-call(s32[7]{0:T(128)S(1)} %stack.34.place_ref, f32[8,64,256]{2,1,0:T(8,128)S(1)} %copy-done.2, f32[8,64,256]{2,1,0:T(8,128)S(1)} %collective-permute-done.1.e2, f32[8,64,256]{2,1,0:T(8,128)S(1)} %collective-permute-done.2.o2, f32[6,64,256]{2,1,0:T(8,128)S(1)} %copy-done.4, ...), custom_call_target="tpu_custom_call" | custom-call | tf_op jit(solution)/shard_map/spectral/pallas_call | solution.py:225
  79.7 0.0 copy-start.9
  79.7 0.1 collective-permute-start.5
  79.8 0.0 copy-done.8
  79.8 0.1 copy.6.noise
  79.9 0.5 copy-done.9
  80.4 0.1 copy.5.mult
  80.5 1.8 %collective-permute-done.5.got = f32[3,4,64,256]{3,2,1,0:T(8,128)S(1)} collective-permute-done((f32[3,4,64,256]{3,2,1,0:T(8,128)}, f32[3,4,64,256]{3,2,1,0:T(8,128)S(1)}, u32[]{:S(2)}, u32[]{:S(2)}) %collective-permute-start.5) | collective-permute-done | bytes 786464 | tf_op jit(solution)/shard_map/ppermute | solution.py:195
  82.3 0.0 copy-done
  82.3 0.0 copy-done.1
  82.3 10.2 %spatial.1 = f32[4,128,256]{2,1,0:T(8,128)} custom-call(s32[1]{0:T(128)} %bitcast.core_ref, s32[6,4]{1,0:T(8,128)S(1)} %copy.5.mult, s32[4,6,4]{2,1,0:T(8,128)S(1)} %copy.6.noise, f32[4,128,256]{2,1,0:T(8,128)S(1)} %copy-done, f32[3,4,64,256]{3,2,1,0:T(8,128)S(1)} %get-tuple-element.13.own, f32[3,4,64,256]{3,2,1,0:T(8,128)S(1)} %collective-permute-done.5.got, ...), custom_call_target="tpu_custom_call" | custom-call | tf_op jit(solution)/shard_map/spatial/pallas_call | solution.py:238
  (8 shorter events, 0.0 us)
Async XLA Ops:
  1.0 1.7 %collective-permute-start = (f32[4,64,256]{2,1,0:T(8,128)S(1)}, f32[4,64,256]{2,1,0:T(8,128)S(1)}, u32[]{:S(2)}, u32[]{:S(2)}) collective-permute-start(f32[4,64,256]{2,1,0:T(8,128)S(1)} %constant_dynamic-slice_fusion), channel_id=1, source_target_pairs={{0,1},{1,0},{2,3},{3,2},{4,5},{5,4},{6,7},{7,6},{8,9},{9,8},{10,11... | collective-permute-start | bytes 786440 | tf_op jit(solution)/shard_map/ppermute | solution.py:195
  2.7 0.7 copy-start.7
  44.9 28.6 %collective-permute-start.1 = (f32[8,64,256]{2,1,0:T(8,128)}, f32[8,64,256]{2,1,0:T(8,128)S(1)}, u32[]{:S(2)}, u32[]{:S(2)}) collective-permute-start(f32[8,64,256]{2,1,0:T(8,128)} %get-tuple-element.10.v8), channel_id=1, source_target_pairs={{0,2},{1,3},{2,0},{3,1},{4,6},{5,7},{6,4},{7,5},{8,10},{9,11},{10,... | collective-permute-start | bytes 1572872 | tf_op jit(solution)/shard_map/ppermute | solution.py:195
  47.9 25.6 %collective-permute-start.2 = (f32[8,64,256]{2,1,0:T(8,128)}, f32[8,64,256]{2,1,0:T(8,128)S(1)}, u32[]{:S(2)}, u32[]{:S(2)}) collective-permute-start(f32[8,64,256]{2,1,0:T(8,128)} %get-tuple-element.10.v8), channel_id=1, source_target_pairs={{2,4},{3,5},{4,2},{5,3},{6,8},{7,9},{8,6},{9,7},{10,12},{11,13},{1... | collective-permute-start | bytes 1572872 | tf_op jit(solution)/shard_map/ppermute | solution.py:195
  48.6 23.4 %collective-permute-start.3 = (f32[6,64,256]{2,1,0:T(8,128)}, f32[6,64,256]{2,1,0:T(8,128)S(1)}, u32[]{:S(2)}, u32[]{:S(2)}) collective-permute-start(f32[6,64,256]{2,1,0:T(8,128)} %get-tuple-element.11), channel_id=1, source_target_pairs={{0,4},{1,5},{2,6},{3,7},{4,0},{5,1},{6,2},{7,3},{8,12},{9,13},{10,... | collective-permute-start | bytes 1179656 | tf_op jit(solution)/shard_map/ppermute | solution.py:195
  51.5 21.3 %collective-permute-start.4 = (f32[6,64,256]{2,1,0:T(8,128)}, f32[6,64,256]{2,1,0:T(8,128)S(1)}, u32[]{:S(2)}, u32[]{:S(2)}) collective-permute-start(f32[6,64,256]{2,1,0:T(8,128)} %get-tuple-element.12), channel_id=1, source_target_pairs={{4,8},{5,9},{6,10},{7,11},{8,4},{9,5},{10,6},{11,7},{20,24},{21,25... | collective-permute-start | bytes 1179656 | tf_op jit(solution)/shard_map/ppermute | solution.py:195
  52.3 30.0 %copy-start = (f32[4,128,256]{2,1,0:T(8,128)S(1)}, f32[4,128,256]{2,1,0:T(8,128)}, u32[]{:S(2)}) copy-start(f32[4,128,256]{2,1,0:T(8,128)} %cube.3) | copy-start | bytes 1572868
  52.3 30.0 %copy-start.1 = (bf16[5,256,256]{2,1,0:T(8,128)(2,1)S(1)}, bf16[5,256,256]{2,1,0:T(8,128)(2,1)}, u32[]{:S(2)}) copy-start(bf16[5,256,256]{2,1,0:T(8,128)(2,1)} %constant.66.clone.mats) | copy-start | bytes 1966084
  72.0 0.7 copy-start.3
  72.7 0.8 copy-start.5
  73.5 1.0 %copy-start.2 = (f32[8,64,256]{2,1,0:T(8,128)S(1)}, f32[8,64,256]{2,1,0:T(8,128)}, u32[]{:S(2)}) copy-start(f32[8,64,256]{2,1,0:T(8,128)} %get-tuple-element.10.v8) | copy-start | bytes 1572868
  74.5 1.0 %copy-start.4 = (f32[6,64,256]{2,1,0:T(8,128)S(1)}, f32[6,64,256]{2,1,0:T(8,128)}, u32[]{:S(2)}) copy-start(f32[6,64,256]{2,1,0:T(8,128)} %copy-done.3) | copy-start | bytes 1179652
  75.5 1.0 %copy-start.6 = (f32[6,64,256]{2,1,0:T(8,128)S(1)}, f32[6,64,256]{2,1,0:T(8,128)}, u32[]{:S(2)}) copy-start(f32[6,64,256]{2,1,0:T(8,128)} %copy-done.5) | copy-start | bytes 1179652
  76.5 3.3 %copy-start.8 = (s32[4,6,4]{1,2,0:T(4,128)S(1)}, s32[4,6,4]{1,2,0:T(4,128)}, u32[]{:S(2)}) copy-start(s32[4,6,4]{1,2,0:T(4,128)} %param.6) | copy-start | bytes 1156
  79.7 0.7 copy-start.9
  79.7 2.6 %collective-permute-start.5 = (f32[3,4,64,256]{3,2,1,0:T(8,128)}, f32[3,4,64,256]{3,2,1,0:T(8,128)S(1)}, u32[]{:S(2)}, u32[]{:S(2)}) collective-permute-start(f32[3,4,64,256]{3,2,1,0:T(8,128)} %get-tuple-element.14), channel_id=1, source_target_pairs={{0,1},{1,0},{2,3},{3,2},{4,5},{5,4},{6,7},{7,6},{8,9},{9,8},{10,11... | collective-permute-start | bytes 2359304 | tf_op jit(solution)/shard_map/ppermute | solution.py:195

commit v2 on v0

v2 whole, which is shorter than its diff:
```python
import functools

import jax
import jax.numpy as jnp
import numpy as np
from jax import lax
from jax.experimental import pallas as pl
from jax.experimental.pallas import tpu as pltpu
from jax.sharding import PartitionSpec as P

SCALES_XY = 5
SCALES_NU = 3
TAPS = (1, 4, 6, 4, 1)
REACH = 14
LANES = 128
EDGE = 8
F32 = jnp.float32
BF16 = jnp.bfloat16


def pairs(count, distance, phase):
    out = []
    for i in range(count):
        j = i + distance if (i // distance) % 2 == phase else i - distance
        if 0 <= j < count:
            out.append((i, j))
    return out


def column_matrices(cols):
    place = np.arange(cols)
    offset = place[None, :] - place[:, None]
    mats = []
    for j in range(SCALES_XY):
        m = np.zeros((cols, cols), np.float32)
        for k, w in enumerate(TAPS):
            m += np.where(offset == (k - 2) * 2**j, np.float32(w / 256.0), np.float32(0))
        mats.append(m)
    return jnp.asarray(np.stack(mats), BF16)


def plus(*terms):
    terms = [t for t in terms if t is not None]
    out = terms[0]
    for t in terms[1:]:
        out = out + t
    return out


def pick(values, k):
    return values[k] if 0 <= k < len(values) else None


def spline4(values, first, step, lo, hi):
    cur = dict(enumerate(values, first))
    for shift in (-1, -1, 1, 1):
        cur = {k: v + cur[k + shift * step] for k, v in cur.items() if k + shift * step in cur}
    return [cur[k] for k in range(lo, hi)]


def split(x):
    hi = x.astype(BF16)
    return hi, (x - hi.astype(F32)).astype(BF16)


def denoise_kernel(rows, cols, local, pieces, place, mult, noise, *refs):
    ins = refs[:pieces]
    mats, out = refs[pieces : pieces + 2]
    ext, detail, a, p, acc, done, sem, out_sem = refs[pieces + 2 :]
    halves = cols // LANES
    groups = rows // 8
    centre = 5 * local
    copies = [
        pltpu.make_async_copy(ref, ext.at[pl.ds(place[2 + n], ref.shape[0])], sem.at[n])
        for n, ref in enumerate(ins)
    ]
    for c in copies:
        c.start()
    for s in range(SCALES_NU + 1):
        for h in range(halves):
            p[s, h, :EDGE] = jnp.zeros((EDGE, LANES), F32)
            p[s, h, EDGE + rows :] = jnp.zeros((EDGE, LANES), F32)
    first, channels = place[0], place[1]
    inside = {}
    for k in list(range(-12, 0)) + list(range(local, local + 12)):
        at = first + k
        inside[k] = jnp.where((at >= 0) & (at < channels), 1.0, 0.0).astype(F32)
    for c in copies:
        c.wait()

    def spectral(g, carry):
        r = pl.ds(pl.multiple_of(g * 8, 8), 8)
        for h in range(halves):
            lanes = pl.ds(h * LANES, LANES)
            x = [ext[centre + k, r, lanes] for k in range(-REACH, local + REACH)]
            c1 = spline4(x, -14, 1, -12, local + 12)
            c1 = [v * inside[k] if k in inside else v for k, v in enumerate(c1, -12)]
            c2 = spline4(c1, -12, 2, -8, local + 8)
            c2 = [v * inside[k] if k in inside else v for k, v in enumerate(c2, -8)]
            c3 = spline4(c2, -8, 4, 0, local)
            for k in range(local):
                e0 = x[k + 14]
                e1 = c1[k + 12] * (1.0 / 16.0)
                e2 = c2[k + 8] * (1.0 / 256.0)
                e3 = c3[k] * (1.0 / 4096.0)
                detail[k, 0, h, r] = e0 - e1
                detail[k, 1, h, r] = e1 - e2
                detail[k, 2, h, r] = e2 - e3
                detail[k, 3, h, r] = e3
        return carry

    lax.fori_loop(0, groups, spectral, 0)

    def spatial(i, carry):
        def limit(j, s):
            return (mult[s, j] * noise[i, s, j]).astype(F32) * (1.0 / 1024.0)

        def shrink(v, j, s):
            lim = limit(j, s)
            return v - jnp.clip(v, -lim, lim)

        def source(j, s):
            return detail.at[i, s] if j == 0 else a.at[s]

        def columns(j, s):
            src = source(j, s)
            hi, lo = split(jnp.concatenate([src[h] for h in range(halves)], 1))
            y = jnp.dot(jnp.concatenate([hi, lo], 0), mats[j], preferred_element_type=F32)
            y = y[:rows] + y[rows:]
            for h in range(halves):
                p[s, h, pl.ds(EDGE, rows)] = y[:, h * LANES : (h + 1) * LANES]

        def smooth_rows(j, s, h):
            d = 2**j

            def load(o):
                return [p[s, h, pl.ds(EDGE + 8 * k + o, 8)] for k in range(groups)]

            x = load(0)
            if d >= 8:
                q = d // 8
                cur = x
                for _ in range(4):
                    cur = [plus(pick(cur, k), pick(cur, k - q)) for k in range(len(cur) + q)]
                return cur[2 * q : 2 * q + groups]
            if d == 4:
                u = [p[s, h, pl.ds(EDGE + 8 * k - 4, 8)] for k in range(groups + 1)]
                near = [u[k] + u[k + 1] for k in range(groups)]
                far = [plus(pick(x, k - 1), pick(x, k + 1)) for k in range(groups)]
            elif d == 2:
                u = [p[s, h, pl.ds(EDGE + 8 * k - 4, 8)] for k in range(groups + 1)]
                near = [m + n for m, n in zip(load(-2), load(2))]
                far = [u[k] + u[k + 1] for k in range(groups)]
            else:
                near = [m + n for m, n in zip(load(-1), load(1))]
                far = [m + n for m, n in zip(load(-2), load(2))]
            return [6.0 * x[k] + 4.0 * near[k] + far[k] for k in range(groups)]

        for j in range(SCALES_XY):
            for s in range(SCALES_NU + 1):
                columns(j, s)
            for h in range(halves):
                total = [None] * groups
                for s in range(SCALES_NU + 1):
                    src = source(j, s)
                    y = smooth_rows(j, s, h)
                    for k in range(groups):
                        r = pl.ds(8 * k, 8)
                        v = shrink(src[h, r] - y[k], j, s)
                        a[s, h, r] = y[k]
                        total[k] = plus(total[k], v)
                for k in range(groups):
                    r = pl.ds(8 * k, 8)
                    if j == 0:
                        acc[h, r] = total[k]
                    else:
                        acc[h, r] += total[k]
        for h in range(halves):
            total = acc[h] + a[SCALES_NU, h]
            for s in range(SCALES_NU):
                total = total + shrink(a[s, h], SCALES_XY, s)
            done[i, :, h * LANES : (h + 1) * LANES] = total
        pltpu.make_async_copy(done.at[i], out.at[i], out_sem.at[i]).start()
        return carry

    lax.fori_loop(0, local, spatial, 0)
    for i in range(local):
        pltpu.make_async_copy(done.at[i], out.at[i], out_sem.at[i]).wait()


def per_device(count, cube, multipliers, noise_code):
    local, rows, cols = cube.shape
    assert local == 4 and count % 2 == 0 and rows % 8 == 0 and cols % LANES == 0
    me = lax.axis_index("chan").astype(jnp.int32)
    core = me % 2
    g2 = (me // 2) % 2
    g4 = (me // 4) % 2
    beside = 1 - 2 * core

    def permute(v, distance, phase):
        return lax.ppermute(v, "chan", pairs(count, distance, phase))

    pieces = [(cube, 0)]
    for distance, group in ((2, g2), (4, g4)):
        for phase in (0, 1):
            up = jnp.where(group == phase, 1, -1)
            pieces.append((permute(cube, distance, phase), up * distance))
    pieces += [(permute(v, 1, 0), at + beside) for v, at in pieces]
    place = jnp.stack([me * local, jnp.int32(count * local)] + [(5 + at) * local for _, at in pieces]).astype(jnp.int32)
    smem = pl.BlockSpec(memory_space=pltpu.SMEM)
    vmem = pl.BlockSpec(memory_space=pltpu.VMEM)
    plane = (cols // LANES, rows, LANES)
    scales = SCALES_NU + 1
    return pl.pallas_call(
        functools.partial(denoise_kernel, rows, cols, local, len(pieces)),
        in_specs=[smem] * 3 + [vmem] * (len(pieces) + 1),
        out_specs=pl.BlockSpec(memory_space=pltpu.HBM),
        out_shape=jax.ShapeDtypeStruct(cube.shape, F32),
        scratch_shapes=[
            pltpu.VMEM((11 * local, rows, cols), F32),
            pltpu.VMEM((local, scales) + plane, F32),
            pltpu.VMEM((scales,) + plane, F32),
            pltpu.VMEM((scales, cols // LANES, rows + 2 * EDGE, LANES), F32),
            pltpu.VMEM(plane, F32),
            pltpu.VMEM((local, rows, cols), F32),
            pltpu.SemaphoreType.DMA((len(pieces),)),
            pltpu.SemaphoreType.DMA((local,)),
        ],
        compiler_params=pltpu.CompilerParams(vmem_limit_bytes=18 * 2**20),
        name="denoise",
    )(place, multipliers.T, noise_code.transpose(0, 2, 1), *[v for v, _ in pieces], column_matrices(cols))


def solution(mesh):
    placed = (P(("slab", "chan"), None, None), P(), P(("slab", "chan"), None, None))
    return jax.shard_map(
        functools.partial(per_device, mesh.shape["chan"]),
        mesh=mesh,
        in_specs=placed,
        out_specs=P(("slab", "chan"), None, None),
        check_vma=False,
    )
```

time: 373 us -> 48.3 us (0.13)
  the two profiles are of different devices: /device:TPU:12 before, /device:TPU:9 now
where the time goes in v2:
time: 48.3 us; the launch traced here: 48.1 us
  waiting for transfers between devices  18.4 us (38%)
  starting transfers between devices  16.5 us (34%)
  Pallas kernels  10.8 us (22%)
  local copies, waits for them, and re-layouts  2.22 us (5%)
    ppermute x9, waiting for transfers between devices, permute(): return lax.ppermute(v, 'chan', pairs(count, distance, phase))  18.4 us
    ppermute x9, starting transfers between devices, permute(): return lax.ppermute(v, 'chan', pairs(count, distance, phase))  16.5 us
    pallas_call x1, Pallas kernels, per_device(): pl.pallas_call(functools.partial(denoise_kernel, rows, cols, local, len(p...  10.8 us
    unnamed x8, local copies, waits for them, and re-layouts  2.14 us
  transfers between devices with their start and end apart: 9, of which 4 were waited for; matrix products, arithmetic and copies ran while one was open for 0% of the time, Pallas kernels for 0%

profile of v2, /device:TPU:9, one launch (start us, length us, event | category | flops | bytes accessed | tf_op | source)
XLA Modules:
  0.0 48.1 jit_solution(2457365866038960736)
XLA Ops:
  0.0 3.2 %collective-permute-start.3 = (f32[4,128,256]{2,1,0:T(8,128)}, f32[4,128,256]{2,1,0:T(8,128)S(1)}, u32[]{:S(2)}, u32[]{:S(2)}) collective-permute-start(f32[4,128,256]{2,1,0:T(8,128)} %refs_0_.1), channel_id=1, source_target_pairs={{4,8},{5,9},{6,10},{7,11},{8,4},{9,5},{10,6},{11,7},{20,24},{21,25... | collective-permute-start | bytes 1572872 | tf_op jit(solution)/shard_map/ppermute | solution.py:201
  3.2 0.1 collective-permute-start.2
  3.3 4.3 %collective-permute-start.1 = (f32[4,128,256]{2,1,0:T(8,128)}, f32[4,128,256]{2,1,0:T(8,128)S(1)}, u32[]{:S(2)}, u32[]{:S(2)}) collective-permute-start(f32[4,128,256]{2,1,0:T(8,128)} %refs_0_.1), channel_id=1, source_target_pairs={{2,4},{3,5},{4,2},{5,3},{6,8},{7,9},{8,6},{9,7},{10,12},{11,13},{1... | collective-permute-start | bytes 1572872 | tf_op jit(solution)/shard_map/ppermute | solution.py:201
  7.6 0.1 collective-permute-start
  7.7 1.6 %collective-permute-start.4 = (f32[4,128,256]{2,1,0:T(8,128)}, f32[4,128,256]{2,1,0:T(8,128)S(1)}, u32[]{:S(2)}, u32[]{:S(2)}) collective-permute-start(f32[4,128,256]{2,1,0:T(8,128)} %refs_0_.1), channel_id=1, source_target_pairs={{0,1},{1,0},{2,3},{3,2},{4,5},{5,4},{6,7},{7,6},{8,9},{9,8},{10,11... | collective-permute-start | bytes 1572872 | tf_op jit(solution)/shard_map/ppermute | solution.py:201
  9.3 5.6 %collective-permute-done.3.refs_4_ = f32[4,128,256]{2,1,0:T(8,128)S(1)} collective-permute-done((f32[4,128,256]{2,1,0:T(8,128)}, f32[4,128,256]{2,1,0:T(8,128)S(1)}, u32[]{:S(2)}, u32[]{:S(2)}) %collective-permute-start.3) | collective-permute-done | bytes 524320 | tf_op jit(solution)/shard_map/ppermute | solution.py:201
  14.9 2.7 %collective-permute-start.8 = (f32[4,128,256]{2,1,0:T(8,128)S(1)}, f32[4,128,256]{2,1,0:T(8,128)S(1)}, u32[]{:S(2)}, u32[]{:S(2)}) collective-permute-start(f32[4,128,256]{2,1,0:T(8,128)S(1)} %collective-permute-done.3.refs_4_), channel_id=1, source_target_pairs={{0,1},{1,0},{2,3},{3,2},{4,5},{5,4},{6,7},{7,6},{8,9},{9,8},{10,11... | collective-permute-start | bytes 1572872 | tf_op jit(solution)/shard_map/ppermute | solution.py:201
  17.6 0.0 collective-permute-done.2.refs_3_
  17.6 0.2 collective-permute-start.7
  17.8 10.4 %collective-permute-done.1.refs_2_ = f32[4,128,256]{2,1,0:T(8,128)S(1)} collective-permute-done((f32[4,128,256]{2,1,0:T(8,128)}, f32[4,128,256]{2,1,0:T(8,128)S(1)}, u32[]{:S(2)}, u32[]{:S(2)}) %collective-permute-start.1) | collective-permute-done | bytes 524320 | tf_op jit(solution)/shard_map/ppermute | solution.py:201
  28.2 1.9 %collective-permute-start.6 = (f32[4,128,256]{2,1,0:T(8,128)S(1)}, f32[4,128,256]{2,1,0:T(8,128)}, u32[]{:S(2)}, u32[]{:S(2)}) collective-permute-start(f32[4,128,256]{2,1,0:T(8,128)S(1)} %collective-permute-done.1.refs_2_), channel_id=1, source_target_pairs={{0,1},{1,0},{2,3},{3,2},{4,5},{5,4},{6,7},{7,6},{8,9},{9,8},{10,11... | collective-permute-start | bytes 1572872 | tf_op jit(solution)/shard_map/ppermute | solution.py:201
  30.1 0.9 %collective-permute-done.refs_1_ = f32[4,128,256]{2,1,0:T(8,128)S(1)} collective-permute-done((f32[4,128,256]{2,1,0:T(8,128)}, f32[4,128,256]{2,1,0:T(8,128)S(1)}, u32[]{:S(2)}, u32[]{:S(2)}) %collective-permute-start) | collective-permute-done | bytes 524320 | tf_op jit(solution)/shard_map/ppermute | solution.py:201
  31.0 2.4 %collective-permute-start.5 = (f32[4,128,256]{2,1,0:T(8,128)S(1)}, f32[4,128,256]{2,1,0:T(8,128)}, u32[]{:S(2)}, u32[]{:S(2)}) collective-permute-start(f32[4,128,256]{2,1,0:T(8,128)S(1)} %collective-permute-done.refs_1_), channel_id=1, source_target_pairs={{0,1},{1,0},{2,3},{3,2},{4,5},{5,4},{6,7},{7,6},{8,9},{9,8},{10,11... | collective-permute-start | bytes 1572872 | tf_op jit(solution)/shard_map/ppermute | solution.py:201
  33.4 0.0 copy-start.2
  33.5 0.1 stack.43.place
  33.5 0.0 copy-start.3
  33.5 0.0 collective-permute-done.4.refs_5_
  33.6 0.0 collective-permute-done.8.refs_9_
  33.6 0.0 collective-permute-done.7.refs_8_
  33.6 0.0 collective-permute-done.6.refs_7_
  33.6 1.5 %collective-permute-done.5.refs_6_ = f32[4,128,256]{2,1,0:T(8,128)} collective-permute-done((f32[4,128,256]{2,1,0:T(8,128)S(1)}, f32[4,128,256]{2,1,0:T(8,128)}, u32[]{:S(2)}, u32[]{:S(2)}) %collective-permute-start.5) | collective-permute-done | bytes 524320 | tf_op jit(solution)/shard_map/ppermute | solution.py:201
  35.1 0.0 copy-done.2
  35.1 0.0 copy-done.3
  35.1 0.0 copy-start
  35.1 1.1 %copy-done = bf16[5,256,256]{2,1,0:T(8,128)(2,1)S(1)} copy-done((bf16[5,256,256]{2,1,0:T(8,128)(2,1)S(1)}, bf16[5,256,256]{2,1,0:T(8,128)(2,1)}, u32[]{:S(2)}) %copy-start) | copy-done | bytes 655384
  36.2 0.0 copy-start.1
  36.2 1.0 %copy-done.1 = f32[4,128,256]{2,1,0:T(8,128)S(1)} copy-done((f32[4,128,256]{2,1,0:T(8,128)S(1)}, f32[4,128,256]{2,1,0:T(8,128)}, u32[]{:S(2)}) %copy-start.1) | copy-done | bytes 524312
  37.3 10.8 %denoise.1 = f32[4,128,256]{2,1,0:T(8,128)} custom-call(s32[12]{0:T(128)S(1)} %stack.43.place, s32[4,6]{1,0:T(4,128)S(1)} %bitcast.13, s32[4,4,6]{2,1,0:T(4,128)S(1)} %bitcast.12, f32[4,128,256]{2,1,0:T(8,128)S(1)} %copy-done.1, f32[4,128,256]{2,1,0:T(8,128)S(1)} %collective-permute-done.refs_1_, f32[4,128,256]{2,1,0:T(8,128)S(1)} %collective-permute-done.1.refs_2_, ...), custom_call_target="tpu_custom_call" | custom-call | tf_op jit(solution)/shard_map/denoise/pallas_call | solution.py:214
Async XLA Ops:
  0.0 14.9 %collective-permute-start.3 = (f32[4,128,256]{2,1,0:T(8,128)}, f32[4,128,256]{2,1,0:T(8,128)S(1)}, u32[]{:S(2)}, u32[]{:S(2)}) collective-permute-start(f32[4,128,256]{2,1,0:T(8,128)} %refs_0_.1), channel_id=1, source_target_pairs={{4,8},{5,9},{6,10},{7,11},{8,4},{9,5},{10,6},{11,7},{20,24},{21,25... | collective-permute-start | bytes 1572872 | tf_op jit(solution)/shard_map/ppermute | solution.py:201
  3.2 14.4 %collective-permute-start.2 = (f32[4,128,256]{2,1,0:T(8,128)}, f32[4,128,256]{2,1,0:T(8,128)S(1)}, u32[]{:S(2)}, u32[]{:S(2)}) collective-permute-start(f32[4,128,256]{2,1,0:T(8,128)} %refs_0_.1), channel_id=1, source_target_pairs={{0,4},{1,5},{2,6},{3,7},{4,0},{5,1},{6,2},{7,3},{8,12},{9,13},{10,... | collective-permute-start | bytes 1572872 | tf_op jit(solution)/shard_map/ppermute | solution.py:201
  3.3 24.9 %collective-permute-start.1 = (f32[4,128,256]{2,1,0:T(8,128)}, f32[4,128,256]{2,1,0:T(8,128)S(1)}, u32[]{:S(2)}, u32[]{:S(2)}) collective-permute-start(f32[4,128,256]{2,1,0:T(8,128)} %refs_0_.1), channel_id=1, source_target_pairs={{2,4},{3,5},{4,2},{5,3},{6,8},{7,9},{8,6},{9,7},{10,12},{11,13},{1... | collective-permute-start | bytes 1572872 | tf_op jit(solution)/shard_map/ppermute | solution.py:201
  7.6 23.4 %collective-permute-start = (f32[4,128,256]{2,1,0:T(8,128)}, f32[4,128,256]{2,1,0:T(8,128)S(1)}, u32[]{:S(2)}, u32[]{:S(2)}) collective-permute-start(f32[4,128,256]{2,1,0:T(8,128)} %refs_0_.1), channel_id=1, source_target_pairs={{0,2},{1,3},{2,0},{3,1},{4,6},{5,7},{6,4},{7,5},{8,10},{9,11},{10,... | collective-permute-start | bytes 1572872 | tf_op jit(solution)/shard_map/ppermute | solution.py:201
  7.7 25.9 %collective-permute-start.4 = (f32[4,128,256]{2,1,0:T(8,128)}, f32[4,128,256]{2,1,0:T(8,128)S(1)}, u32[]{:S(2)}, u32[]{:S(2)}) collective-permute-start(f32[4,128,256]{2,1,0:T(8,128)} %refs_0_.1), channel_id=1, source_target_pairs={{0,1},{1,0},{2,3},{3,2},{4,5},{5,4},{6,7},{7,6},{8,9},{9,8},{10,11... | collective-permute-start | bytes 1572872 | tf_op jit(solution)/shard_map/ppermute | solution.py:201
  14.9 18.7 %collective-permute-start.8 = (f32[4,128,256]{2,1,0:T(8,128)S(1)}, f32[4,128,256]{2,1,0:T(8,128)S(1)}, u32[]{:S(2)}, u32[]{:S(2)}) collective-permute-start(f32[4,128,256]{2,1,0:T(8,128)S(1)} %collective-permute-done.3.refs_4_), channel_id=1, source_target_pairs={{0,1},{1,0},{2,3},{3,2},{4,5},{5,4},{6,7},{7,6},{8,9},{9,8},{10,11... | collective-permute-start | bytes 1572872 | tf_op jit(solution)/shard_map/ppermute | solution.py:201
  17.6 16.0 %collective-permute-start.7 = (f32[4,128,256]{2,1,0:T(8,128)S(1)}, f32[4,128,256]{2,1,0:T(8,128)}, u32[]{:S(2)}, u32[]{:S(2)}) collective-permute-start(f32[4,128,256]{2,1,0:T(8,128)S(1)} %collective-permute-done.2.refs_3_), channel_id=1, source_target_pairs={{0,1},{1,0},{2,3},{3,2},{4,5},{5,4},{6,7},{7,6},{8,9},{9,8},{10,11... | collective-permute-start | bytes 1572872 | tf_op jit(solution)/shard_map/ppermute | solution.py:201
  28.2 5.4 %collective-permute-start.6 = (f32[4,128,256]{2,1,0:T(8,128)S(1)}, f32[4,128,256]{2,1,0:T(8,128)}, u32[]{:S(2)}, u32[]{:S(2)}) collective-permute-start(f32[4,128,256]{2,1,0:T(8,128)S(1)} %collective-permute-done.1.refs_2_), channel_id=1, source_target_pairs={{0,1},{1,0},{2,3},{3,2},{4,5},{5,4},{6,7},{7,6},{8,9},{9,8},{10,11... | collective-permute-start | bytes 1572872 | tf_op jit(solution)/shard_map/ppermute | solution.py:201
  31.0 4.1 %collective-permute-start.5 = (f32[4,128,256]{2,1,0:T(8,128)S(1)}, f32[4,128,256]{2,1,0:T(8,128)}, u32[]{:S(2)}, u32[]{:S(2)}) collective-permute-start(f32[4,128,256]{2,1,0:T(8,128)S(1)} %collective-permute-done.refs_1_), channel_id=1, source_target_pairs={{0,1},{1,0},{2,3},{3,2},{4,5},{5,4},{6,7},{7,6},{8,9},{9,8},{10,11... | collective-permute-start | bytes 1572872 | tf_op jit(solution)/shard_map/ppermute | solution.py:201
  33.4 1.7 %copy-start.2 = (s32[4,6,4]{1,2,0:T(4,128)S(1)}, s32[4,6,4]{1,2,0:T(4,128)}, u32[]{:S(2)}) copy-start(s32[4,6,4]{1,2,0:T(4,128)} %param.6) | copy-start | bytes 1156
  33.5 1.6 %copy-start.3 = (s32[6,4]{0,1:T(4,128)S(1)}, s32[6,4]{0,1:T(4,128)}, u32[]{:S(2)}) copy-start(s32[6,4]{0,1:T(4,128)} %param.5) | copy-start | bytes 292
  35.1 1.1 %copy-start = (bf16[5,256,256]{2,1,0:T(8,128)(2,1)S(1)}, bf16[5,256,256]{2,1,0:T(8,128)(2,1)}, u32[]{:S(2)}) copy-start(bf16[5,256,256]{2,1,0:T(8,128)(2,1)} %constant.60.clone.refs_10_) | copy-start | bytes 1966084
  36.2 1.0 %copy-start.1 = (f32[4,128,256]{2,1,0:T(8,128)S(1)}, f32[4,128,256]{2,1,0:T(8,128)}, u32[]{:S(2)}) copy-start(f32[4,128,256]{2,1,0:T(8,128)} %refs_0_.1) | copy-start | bytes 1572868

commit v3 on v2

--- a/solution.py
+++ b/solution.py
@@ -2,7 +2,6 @@
 
 import jax
 import jax.numpy as jnp
-import numpy as np
 from jax import lax
 from jax.experimental import pallas as pl
 from jax.experimental.pallas import tpu as pltpu
@@ -27,18 +26,6 @@
     return out
 
 
-def column_matrices(cols):
-    place = np.arange(cols)
-    offset = place[None, :] - place[:, None]
-    mats = []
-    for j in range(SCALES_XY):
-        m = np.zeros((cols, cols), np.float32)
-        for k, w in enumerate(TAPS):
-            m += np.where(offset == (k - 2) * 2**j, np.float32(w / 256.0), np.float32(0))
-        mats.append(m)
-    return jnp.asarray(np.stack(mats), BF16)
-
-
 def plus(*terms):
     terms = [t for t in terms if t is not None]
     out = terms[0]
@@ -69,7 +56,7 @@
     ext, detail, a, p, acc, done, sem, out_sem = refs[pieces + 2 :]
     halves = cols // LANES
     groups = rows // 8
-    centre = 5 * local
+    centre = 4 * local
     copies = [
         pltpu.make_async_copy(ref, ext.at[pl.ds(place[2 + n], ref.shape[0])], sem.at[n])
         for n, ref in enumerate(ins)
@@ -188,6 +175,19 @@
         pltpu.make_async_copy(done.at[i], out.at[i], out_sem.at[i]).wait()
 
 
+def setup_kernel(cols, cube, copy, mats, sem):
+    fetch = pltpu.make_async_copy(cube, copy, sem)
+    fetch.start()
+    row = lax.broadcasted_iota(jnp.int32, (cols, cols), 0)
+    offset = lax.broadcasted_iota(jnp.int32, (cols, cols), 1) - row
+    for j in range(SCALES_XY):
+        m = jnp.zeros((cols, cols), F32)
+        for k, w in enumerate(TAPS):
+            m = jnp.where(offset == (k - 2) * 2**j, w / 256.0, m)
+        mats[j] = m.astype(BF16)
+    fetch.wait()
+
+
 def per_device(count, cube, multipliers, noise_code):
     local, rows, cols = cube.shape
     assert local == 4 and count % 2 == 0 and rows % 8 == 0 and cols % LANES == 0
@@ -196,28 +196,49 @@
     g2 = (me // 2) % 2
     g4 = (me // 4) % 2
     beside = 1 - 2 * core
+    smem = pl.BlockSpec(memory_space=pltpu.SMEM)
+    hbm = pl.BlockSpec(memory_space=pltpu.HBM)
+    vmem = pl.BlockSpec(memory_space=pltpu.VMEM)
+    anyspace = pl.BlockSpec(memory_space=pl.ANY)
 
     def permute(v, distance, phase):
         return lax.ppermute(v, "chan", pairs(count, distance, phase))
 
-    pieces = [(cube, 0)]
-    for distance, group in ((2, g2), (4, g4)):
-        for phase in (0, 1):
-            up = jnp.where(group == phase, 1, -1)
-            pieces.append((permute(cube, distance, phase), up * distance))
-    pieces += [(permute(v, 1, 0), at + beside) for v, at in pieces]
-    place = jnp.stack([me * local, jnp.int32(count * local)] + [(5 + at) * local for _, at in pieces]).astype(jnp.int32)
-    smem = pl.BlockSpec(memory_space=pltpu.SMEM)
-    vmem = pl.BlockSpec(memory_space=pltpu.VMEM)
+    relay = [(i, i + 4) for i in range(count - 4) if (i // 2) % 2 == 0]
+    relay += [(i, i - 4) for i in range(4, count) if (i // 2) % 2 == 1]
+    cut = local // 2
+    near = permute(cube, 2, 0)
+    two_a = permute(cube, 4, 0)
+    two_b = permute(cube, 4, 1)
+    far_hi = permute(cube[cut:], 2, 1)
+    far_lo = lax.ppermute(near[:cut], "chan", relay)
+    here, mats = pl.pallas_call(
+        functools.partial(setup_kernel, cols),
+        in_specs=[anyspace],
+        out_specs=[vmem] * 2,
+        out_shape=[jax.ShapeDtypeStruct(cube.shape, F32), jax.ShapeDtypeStruct((SCALES_XY, cols, cols), BF16)],
+        scratch_shapes=[pltpu.SemaphoreType.DMA],
+        compiler_params=pltpu.CompilerParams(vmem_limit_bytes=4 * 2**20),
+        cost_estimate=pl.CostEstimate(flops=10**7, bytes_accessed=2 * 10**6, transcendentals=0),
+        name="setup",
+    )(cube)
+    two_a, two_b, near, here, mats = lax.optimization_barrier((two_a, two_b, near, here, mats))
+    far_hi, far_lo = lax.optimization_barrier((far_hi, far_lo))
+    up2 = jnp.where(g2 == 0, 2, -2)
+    up4 = jnp.where(g4 == 0, 4, -4)
+    pieces = [(here, 0, 0), (near, up2, 0), (two_a, up4, 0), (two_b, -up4, 0), (far_hi, -up2, cut), (far_lo, -up2, 0)]
+    pieces += [(permute(cube if n == 0 else v, 1, 0), at + beside, o) for n, (v, at, o) in enumerate(pieces)]
+    place = [jnp.where(abs(at) > 4, 9, at + 4) * local + o for _, at, o in pieces]
+    place = jnp.stack([me * local, jnp.int32(count * local)] + place).astype(jnp.int32)
     plane = (cols // LANES, rows, LANES)
     scales = SCALES_NU + 1
     return pl.pallas_call(
         functools.partial(denoise_kernel, rows, cols, local, len(pieces)),
-        in_specs=[smem] * 3 + [vmem] * (len(pieces) + 1),
-        out_specs=pl.BlockSpec(memory_space=pltpu.HBM),
+        in_specs=[smem] * 3 + [anyspace] * len(pieces) + [vmem],
+        out_specs=hbm,
         out_shape=jax.ShapeDtypeStruct(cube.shape, F32),
         scratch_shapes=[
-            pltpu.VMEM((11 * local, rows, cols), F32),
+            pltpu.VMEM((10 * local, rows, cols), F32),
             pltpu.VMEM((local, scales) + plane, F32),
             pltpu.VMEM((scales,) + plane, F32),
             pltpu.VMEM((scales, cols // LANES, rows + 2 * EDGE, LANES), F32),
@@ -226,9 +247,9 @@
             pltpu.SemaphoreType.DMA((len(pieces),)),
             pltpu.SemaphoreType.DMA((local,)),
         ],
-        compiler_params=pltpu.CompilerParams(vmem_limit_bytes=18 * 2**20),
+        compiler_params=pltpu.CompilerParams(vmem_limit_bytes=11 * 2**20),
         name="denoise",
-    )(place, multipliers.T, noise_code.transpose(0, 2, 1), *[v for v, _ in pieces], column_matrices(cols))
+    )(place, multipliers.T, noise_code.transpose(0, 2, 1), *[v for v, _, _ in pieces], mats)
 
 
 def solution(mesh):

time: 48.3 us -> 39 us (0.81)
  the two profiles are of different devices: /device:TPU:9 before, /device:TPU:5 now
where the time goes in v3:
time: 39 us; the launch traced here: 38.7 us
  starting transfers between devices  15.6 us (40%)
  Pallas kernels  11.8 us (30%)
  waiting for transfers between devices  10 us (26%)
  local copies, waits for them, and re-layouts  1.09 us (3%)
    ppermute x10, starting transfers between devices, permute(): return lax.ppermute(v, 'chan', pairs(count, distance, phase))  14.3 us
    pallas_call x1, Pallas kernels, per_device(): pl.pallas_call(functools.partial(denoise_kernel, rows, cols, local, len(p...  11.5 us
    ppermute x10, waiting for transfers between devices, permute(): return lax.ppermute(v, 'chan', pairs(count, distance, phase))  10 us
    ppermute x1, starting transfers between devices, per_device(): far_lo = lax.ppermute(near[:cut], 'chan', relay)  1.29 us
    slice x1, local copies, waits for them, and re-layouts, per_device(): far_hi = permute(cube[cut:], 2, 1)  0.97 us
  transfers between devices with their start and end apart: 11, of which 5 were waited for; matrix products, arithmetic and copies ran while one was open for 3% of the time, Pallas kernels for 1%

profile of v3, /device:TPU:5, one launch (start us, length us, event | category | flops | bytes accessed | tf_op | source)
XLA Modules:
  0.0 38.7 jit_solution(14060667199209232666)
XLA Ops:
  0.0 0.0 copy-start
  0.0 0.0 collective-permute-start.2
  0.0 0.8 %collective-permute-start.1 = (f32[4,128,256]{2,1,0:T(8,128)}, f32[4,128,256]{2,1,0:T(8,128)S(1)}, u32[]{:S(2)}, u32[]{:S(2)}) collective-permute-start(f32[4,128,256]{2,1,0:T(8,128)} %cube.1), channel_id=1, source_target_pairs={{4,8},{5,9},{6,10},{7,11},{8,4},{9,5},{10,6},{11,7},{20,24},{21,25... | collective-permute-start | bytes 1572872 | tf_op jit(solution)/shard_map/ppermute | solution.py:205
  0.8 4.0 %collective-permute-start = (f32[4,128,256]{2,1,0:T(8,128)}, f32[4,128,256]{2,1,0:T(8,128)S(1)}, u32[]{:S(2)}, u32[]{:S(2)}) collective-permute-start(f32[4,128,256]{2,1,0:T(8,128)} %cube.1), channel_id=1, source_target_pairs={{0,4},{1,5},{2,6},{3,7},{4,0},{5,1},{6,2},{7,3},{8,12},{9,13},{10,... | collective-permute-start | bytes 1572872 | tf_op jit(solution)/shard_map/ppermute | solution.py:205
  4.8 1.5 %collective-permute-start.5 = (f32[4,128,256]{2,1,0:T(8,128)}, f32[4,128,256]{2,1,0:T(8,128)S(1)}, u32[]{:S(2)}, u32[]{:S(2)}) collective-permute-start(f32[4,128,256]{2,1,0:T(8,128)} %cube.1), channel_id=1, source_target_pairs={{0,1},{1,0},{2,3},{3,2},{4,5},{5,4},{6,7},{7,6},{8,9},{9,8},{10,11... | collective-permute-start | bytes 1572872 | tf_op jit(solution)/shard_map/ppermute | solution.py:205
  6.3 1.0 %slice.6 = f32[2,128,256]{2,1,0:T(8,128)S(1)} slice(f32[4,128,256]{2,1,0:T(8,128)} %cube.1), slice={[2:4], [0:128], [0:256]} | slice | bytes 524288 | tf_op jit(solution)/shard_map/slice | solution.py:213
  7.3 2.7 %collective-permute-start.3 = (f32[2,128,256]{2,1,0:T(8,128)S(1)}, f32[2,128,256]{2,1,0:T(8,128)S(1)}, u32[]{:S(2)}, u32[]{:S(2)}) collective-permute-start(f32[2,128,256]{2,1,0:T(8,128)S(1)} %slice.6), channel_id=1, source_target_pairs={{2,4},{3,5},{4,2},{5,3},{6,8},{7,9},{8,6},{9,7},{10,12},{11,13},{1... | collective-permute-start | bytes 786440 | tf_op jit(solution)/shard_map/ppermute | solution.py:205
  9.9 0.0 copy-done
  10.0 0.3 setup.1
  10.3 2.7 %collective-permute-done.2.refs_1_ = f32[4,128,256]{2,1,0:T(8,128)S(1)} collective-permute-done((f32[4,128,256]{2,1,0:T(8,128)}, f32[4,128,256]{2,1,0:T(8,128)S(1)}, u32[]{:S(2)}, u32[]{:S(2)}) %collective-permute-start.2) | collective-permute-done | bytes 524320 | tf_op jit(solution)/shard_map/ppermute | solution.py:205
  13.0 1.3 %collective-permute-start.4 = (f32[2,128,256]{2,1,0:T(8,128)S(1)}, f32[2,128,256]{2,1,0:T(8,128)}, u32[]{:S(2)}, u32[]{:S(2)}) collective-permute-start(f32[2,128,256]{2,1,0:T(8,128)S(1)} %slice.8), channel_id=1, source_target_pairs={{0,4},{1,5},{4,8},{5,9},{8,12},{9,13},{6,2},{7,3},{10,6},{11,7},{1... | collective-permute-start | bytes 786440 | tf_op jit(solution)/shard_map/ppermute | solution.py:214
  14.3 0.0 collective-permute-done.1.refs_3_
  14.3 1.7 %collective-permute-done.refs_2_ = f32[4,128,256]{2,1,0:T(8,128)S(1)} collective-permute-done((f32[4,128,256]{2,1,0:T(8,128)}, f32[4,128,256]{2,1,0:T(8,128)S(1)}, u32[]{:S(2)}, u32[]{:S(2)}) %collective-permute-start) | collective-permute-done | bytes 524320 | tf_op jit(solution)/shard_map/ppermute | solution.py:205
  16.0 3.0 %collective-permute-start.6 = (f32[4,128,256]{2,1,0:T(8,128)S(1)}, f32[4,128,256]{2,1,0:T(8,128)}, u32[]{:S(2)}, u32[]{:S(2)}) collective-permute-start(f32[4,128,256]{2,1,0:T(8,128)S(1)} %collective-permute-done.2.refs_1_), channel_id=1, source_target_pairs={{0,1},{1,0},{2,3},{3,2},{4,5},{5,4},{6,7},{7,6},{8,9},{9,8},{10,11... | collective-permute-start | bytes 1572872 | tf_op jit(solution)/shard_map/ppermute | solution.py:205
  19.0 0.0 collective-permute-start.7
  19.0 3.6 %collective-permute-done.3.refs_4_ = f32[2,128,256]{2,1,0:T(8,128)S(1)} collective-permute-done((f32[2,128,256]{2,1,0:T(8,128)S(1)}, f32[2,128,256]{2,1,0:T(8,128)S(1)}, u32[]{:S(2)}, u32[]{:S(2)}) %collective-permute-start.3) | collective-permute-done | bytes 262176 | tf_op jit(solution)/shard_map/ppermute | solution.py:205
  22.6 1.9 %collective-permute-start.8 = (f32[4,128,256]{2,1,0:T(8,128)S(1)}, f32[4,128,256]{2,1,0:T(8,128)}, u32[]{:S(2)}, u32[]{:S(2)}) collective-permute-start(f32[4,128,256]{2,1,0:T(8,128)S(1)} %collective-permute-done.1.refs_3_), channel_id=1, source_target_pairs={{0,1},{1,0},{2,3},{3,2},{4,5},{5,4},{6,7},{7,6},{8,9},{9,8},{10,11... | collective-permute-start | bytes 1572872 | tf_op jit(solution)/shard_map/ppermute | solution.py:205
  24.5 0.0 collective-permute-done.4.refs_5_
  24.5 0.0 collective-permute-start.9
  24.5 0.0 collective-permute-done.5.refs_6_
  24.5 0.5 %collective-permute-start.10 = (f32[2,128,256]{2,1,0:T(8,128)}, f32[2,128,256]{2,1,0:T(8,128)}, u32[]{:S(2)}, u32[]{:S(2)}) collective-permute-start(f32[2,128,256]{2,1,0:T(8,128)} %collective-permute-done.4.refs_5_), channel_id=1, source_target_pairs={{0,1},{1,0},{2,3},{3,2},{4,5},{5,4},{6,7},{7,6},{8,9},{9,8},{10,11... | collective-permute-start | bytes 786440 | tf_op jit(solution)/shard_map/ppermute | solution.py:205
  25.0 0.0 copy-start.1
  25.0 0.1 stack.52.place
  25.1 0.0 copy-start.2
  25.1 1.8 %collective-permute-done.9.refs_10_ = f32[2,128,256]{2,1,0:T(8,128)} collective-permute-done((f32[2,128,256]{2,1,0:T(8,128)S(1)}, f32[2,128,256]{2,1,0:T(8,128)}, u32[]{:S(2)}, u32[]{:S(2)}) %collective-permute-start.9) | collective-permute-done | bytes 262176 | tf_op jit(solution)/shard_map/ppermute | solution.py:205
  26.9 0.2 collective-permute-done.10.refs_11_
  27.1 0.0 collective-permute-done.6.refs_7_
  27.1 0.0 collective-permute-done.7.refs_8_
  27.1 0.0 collective-permute-done.8.refs_9_
  27.1 0.0 copy-done.1
  27.1 0.0 copy-done.2
  27.1 11.5 %denoise.1 = f32[4,128,256]{2,1,0:T(8,128)} custom-call(s32[14]{0:T(128)S(1)} %stack.52.place, s32[4,6]{1,0:T(4,128)S(1)} %bitcast.15, s32[4,4,6]{2,1,0:T(4,128)S(1)} %bitcast.14, f32[4,128,256]{2,1,0:T(8,128)S(1)} %get-tuple-element.16.refs_0_, f32[4,128,256]{2,1,0:T(8,128)S(1)} %collective-permute-done.2.refs_1_, ...), custom_call_target="tpu_custom_call" | custom-call | tf_op jit(solution)/shard_map/denoise/pallas_call | solution.py:235
  (1 shorter events, 0.0 us)
Async XLA Ops:
  0.0 9.9 %copy-start = (f32[4,128,256]{2,1,0:T(8,128)S(1)}, f32[4,128,256]{2,1,0:T(8,128)}, u32[]{:S(2)}) copy-start(f32[4,128,256]{2,1,0:T(8,128)} %cube.1) | copy-start | bytes 1572868
  0.0 13.0 %collective-permute-start.2 = (f32[4,128,256]{2,1,0:T(8,128)}, f32[4,128,256]{2,1,0:T(8,128)S(1)}, u32[]{:S(2)}, u32[]{:S(2)}) collective-permute-start(f32[4,128,256]{2,1,0:T(8,128)} %cube.1), channel_id=1, source_target_pairs={{0,2},{1,3},{2,0},{3,1},{4,6},{5,7},{6,4},{7,5},{8,10},{9,11},{10,... | collective-permute-start | bytes 1572872 | tf_op jit(solution)/shard_map/ppermute | solution.py:205
  0.0 14.3 %collective-permute-start.1 = (f32[4,128,256]{2,1,0:T(8,128)}, f32[4,128,256]{2,1,0:T(8,128)S(1)}, u32[]{:S(2)}, u32[]{:S(2)}) collective-permute-start(f32[4,128,256]{2,1,0:T(8,128)} %cube.1), channel_id=1, source_target_pairs={{4,8},{5,9},{6,10},{7,11},{8,4},{9,5},{10,6},{11,7},{20,24},{21,25... | collective-permute-start | bytes 1572872 | tf_op jit(solution)/shard_map/ppermute | solution.py:205
  0.8 15.2 %collective-permute-start = (f32[4,128,256]{2,1,0:T(8,128)}, f32[4,128,256]{2,1,0:T(8,128)S(1)}, u32[]{:S(2)}, u32[]{:S(2)}) collective-permute-start(f32[4,128,256]{2,1,0:T(8,128)} %cube.1), channel_id=1, source_target_pairs={{0,4},{1,5},{2,6},{3,7},{4,0},{5,1},{6,2},{7,3},{8,12},{9,13},{10,... | collective-permute-start | bytes 1572872 | tf_op jit(solution)/shard_map/ppermute | solution.py:205
  4.8 19.7 %collective-permute-start.5 = (f32[4,128,256]{2,1,0:T(8,128)}, f32[4,128,256]{2,1,0:T(8,128)S(1)}, u32[]{:S(2)}, u32[]{:S(2)}) collective-permute-start(f32[4,128,256]{2,1,0:T(8,128)} %cube.1), channel_id=1, source_target_pairs={{0,1},{1,0},{2,3},{3,2},{4,5},{5,4},{6,7},{7,6},{8,9},{9,8},{10,11... | collective-permute-start | bytes 1572872 | tf_op jit(solution)/shard_map/ppermute | solution.py:205
  7.3 15.3 %collective-permute-start.3 = (f32[2,128,256]{2,1,0:T(8,128)S(1)}, f32[2,128,256]{2,1,0:T(8,128)S(1)}, u32[]{:S(2)}, u32[]{:S(2)}) collective-permute-start(f32[2,128,256]{2,1,0:T(8,128)S(1)} %slice.6), channel_id=1, source_target_pairs={{2,4},{3,5},{4,2},{5,3},{6,8},{7,9},{8,6},{9,7},{10,12},{11,13},{1... | collective-permute-start | bytes 786440 | tf_op jit(solution)/shard_map/ppermute | solution.py:205
  13.0 11.4 %collective-permute-start.4 = (f32[2,128,256]{2,1,0:T(8,128)S(1)}, f32[2,128,256]{2,1,0:T(8,128)}, u32[]{:S(2)}, u32[]{:S(2)}) collective-permute-start(f32[2,128,256]{2,1,0:T(8,128)S(1)} %slice.8), channel_id=1, source_target_pairs={{0,4},{1,5},{4,8},{5,9},{8,12},{9,13},{6,2},{7,3},{10,6},{11,7},{1... | collective-permute-start | bytes 786440 | tf_op jit(solution)/shard_map/ppermute | solution.py:214
  16.0 11.1 %collective-permute-start.6 = (f32[4,128,256]{2,1,0:T(8,128)S(1)}, f32[4,128,256]{2,1,0:T(8,128)}, u32[]{:S(2)}, u32[]{:S(2)}) collective-permute-start(f32[4,128,256]{2,1,0:T(8,128)S(1)} %collective-permute-done.2.refs_1_), channel_id=1, source_target_pairs={{0,1},{1,0},{2,3},{3,2},{4,5},{5,4},{6,7},{7,6},{8,9},{9,8},{10,11... | collective-permute-start | bytes 1572872 | tf_op jit(solution)/shard_map/ppermute | solution.py:205
  19.0 8.1 %collective-permute-start.7 = (f32[4,128,256]{2,1,0:T(8,128)S(1)}, f32[4,128,256]{2,1,0:T(8,128)}, u32[]{:S(2)}, u32[]{:S(2)}) collective-permute-start(f32[4,128,256]{2,1,0:T(8,128)S(1)} %collective-permute-done.refs_2_), channel_id=1, source_target_pairs={{0,1},{1,0},{2,3},{3,2},{4,5},{5,4},{6,7},{7,6},{8,9},{9,8},{10,11... | collective-permute-start | bytes 1572872 | tf_op jit(solution)/shard_map/ppermute | solution.py:205
  22.6 4.5 %collective-permute-start.8 = (f32[4,128,256]{2,1,0:T(8,128)S(1)}, f32[4,128,256]{2,1,0:T(8,128)}, u32[]{:S(2)}, u32[]{:S(2)}) collective-permute-start(f32[4,128,256]{2,1,0:T(8,128)S(1)} %collective-permute-done.1.refs_3_), channel_id=1, source_target_pairs={{0,1},{1,0},{2,3},{3,2},{4,5},{5,4},{6,7},{7,6},{8,9},{9,8},{10,11... | collective-permute-start | bytes 1572872 | tf_op jit(solution)/shard_map/ppermute | solution.py:205
  24.5 2.4 %collective-permute-start.9 = (f32[2,128,256]{2,1,0:T(8,128)S(1)}, f32[2,128,256]{2,1,0:T(8,128)}, u32[]{:S(2)}, u32[]{:S(2)}) collective-permute-start(f32[2,128,256]{2,1,0:T(8,128)S(1)} %collective-permute-done.3.refs_4_), channel_id=1, source_target_pairs={{0,1},{1,0},{2,3},{3,2},{4,5},{5,4},{6,7},{7,6},{8,9},{9,8},{10,11... | collective-permute-start | bytes 786440 | tf_op jit(solution)/shard_map/ppermute | solution.py:205
  24.5 2.6 %collective-permute-start.10 = (f32[2,128,256]{2,1,0:T(8,128)}, f32[2,128,256]{2,1,0:T(8,128)}, u32[]{:S(2)}, u32[]{:S(2)}) collective-permute-start(f32[2,128,256]{2,1,0:T(8,128)} %collective-permute-done.4.refs_5_), channel_id=1, source_target_pairs={{0,1},{1,0},{2,3},{3,2},{4,5},{5,4},{6,7},{7,6},{8,9},{9,8},{10,11... | collective-permute-start | bytes 786440 | tf_op jit(solution)/shard_map/ppermute | solution.py:205
  25.0 2.1 %copy-start.1 = (s32[4,6,4]{1,2,0:T(4,128)S(1)}, s32[4,6,4]{1,2,0:T(4,128)}, u32[]{:S(2)}) copy-start(s32[4,6,4]{1,2,0:T(4,128)} %param.5) | copy-start | bytes 1156
  25.1 2.0 %copy-start.2 = (s32[6,4]{0,1:T(4,128)S(1)}, s32[6,4]{0,1:T(4,128)}, u32[]{:S(2)}) copy-start(s32[6,4]{0,1:T(4,128)} %param.4) | copy-start | bytes 292

commit v4 on v3

--- a/solution.py
+++ b/solution.py
@@ -50,36 +50,23 @@
     return hi, (x - hi.astype(F32)).astype(BF16)
 
 
-def denoise_kernel(rows, cols, local, pieces, place, mult, noise, *refs):
+def denoise_kernel(rows, cols, local, count, mult, noise, *refs):
+    pieces = 12
     ins = refs[:pieces]
     mats, out = refs[pieces : pieces + 2]
-    ext, detail, a, p, acc, done, sem, out_sem = refs[pieces + 2 :]
+    detail, a, p, acc, done, out_sem = refs[pieces + 2 :]
     halves = cols // LANES
     groups = rows // 8
-    centre = 4 * local
-    copies = [
-        pltpu.make_async_copy(ref, ext.at[pl.ds(place[2 + n], ref.shape[0])], sem.at[n])
-        for n, ref in enumerate(ins)
-    ]
-    for c in copies:
-        c.start()
+    me = lax.axis_index("chan").astype(jnp.int32)
     for s in range(SCALES_NU + 1):
         for h in range(halves):
             p[s, h, :EDGE] = jnp.zeros((EDGE, LANES), F32)
             p[s, h, EDGE + rows :] = jnp.zeros((EDGE, LANES), F32)
-    first, channels = place[0], place[1]
-    inside = {}
-    for k in list(range(-12, 0)) + list(range(local, local + 12)):
-        at = first + k
-        inside[k] = jnp.where((at >= 0) & (at < channels), 1.0, 0.0).astype(F32)
-    for c in copies:
-        c.wait()
-
-    def spectral(g, carry):
+    def spectral(where, inside, g, carry):
         r = pl.ds(pl.multiple_of(g * 8, 8), 8)
         for h in range(halves):
             lanes = pl.ds(h * LANES, LANES)
-            x = [ext[centre + k, r, lanes] for k in range(-REACH, local + REACH)]
+            x = [where[k][0][where[k][1], r, lanes] for k in range(-REACH, local + REACH)]
             c1 = spline4(x, -14, 1, -12, local + 12)
             c1 = [v * inside[k] if k in inside else v for k, v in enumerate(c1, -12)]
             c2 = spline4(c1, -12, 2, -8, local + 8)
@@ -96,15 +83,33 @@
                 detail[k, 3, h, r] = e3
         return carry
 
-    lax.fori_loop(0, groups, spectral, 0)
+    for turn in range(8):
+        beside = 1 - 2 * (turn % 2)
+        up2 = 2 - 4 * (turn // 2 % 2)
+        up4 = 4 - 8 * (turn // 4)
+        held = [(0, 0), (up2, 0), (up4, 0), (-up4, 0), (-up2, local // 2), (-up2, 0)]
+        held += [(block + beside, o) for block, o in held]
+        where = {}
+        for (block, o), ref in zip(held, ins):
+            for k in range(ref.shape[0]):
+                where[block * local + o + k] = (ref, k)
+
+        @pl.when(me % 8 == turn)
+        def _():
+            inside = {}
+            for k in range(-12, -local * turn):
+                inside[k] = (me > turn).astype(F32)
+            for k in range(local * (8 - turn), local + 12):
+                inside[k] = (me < count - 8 + turn).astype(F32)
+            lax.fori_loop(0, groups, functools.partial(spectral, where, inside), 0)
 
     def spatial(i, carry):
-        def limit(j, s):
-            return (mult[s, j] * noise[i, s, j]).astype(F32) * (1.0 / 1024.0)
-
-        def shrink(v, j, s):
-            lim = limit(j, s)
-            return v - jnp.clip(v, -lim, lim)
+        def limits(j, s):
+            level = jnp.full((8, LANES), (mult[s, j] * noise[i, s, j]).astype(F32) * (1.0 / 1024.0))
+            return -level, level
+
+        def shrink(v, ends):
+            return v - jnp.minimum(jnp.maximum(v, ends[0]), ends[1])
 
         def source(j, s):
             return detail.at[i, s] if j == 0 else a.at[s]
@@ -144,6 +149,7 @@
             return [6.0 * x[k] + 4.0 * near[k] + far[k] for k in range(groups)]
 
         for j in range(SCALES_XY):
+            ends = [limits(j, s) for s in range(SCALES_NU + 1)]
             for s in range(SCALES_NU + 1):
                 columns(j, s)
             for h in range(halves):
@@ -153,7 +159,7 @@
                     y = smooth_rows(j, s, h)
                     for k in range(groups):
                         r = pl.ds(8 * k, 8)
-                        v = shrink(src[h, r] - y[k], j, s)
+                        v = shrink(src[h, r] - y[k], ends[s])
                         a[s, h, r] = y[k]
                         total[k] = plus(total[k], v)
                 for k in range(groups):
@@ -162,11 +168,14 @@
                         acc[h, r] = total[k]
                     else:
                         acc[h, r] += total[k]
+        ends = [limits(SCALES_XY, s) for s in range(SCALES_NU)]
         for h in range(halves):
-            total = acc[h] + a[SCALES_NU, h]
-            for s in range(SCALES_NU):
-                total = total + shrink(a[s, h], SCALES_XY, s)
-            done[i, :, h * LANES : (h + 1) * LANES] = total
+            for k in range(groups):
+                r = pl.ds(8 * k, 8)
+                total = acc[h, r] + a[SCALES_NU, h, r]
+                for s in range(SCALES_NU):
+                    total = total + shrink(a[s, h, r], ends[s])
+                done[i, r, h * LANES : (h + 1) * LANES] = total
         pltpu.make_async_copy(done.at[i], out.at[i], out_sem.at[i]).start()
         return carry
 
@@ -190,12 +199,7 @@
 
 def per_device(count, cube, multipliers, noise_code):
     local, rows, cols = cube.shape
-    assert local == 4 and count % 2 == 0 and rows % 8 == 0 and cols % LANES == 0
-    me = lax.axis_index("chan").astype(jnp.int32)
-    core = me % 2
-    g2 = (me // 2) % 2
-    g4 = (me // 4) % 2
-    beside = 1 - 2 * core
+    assert local == 4 and count % 8 == 0 and rows % 8 == 0 and cols % LANES == 0
     smem = pl.BlockSpec(memory_space=pltpu.SMEM)
     hbm = pl.BlockSpec(memory_space=pltpu.HBM)
     vmem = pl.BlockSpec(memory_space=pltpu.VMEM)
@@ -224,32 +228,26 @@
     )(cube)
     two_a, two_b, near, here, mats = lax.optimization_barrier((two_a, two_b, near, here, mats))
     far_hi, far_lo = lax.optimization_barrier((far_hi, far_lo))
-    up2 = jnp.where(g2 == 0, 2, -2)
-    up4 = jnp.where(g4 == 0, 4, -4)
-    pieces = [(here, 0, 0), (near, up2, 0), (two_a, up4, 0), (two_b, -up4, 0), (far_hi, -up2, cut), (far_lo, -up2, 0)]
-    pieces += [(permute(cube if n == 0 else v, 1, 0), at + beside, o) for n, (v, at, o) in enumerate(pieces)]
-    place = [jnp.where(abs(at) > 4, 9, at + 4) * local + o for _, at, o in pieces]
-    place = jnp.stack([me * local, jnp.int32(count * local)] + place).astype(jnp.int32)
+    pieces = [here, near, two_a, two_b, far_hi, far_lo]
+    pieces += [permute(cube if n == 0 else v, 1, 0) for n, v in enumerate(pieces)]
     plane = (cols // LANES, rows, LANES)
     scales = SCALES_NU + 1
     return pl.pallas_call(
-        functools.partial(denoise_kernel, rows, cols, local, len(pieces)),
-        in_specs=[smem] * 3 + [anyspace] * len(pieces) + [vmem],
+        functools.partial(denoise_kernel, rows, cols, local, count),
+        in_specs=[smem] * 2 + [vmem] * len(pieces) + [vmem],
         out_specs=hbm,
         out_shape=jax.ShapeDtypeStruct(cube.shape, F32),
         scratch_shapes=[
-            pltpu.VMEM((10 * local, rows, cols), F32),
             pltpu.VMEM((local, scales) + plane, F32),
             pltpu.VMEM((scales,) + plane, F32),
             pltpu.VMEM((scales, cols // LANES, rows + 2 * EDGE, LANES), F32),
             pltpu.VMEM(plane, F32),
             pltpu.VMEM((local, rows, cols), F32),
-            pltpu.SemaphoreType.DMA((len(pieces),)),
             pltpu.SemaphoreType.DMA((local,)),
         ],
         compiler_params=pltpu.CompilerParams(vmem_limit_bytes=11 * 2**20),
         name="denoise",
-    )(place, multipliers.T, noise_code.transpose(0, 2, 1), *[v for v, _, _ in pieces], mats)
+    )(multipliers.T, noise_code.transpose(0, 2, 1), *pieces, mats)
 
 
 def solution(mesh):

time: 39 us -> 35.9 us (0.921)
  Pallas kernels: 11.8 us -> 9.09 us
    pallas_call x1, Pallas kernels: 11.5 us -> 8.8 us  [per_device(): pl.pallas_call(functools.partial(denoise_kernel, rows, cols, local, count...]
where the time goes in v4:
time: 35.9 us; the launch traced here: 35.6 us
  starting transfers between devices  15.6 us (43%)
  waiting for transfers between devices  9.78 us (27%)
  Pallas kernels  9.09 us (25%)
  local copies, waits for them, and re-layouts  1 us (3%)
    ppermute x10, starting transfers between devices, permute(): return lax.ppermute(v, 'chan', pairs(count, distance, phase))  14.3 us
    ppermute x10, waiting for transfers between devices, permute(): return lax.ppermute(v, 'chan', pairs(count, distance, phase))  9.78 us
    pallas_call x1, Pallas kernels, per_device(): pl.pallas_call(functools.partial(denoise_kernel, rows, cols, local, count...  8.8 us
    ppermute x1, starting transfers between devices, per_device(): far_lo = lax.ppermute(near[:cut], 'chan', relay)  1.29 us
    slice x1, local copies, waits for them, and re-layouts, per_device(): far_hi = permute(cube[cut:], 2, 1)  0.97 us
  transfers between devices with their start and end apart: 11, of which 5 were waited for; matrix products, arithmetic and copies ran while one was open for 3% of the time, Pallas kernels for 1%

profile of v4, /device:TPU:5, one launch (start us, length us, event | category | flops | bytes accessed | tf_op | source)
XLA Modules:
  0.0 35.6 jit_solution(16387175576037304072)
XLA Ops:
  0.0 0.0 copy-start
  0.0 0.0 collective-permute-start.2
  0.0 0.8 %collective-permute-start.1 = (f32[4,128,256]{2,1,0:T(8,128)}, f32[4,128,256]{2,1,0:T(8,128)S(1)}, u32[]{:S(2)}, u32[]{:S(2)}) collective-permute-start(f32[4,128,256]{2,1,0:T(8,128)} %cube.1), channel_id=1, source_target_pairs={{4,8},{5,9},{6,10},{7,11},{8,4},{9,5},{10,6},{11,7},{20,24},{21,25... | collective-permute-start | bytes 1572872 | tf_op jit(solution)/shard_map/ppermute | solution.py:209
  0.8 4.0 %collective-permute-start = (f32[4,128,256]{2,1,0:T(8,128)}, f32[4,128,256]{2,1,0:T(8,128)S(1)}, u32[]{:S(2)}, u32[]{:S(2)}) collective-permute-start(f32[4,128,256]{2,1,0:T(8,128)} %cube.1), channel_id=1, source_target_pairs={{0,4},{1,5},{2,6},{3,7},{4,0},{5,1},{6,2},{7,3},{8,12},{9,13},{10,... | collective-permute-start | bytes 1572872 | tf_op jit(solution)/shard_map/ppermute | solution.py:209
  4.8 1.5 %collective-permute-start.5 = (f32[4,128,256]{2,1,0:T(8,128)}, f32[4,128,256]{2,1,0:T(8,128)S(1)}, u32[]{:S(2)}, u32[]{:S(2)}) collective-permute-start(f32[4,128,256]{2,1,0:T(8,128)} %cube.1), channel_id=1, source_target_pairs={{0,1},{1,0},{2,3},{3,2},{4,5},{5,4},{6,7},{7,6},{8,9},{9,8},{10,11... | collective-permute-start | bytes 1572872 | tf_op jit(solution)/shard_map/ppermute | solution.py:209
  6.3 1.0 %slice.6 = f32[2,128,256]{2,1,0:T(8,128)S(1)} slice(f32[4,128,256]{2,1,0:T(8,128)} %cube.1), slice={[2:4], [0:128], [0:256]} | slice | bytes 524288 | tf_op jit(solution)/shard_map/slice | solution.py:217
  7.3 2.7 %collective-permute-start.3 = (f32[2,128,256]{2,1,0:T(8,128)S(1)}, f32[2,128,256]{2,1,0:T(8,128)S(1)}, u32[]{:S(2)}, u32[]{:S(2)}) collective-permute-start(f32[2,128,256]{2,1,0:T(8,128)S(1)} %slice.6), channel_id=1, source_target_pairs={{2,4},{3,5},{4,2},{5,3},{6,8},{7,9},{8,6},{9,7},{10,12},{11,13},{1... | collective-permute-start | bytes 786440 | tf_op jit(solution)/shard_map/ppermute | solution.py:209
  9.9 0.0 copy-done
  10.0 0.3 setup.1
  10.3 2.7 %collective-permute-done.2.refs_1_ = f32[4,128,256]{2,1,0:T(8,128)S(1)} collective-permute-done((f32[4,128,256]{2,1,0:T(8,128)}, f32[4,128,256]{2,1,0:T(8,128)S(1)}, u32[]{:S(2)}, u32[]{:S(2)}) %collective-permute-start.2) | collective-permute-done | bytes 524320 | tf_op jit(solution)/shard_map/ppermute | solution.py:209
  13.0 0.0 copy-start.1
  13.0 1.3 %collective-permute-start.4 = (f32[2,128,256]{2,1,0:T(8,128)S(1)}, f32[2,128,256]{2,1,0:T(8,128)S(1)}, u32[]{:S(2)}, u32[]{:S(2)}) collective-permute-start(f32[2,128,256]{2,1,0:T(8,128)S(1)} %slice.8), channel_id=1, source_target_pairs={{0,4},{1,5},{4,8},{5,9},{8,12},{9,13},{6,2},{7,3},{10,6},{11,7},{1... | collective-permute-start | bytes 786440 | tf_op jit(solution)/shard_map/ppermute | solution.py:218
  14.3 0.0 collective-permute-done.1.refs_3_
  14.3 1.7 %collective-permute-done.refs_2_ = f32[4,128,256]{2,1,0:T(8,128)S(1)} collective-permute-done((f32[4,128,256]{2,1,0:T(8,128)}, f32[4,128,256]{2,1,0:T(8,128)S(1)}, u32[]{:S(2)}, u32[]{:S(2)}) %collective-permute-start) | collective-permute-done | bytes 524320 | tf_op jit(solution)/shard_map/ppermute | solution.py:209
  16.0 0.0 copy-start.2
  16.0 3.0 %collective-permute-start.6 = (f32[4,128,256]{2,1,0:T(8,128)S(1)}, f32[4,128,256]{2,1,0:T(8,128)S(1)}, u32[]{:S(2)}, u32[]{:S(2)}) collective-permute-start(f32[4,128,256]{2,1,0:T(8,128)S(1)} %collective-permute-done.2.refs_1_), channel_id=1, source_target_pairs={{0,1},{1,0},{2,3},{3,2},{4,5},{5,4},{6,7},{7,6},{8,9},{9,8},{10,11... | collective-permute-start | bytes 1572872 | tf_op jit(solution)/shard_map/ppermute | solution.py:209
  19.0 0.0 collective-permute-start.7
  19.0 3.6 %collective-permute-done.3.refs_4_ = f32[2,128,256]{2,1,0:T(8,128)S(1)} collective-permute-done((f32[2,128,256]{2,1,0:T(8,128)S(1)}, f32[2,128,256]{2,1,0:T(8,128)S(1)}, u32[]{:S(2)}, u32[]{:S(2)}) %collective-permute-start.3) | collective-permute-done | bytes 262176 | tf_op jit(solution)/shard_map/ppermute | solution.py:209
  22.6 1.9 %collective-permute-start.8 = (f32[4,128,256]{2,1,0:T(8,128)S(1)}, f32[4,128,256]{2,1,0:T(8,128)S(1)}, u32[]{:S(2)}, u32[]{:S(2)}) collective-permute-start(f32[4,128,256]{2,1,0:T(8,128)S(1)} %collective-permute-done.1.refs_3_), channel_id=1, source_target_pairs={{0,1},{1,0},{2,3},{3,2},{4,5},{5,4},{6,7},{7,6},{8,9},{9,8},{10,11... | collective-permute-start | bytes 1572872 | tf_op jit(solution)/shard_map/ppermute | solution.py:209
  24.5 0.0 collective-permute-done.4.refs_5_
  24.5 0.0 collective-permute-start.9
  24.5 0.0 collective-permute-done.5.refs_6_
  24.5 0.5 %collective-permute-start.10 = (f32[2,128,256]{2,1,0:T(8,128)S(1)}, f32[2,128,256]{2,1,0:T(8,128)S(1)}, u32[]{:S(2)}, u32[]{:S(2)}) collective-permute-start(f32[2,128,256]{2,1,0:T(8,128)S(1)} %collective-permute-done.4.refs_5_), channel_id=1, source_target_pairs={{0,1},{1,0},{2,3},{3,2},{4,5},{5,4},{6,7},{7,6},{8,9},{9,8},{10,11... | collective-permute-start | bytes 786440 | tf_op jit(solution)/shard_map/ppermute | solution.py:209
  25.0 1.4 %collective-permute-done.9.refs_10_ = f32[2,128,256]{2,1,0:T(8,128)S(1)} collective-permute-done((f32[2,128,256]{2,1,0:T(8,128)S(1)}, f32[2,128,256]{2,1,0:T(8,128)S(1)}, u32[]{:S(2)}, u32[]{:S(2)}) %collective-permute-start.9) | collective-permute-done | bytes 262176 | tf_op jit(solution)/shard_map/ppermute | solution.py:209
  26.4 0.4 %collective-permute-done.10.refs_11_ = f32[2,128,256]{2,1,0:T(8,128)S(1)} collective-permute-done((f32[2,128,256]{2,1,0:T(8,128)S(1)}, f32[2,128,256]{2,1,0:T(8,128)S(1)}, u32[]{:S(2)}, u32[]{:S(2)}) %collective-permute-start.10) | collective-permute-done | bytes 262176 | tf_op jit(solution)/shard_map/ppermute | solution.py:209
  26.7 0.0 collective-permute-done.6.refs_7_
  26.7 0.0 collective-permute-done.7.refs_8_
  26.7 0.0 collective-permute-done.8.refs_9_
  26.8 0.0 copy-done.1
  26.8 0.0 copy-done.2
  26.8 8.8 %denoise.1 = f32[4,128,256]{2,1,0:T(8,128)} custom-call(s32[4,6]{1,0:T(4,128)S(1)} %bitcast.3, s32[4,4,6]{2,1,0:T(4,128)S(1)} %bitcast.2, f32[4,128,256]{2,1,0:T(8,128)S(1)} %get-tuple-element.16.refs_0_, f32[4,128,256]{2,1,0:T(8,128)S(1)} %collective-permute-done.2.refs_1_, f32[4,128,256]{2,1,0:T(8,128)S(1)} %collective-permute-done.refs_2_, ...), custom_call_target="tpu_custom_call" | custom-call | tf_op jit(solution)/shard_map/denoise/pallas_call | solution.py:235
  (1 shorter events, 0.0 us)
Async XLA Ops:
  0.0 9.9 %copy-start = (f32[4,128,256]{2,1,0:T(8,128)S(1)}, f32[4,128,256]{2,1,0:T(8,128)}, u32[]{:S(2)}) copy-start(f32[4,128,256]{2,1,0:T(8,128)} %cube.1) | copy-start | bytes 1572868
  0.0 13.0 %collective-permute-start.2 = (f32[4,128,256]{2,1,0:T(8,128)}, f32[4,128,256]{2,1,0:T(8,128)S(1)}, u32[]{:S(2)}, u32[]{:S(2)}) collective-permute-start(f32[4,128,256]{2,1,0:T(8,128)} %cube.1), channel_id=1, source_target_pairs={{0,2},{1,3},{2,0},{3,1},{4,6},{5,7},{6,4},{7,5},{8,10},{9,11},{10,... | collective-permute-start | bytes 1572872 | tf_op jit(solution)/shard_map/ppermute | solution.py:209
  0.0 14.3 %collective-permute-start.1 = (f32[4,128,256]{2,1,0:T(8,128)}, f32[4,128,256]{2,1,0:T(8,128)S(1)}, u32[]{:S(2)}, u32[]{:S(2)}) collective-permute-start(f32[4,128,256]{2,1,0:T(8,128)} %cube.1), channel_id=1, source_target_pairs={{4,8},{5,9},{6,10},{7,11},{8,4},{9,5},{10,6},{11,7},{20,24},{21,25... | collective-permute-start | bytes 1572872 | tf_op jit(solution)/shard_map/ppermute | solution.py:209
  0.8 15.2 %collective-permute-start = (f32[4,128,256]{2,1,0:T(8,128)}, f32[4,128,256]{2,1,0:T(8,128)S(1)}, u32[]{:S(2)}, u32[]{:S(2)}) collective-permute-start(f32[4,128,256]{2,1,0:T(8,128)} %cube.1), channel_id=1, source_target_pairs={{0,4},{1,5},{2,6},{3,7},{4,0},{5,1},{6,2},{7,3},{8,12},{9,13},{10,... | collective-permute-start | bytes 1572872 | tf_op jit(solution)/shard_map/ppermute | solution.py:209
  4.8 19.7 %collective-permute-start.5 = (f32[4,128,256]{2,1,0:T(8,128)}, f32[4,128,256]{2,1,0:T(8,128)S(1)}, u32[]{:S(2)}, u32[]{:S(2)}) collective-permute-start(f32[4,128,256]{2,1,0:T(8,128)} %cube.1), channel_id=1, source_target_pairs={{0,1},{1,0},{2,3},{3,2},{4,5},{5,4},{6,7},{7,6},{8,9},{9,8},{10,11... | collective-permute-start | bytes 1572872 | tf_op jit(solution)/shard_map/ppermute | solution.py:209
  7.3 15.3 %collective-permute-start.3 = (f32[2,128,256]{2,1,0:T(8,128)S(1)}, f32[2,128,256]{2,1,0:T(8,128)S(1)}, u32[]{:S(2)}, u32[]{:S(2)}) collective-permute-start(f32[2,128,256]{2,1,0:T(8,128)S(1)} %slice.6), channel_id=1, source_target_pairs={{2,4},{3,5},{4,2},{5,3},{6,8},{7,9},{8,6},{9,7},{10,12},{11,13},{1... | collective-permute-start | bytes 786440 | tf_op jit(solution)/shard_map/ppermute | solution.py:209
  13.0 13.8 %copy-start.1 = (s32[4,6,4]{1,2,0:T(4,128)S(1)}, s32[4,6,4]{1,2,0:T(4,128)}, u32[]{:S(2)}) copy-start(s32[4,6,4]{1,2,0:T(4,128)} %param.5) | copy-start | bytes 1156
  13.0 11.4 %collective-permute-start.4 = (f32[2,128,256]{2,1,0:T(8,128)S(1)}, f32[2,128,256]{2,1,0:T(8,128)S(1)}, u32[]{:S(2)}, u32[]{:S(2)}) collective-permute-start(f32[2,128,256]{2,1,0:T(8,128)S(1)} %slice.8), channel_id=1, source_target_pairs={{0,4},{1,5},{4,8},{5,9},{8,12},{9,13},{6,2},{7,3},{10,6},{11,7},{1... | collective-permute-start | bytes 786440 | tf_op jit(solution)/shard_map/ppermute | solution.py:218
  16.0 10.8 %copy-start.2 = (s32[6,4]{0,1:T(4,128)S(1)}, s32[6,4]{0,1:T(4,128)}, u32[]{:S(2)}) copy-start(s32[6,4]{0,1:T(4,128)} %param.4) | copy-start | bytes 292
  16.0 10.7 %collective-permute-start.6 = (f32[4,128,256]{2,1,0:T(8,128)S(1)}, f32[4,128,256]{2,1,0:T(8,128)S(1)}, u32[]{:S(2)}, u32[]{:S(2)}) collective-permute-start(f32[4,128,256]{2,1,0:T(8,128)S(1)} %collective-permute-done.2.refs_1_), channel_id=1, source_target_pairs={{0,1},{1,0},{2,3},{3,2},{4,5},{5,4},{6,7},{7,6},{8,9},{9,8},{10,11... | collective-permute-start | bytes 1572872 | tf_op jit(solution)/shard_map/ppermute | solution.py:209
  19.0 7.7 %collective-permute-start.7 = (f32[4,128,256]{2,1,0:T(8,128)S(1)}, f32[4,128,256]{2,1,0:T(8,128)S(1)}, u32[]{:S(2)}, u32[]{:S(2)}) collective-permute-start(f32[4,128,256]{2,1,0:T(8,128)S(1)} %collective-permute-done.refs_2_), channel_id=1, source_target_pairs={{0,1},{1,0},{2,3},{3,2},{4,5},{5,4},{6,7},{7,6},{8,9},{9,8},{10,11... | collective-permute-start | bytes 1572872 | tf_op jit(solution)/shard_map/ppermute | solution.py:209
  22.6 4.2 %collective-permute-start.8 = (f32[4,128,256]{2,1,0:T(8,128)S(1)}, f32[4,128,256]{2,1,0:T(8,128)S(1)}, u32[]{:S(2)}, u32[]{:S(2)}) collective-permute-start(f32[4,128,256]{2,1,0:T(8,128)S(1)} %collective-permute-done.1.refs_3_), channel_id=1, source_target_pairs={{0,1},{1,0},{2,3},{3,2},{4,5},{5,4},{6,7},{7,6},{8,9},{9,8},{10,11... | collective-permute-start | bytes 1572872 | tf_op jit(solution)/shard_map/ppermute | solution.py:209
  24.5 1.9 %collective-permute-start.9 = (f32[2,128,256]{2,1,0:T(8,128)S(1)}, f32[2,128,256]{2,1,0:T(8,128)S(1)}, u32[]{:S(2)}, u32[]{:S(2)}) collective-permute-start(f32[2,128,256]{2,1,0:T(8,128)S(1)} %collective-permute-done.3.refs_4_), channel_id=1, source_target_pairs={{0,1},{1,0},{2,3},{3,2},{4,5},{5,4},{6,7},{7,6},{8,9},{9,8},{10,11... | collective-permute-start | bytes 786440 | tf_op jit(solution)/shard_map/ppermute | solution.py:209
  24.5 2.3 %collective-permute-start.10 = (f32[2,128,256]{2,1,0:T(8,128)S(1)}, f32[2,128,256]{2,1,0:T(8,128)S(1)}, u32[]{:S(2)}, u32[]{:S(2)}) collective-permute-start(f32[2,128,256]{2,1,0:T(8,128)S(1)} %collective-permute-done.4.refs_5_), channel_id=1, source_target_pairs={{0,1},{1,0},{2,3},{3,2},{4,5},{5,4},{6,7},{7,6},{8,9},{9,8},{10,11... | collective-permute-start | bytes 786440 | tf_op jit(solution)/shard_map/ppermute | solution.py:209

commit v5 on v4

--- a/solution.py
+++ b/solution.py
@@ -2,6 +2,7 @@
 
 import jax
 import jax.numpy as jnp
+import numpy as np
 from jax import lax
 from jax.experimental import pallas as pl
 from jax.experimental.pallas import tpu as pltpu
@@ -38,70 +39,68 @@
     return values[k] if 0 <= k < len(values) else None
 
 
-def spline4(values, first, step, lo, hi):
-    cur = dict(enumerate(values, first))
-    for shift in (-1, -1, 1, 1):
-        cur = {k: v + cur[k + shift * step] for k, v in cur.items() if k + shift * step in cur}
-    return [cur[k] for k in range(lo, hi)]
-
-
 def split(x):
     hi = x.astype(BF16)
     return hi, (x - hi.astype(F32)).astype(BF16)
 
 
-def denoise_kernel(rows, cols, local, count, mult, noise, *refs):
-    pieces = 12
-    ins = refs[:pieces]
-    mats, out = refs[pieces : pieces + 2]
-    detail, a, p, acc, done, out_sem = refs[pieces + 2 :]
+def smooths(local, table, planes):
+    hi, lo = split(jnp.concatenate(planes, 0))
+    y = jnp.dot(table[...], hi, preferred_element_type=F32)
+    z = jnp.dot(table[: 8 * SCALES_NU * local], lo, preferred_element_type=F32)
+    out = []
+    for s in range(SCALES_NU):
+        row = []
+        for k in range(local):
+            at = 8 * (s * local + k)
+            v = y[at : at + 8] + z[at : at + 8]
+            if s == SCALES_NU - 1:
+                v = v + y[at + 8 * local : at + 8 * local + 8]
+            row.append(v)
+        out.append(row)
+    return out
+
+
+def spectral_kernel(rows, cols, local, here, near, two_a, two_b, far_hi, far_lo, here2, near2, two_a2, two_b2, table, detail):
+    me = lax.axis_index("chan").astype(jnp.int32)
+    half = local // 2
+    edge_a = half * ((me // 4) % 2)
+    edge_b = half - edge_a
+    for g in range(rows // 8):
+        r = pl.ds(8 * g, 8)
+        planes = [here[k, r] for k in range(local)] + [near[k, r] for k in range(local)]
+        planes += [two_a[edge_a + k, r] for k in range(half)] + [two_b[edge_b + k, r] for k in range(half)]
+        planes += [far_hi[k, r] for k in range(half)] + [far_lo[k, r] for k in range(half)]
+        for ref in (here2, near2, two_a2, two_b2):
+            planes += [ref[k, r] for k in range(local)]
+        e = [planes[:local]] + smooths(local, table, planes)
+        for k in range(local):
+            for s in range(SCALES_NU + 1):
+                d = e[s][k] - e[s + 1][k] if s < SCALES_NU else e[s][k]
+                for h in range(cols // LANES):
+                    detail[k, s, h, r] = d[:, h * LANES : (h + 1) * LANES]
+
+
+def denoise_kernel(rows, cols, local, mult, noise, far_hi2, far_lo2, table, partial, mats, out, *scratch):
+    detail, a, p, acc, done, out_sem = scratch
     halves = cols // LANES
     groups = rows // 8
-    me = lax.axis_index("chan").astype(jnp.int32)
+    half = local // 2
     for s in range(SCALES_NU + 1):
         for h in range(halves):
             p[s, h, :EDGE] = jnp.zeros((EDGE, LANES), F32)
             p[s, h, EDGE + rows :] = jnp.zeros((EDGE, LANES), F32)
-    def spectral(where, inside, g, carry):
-        r = pl.ds(pl.multiple_of(g * 8, 8), 8)
-        for h in range(halves):
-            lanes = pl.ds(h * LANES, LANES)
-            x = [where[k][0][where[k][1], r, lanes] for k in range(-REACH, local + REACH)]
-            c1 = spline4(x, -14, 1, -12, local + 12)
-            c1 = [v * inside[k] if k in inside else v for k, v in enumerate(c1, -12)]
-            c2 = spline4(c1, -12, 2, -8, local + 8)
-            c2 = [v * inside[k] if k in inside else v for k, v in enumerate(c2, -8)]
-            c3 = spline4(c2, -8, 4, 0, local)
-            for k in range(local):
-                e0 = x[k + 14]
-                e1 = c1[k + 12] * (1.0 / 16.0)
-                e2 = c2[k + 8] * (1.0 / 256.0)
-                e3 = c3[k] * (1.0 / 4096.0)
-                detail[k, 0, h, r] = e0 - e1
-                detail[k, 1, h, r] = e1 - e2
-                detail[k, 2, h, r] = e2 - e3
-                detail[k, 3, h, r] = e3
-        return carry
-
-    for turn in range(8):
-        beside = 1 - 2 * (turn % 2)
-        up2 = 2 - 4 * (turn // 2 % 2)
-        up4 = 4 - 8 * (turn // 4)
-        held = [(0, 0), (up2, 0), (up4, 0), (-up4, 0), (-up2, local // 2), (-up2, 0)]
-        held += [(block + beside, o) for block, o in held]
-        where = {}
-        for (block, o), ref in zip(held, ins):
-            for k in range(ref.shape[0]):
-                where[block * local + o + k] = (ref, k)
-
-        @pl.when(me % 8 == turn)
-        def _():
-            inside = {}
-            for k in range(-12, -local * turn):
-                inside[k] = (me > turn).astype(F32)
-            for k in range(local * (8 - turn), local + 12):
-                inside[k] = (me < count - 8 + turn).astype(F32)
-            lax.fori_loop(0, groups, functools.partial(spectral, where, inside), 0)
+    for g in range(groups):
+        r = pl.ds(8 * g, 8)
+        e = smooths(local, table, [far_lo2[k, r] for k in range(half)] + [far_hi2[k, r] for k in range(half)])
+        for k in range(local):
+            for s in range(SCALES_NU + 1):
+                if s == 0:
+                    d = -e[0][k]
+                else:
+                    d = e[s - 1][k] - e[s][k] if s < SCALES_NU else e[s - 1][k]
+                for h in range(halves):
+                    detail[k, s, h, r] = partial[k, s, h, r] + d[:, h * LANES : (h + 1) * LANES]
 
     def spatial(i, carry):
         def limits(j, s):
@@ -184,8 +183,50 @@
         pltpu.make_async_copy(done.at[i], out.at[i], out_sem.at[i]).wait()
 
 
-def setup_kernel(cols, cube, copy, mats, sem):
-    fetch = pltpu.make_async_copy(cube, copy, sem)
+def places(i, local):
+    beside = 1 - 2 * (i % 2)
+    up2 = 2 - 4 * (i // 2 % 2)
+    up4 = 4 - 8 * (i // 4 % 2)
+    half = local // 2
+
+    def block(at, lo=0, hi=local):
+        return [at * local + o for o in range(lo, hi)]
+
+    def edge(at):
+        return block(at, half) if at < 0 else block(at, 0, half)
+
+    early = block(0) + block(up2) + edge(up4) + edge(-up4) + block(-up2, half) + block(-up2, 0, half)
+    for at in (0, up2, up4, -up4):
+        early += block(at + beside)
+    return early, block(-up2 + beside)
+
+
+def spectral_tables(count, local):
+    n = count * local
+    whole = np.eye(n)
+    parts = []
+    for s in range(SCALES_NU):
+        whole = sum(w / 16.0 * np.eye(n, k=(k - 2) * 2**s) for k, w in enumerate(TAPS)) @ whole
+        parts.append(whole)
+    hi = parts[-1].astype(BF16).astype(np.float64)
+    parts[-1:] = [hi, parts[-1] - hi]
+    tables = [], []
+    for i in range(count):
+        own = np.concatenate([p[i * local : (i + 1) * local] for p in parts])
+        both = places(i, local)
+        seen = [at for at in both[0] + both[1] if -REACH <= at < local + REACH]
+        assert sorted(seen) == list(range(-REACH, local + REACH))
+        for table, held in zip(tables, both):
+            taps = np.zeros((own.shape[0], len(held)))
+            for c, at in enumerate(held):
+                if 0 <= i * local + at < n:
+                    taps[:, c] = own[:, i * local + at]
+            table.append(np.kron(taps, np.eye(8)))
+    return [jnp.asarray(np.stack(t), BF16) for t in tables]
+
+
+def setup_kernel(cols, cube, here, mats, sem):
+    fetch = pltpu.make_async_copy(cube, here, sem)
     fetch.start()
     row = lax.broadcasted_iota(jnp.int32, (cols, cols), 0)
     offset = lax.broadcasted_iota(jnp.int32, (cols, cols), 1) - row
@@ -214,7 +255,10 @@
     near = permute(cube, 2, 0)
     two_a = permute(cube, 4, 0)
     two_b = permute(cube, 4, 1)
-    far_hi = permute(cube[cut:], 2, 1)
+    me = lax.axis_index("chan")
+    early, late = [lax.dynamic_index_in_dim(t, me, 0, False) for t in spectral_tables(count, local)]
+    upper, early, late = lax.optimization_barrier((cube[cut:], early, late))
+    far_hi = permute(upper, 2, 1)
     far_lo = lax.ppermute(near[:cut], "chan", relay)
     here, mats = pl.pallas_call(
         functools.partial(setup_kernel, cols),
@@ -229,12 +273,21 @@
     two_a, two_b, near, here, mats = lax.optimization_barrier((two_a, two_b, near, here, mats))
     far_hi, far_lo = lax.optimization_barrier((far_hi, far_lo))
     pieces = [here, near, two_a, two_b, far_hi, far_lo]
-    pieces += [permute(cube if n == 0 else v, 1, 0) for n, v in enumerate(pieces)]
+    passed = [permute(cube if n == 0 else v, 1, 0) for n, v in enumerate(pieces)]
     plane = (cols // LANES, rows, LANES)
     scales = SCALES_NU + 1
+    partial = pl.pallas_call(
+        functools.partial(spectral_kernel, rows, cols, local),
+        in_specs=[vmem] * 11,
+        out_specs=vmem,
+        out_shape=jax.ShapeDtypeStruct((local, scales) + plane, F32),
+        compiler_params=pltpu.CompilerParams(vmem_limit_bytes=11 * 2**20),
+        cost_estimate=pl.CostEstimate(flops=1, bytes_accessed=1, transcendentals=0),
+        name="spectral",
+    )(*pieces, *passed[:4], early)
     return pl.pallas_call(
-        functools.partial(denoise_kernel, rows, cols, local, count),
-        in_specs=[smem] * 2 + [vmem] * len(pieces) + [vmem],
+        functools.partial(denoise_kernel, rows, cols, local),
+        in_specs=[smem] * 2 + [vmem] * 5,
         out_specs=hbm,
         out_shape=jax.ShapeDtypeStruct(cube.shape, F32),
         scratch_shapes=[
@@ -247,7 +300,7 @@
         ],
         compiler_params=pltpu.CompilerParams(vmem_limit_bytes=11 * 2**20),
         name="denoise",
-    )(multipliers.T, noise_code.transpose(0, 2, 1), *pieces, mats)
+    )(multipliers.T, noise_code.transpose(0, 2, 1), *passed[4:], late, partial, mats)
 
 
 def solution(mesh):

time: 35.9 us -> 35.4 us (0.986)
  waiting for transfers between devices: 9.78 us -> 6.4 us
  local copies, waits for them, and re-layouts: 1 us -> 3.66 us
    ppermute x10, waiting for transfers between devices: 9.78 us -> 3.37 us  [permute(): return lax.ppermute(v, 'chan', pairs(count, distance, phase))]
    ppermute x1, waiting for transfers between devices: 0.01 us -> 3.03 us  [per_device(): far_lo = lax.ppermute(near[:cut], 'chan', relay)]
    squeeze x0 -> x2, local copies, waits for them, and re-layouts: none -> 1.61 us  [per_device(): lax.dynamic_index_in_dim(t, me, 0, False)]
    unnamed x6, local copies, waits for them, and re-layouts: 0.01 us -> 1.05 us
    pallas_call x1 -> x2, Pallas kernels: 8.8 us -> 8.99 us  [the longest x1 8 us: per_device(): pl.pallas_call(functools.partial(denoise_kernel, rows, cols, local), in_s...]
  transfers between devices with their start and end apart: 11 -> 11, of which waited for: 5 -> 4; matrix products, arithmetic and copies ran while one was open for 3% -> 7% of each run, Pallas kernels for 1% -> 4%
where the time goes in v5:
time: 35.4 us; the launch traced here: 34.9 us
  starting transfers between devices  15.4 us (44%)
  Pallas kernels  9.28 us (26%)
  waiting for transfers between devices  6.4 us (18%)
  local copies, waits for them, and re-layouts  3.66 us (10%)
    ppermute x10, starting transfers between devices, permute(): return lax.ppermute(v, 'chan', pairs(count, distance, phase))  14.1 us
    pallas_call x1, Pallas kernels, per_device(): pl.pallas_call(functools.partial(denoise_kernel, rows, cols, local), in_s...  8 us
    ppermute x10, waiting for transfers between devices, permute(): return lax.ppermute(v, 'chan', pairs(count, distance, phase))  3.37 us
    ppermute x1, waiting for transfers between devices, per_device(): far_lo = lax.ppermute(near[:cut], 'chan', relay)  3.03 us
    squeeze x2, local copies, waits for them, and re-layouts, per_device(): lax.dynamic_index_in_dim(t, me, 0, False)  1.61 us
    ppermute x1, starting transfers between devices, per_device(): far_lo = lax.ppermute(near[:cut], 'chan', relay)  1.29 us
    unnamed x6, local copies, waits for them, and re-layouts  1.05 us
    pallas_call x1, Pallas kernels, per_device(): pl.pallas_call(functools.partial(spectral_kernel, rows, cols, local), in_...  0.99 us
  transfers between devices with their start and end apart: 11, of which 4 were waited for; matrix products, arithmetic and copies ran while one was open for 7% of the time, Pallas kernels for 4%

profile of v5, /device:TPU:5, one launch (start us, length us, event | category | flops | bytes accessed | tf_op | source)
XLA Modules:
  0.0 34.9 jit_solution(9306090841219223449)
XLA Ops:
  0.0 0.0 collective-permute-start.1
  0.0 1.5 %collective-permute-start.5 = (f32[4,128,256]{2,1,0:T(8,128)}, f32[4,128,256]{2,1,0:T(8,128)S(1)}, u32[]{:S(2)}, u32[]{:S(2)}) collective-permute-start(f32[4,128,256]{2,1,0:T(8,128)} %cube.1), channel_id=1, source_target_pairs={{0,4},{1,5},{2,6},{3,7},{4,0},{5,1},{6,2},{7,3},{8,12},{9,13},{10,... | collective-permute-start | bytes 1572872 | tf_op jit(solution)/shard_map/ppermute | solution.py:250
  1.5 0.7 %collective-permute-start.6 = (f32[4,128,256]{2,1,0:T(8,128)}, f32[4,128,256]{2,1,0:T(8,128)S(1)}, u32[]{:S(2)}, u32[]{:S(2)}) collective-permute-start(f32[4,128,256]{2,1,0:T(8,128)} %cube.1), channel_id=1, source_target_pairs={{4,8},{5,9},{6,10},{7,11},{8,4},{9,5},{10,6},{11,7},{20,24},{21,25... | collective-permute-start | bytes 1572872 | tf_op jit(solution)/shard_map/ppermute | solution.py:250
  2.2 1.0 %slice.6 = f32[2,128,256]{2,1,0:T(8,128)S(1)} slice(f32[4,128,256]{2,1,0:T(8,128)} %cube.1), slice={[2:4], [0:128], [0:256]} | slice | bytes 524288 | tf_op jit(solution)/shard_map/slice | solution.py:260
  3.2 0.8 %dynamic-slice_bitcast_fusion.1.table = bf16[128,32]{1,0:T(8,128)(2,1)S(1)} fusion(bf16[16,128,32]{2,1,0:T(8,128)(2,1)} %constant.19.clone, s32[]{:T(128)S(6)} %select_n.6), kind=kLoop, calls=%fused_computation.1 | loop fusion | bytes 16388 | tf_op jit(solution)/shard_map/jit(dynamic_index_in_dim)/squeeze | solution.py:259
  4.0 0.8 %dynamic-slice_bitcast_fusion.table = bf16[128,256]{1,0:T(8,128)(2,1)S(1)} fusion(bf16[16,128,256]{2,1,0:T(8,128)(2,1)} %constant.18.clone, s32[]{:T(128)S(6)} %select_n.6), kind=kLoop, calls=%fused_computation | loop fusion | bytes 131076 | tf_op jit(solution)/shard_map/jit(dynamic_index_in_dim)/squeeze | solution.py:259
  4.8 6.7 %collective-permute-start = (f32[2,128,256]{2,1,0:T(8,128)S(1)}, f32[2,128,256]{2,1,0:T(8,128)S(1)}, u32[]{:S(2)}, u32[]{:S(2)}) collective-permute-start(f32[2,128,256]{2,1,0:T(8,128)S(1)} %slice.6), channel_id=1, source_target_pairs={{2,4},{3,5},{4,2},{5,3},{6,8},{7,9},{8,6},{9,7},{10,12},{11,13},{1... | collective-permute-start | bytes 786440 | tf_op jit(solution)/shard_map/ppermute | solution.py:250
  11.5 1.9 %collective-permute-start.7 = (f32[4,128,256]{2,1,0:T(8,128)}, f32[4,128,256]{2,1,0:T(8,128)S(1)}, u32[]{:S(2)}, u32[]{:S(2)}) collective-permute-start(f32[4,128,256]{2,1,0:T(8,128)} %cube.1), channel_id=1, source_target_pairs={{0,1},{1,0},{2,3},{3,2},{4,5},{5,4},{6,7},{7,6},{8,9},{9,8},{10,11... | collective-permute-start | bytes 1572872 | tf_op jit(solution)/shard_map/ppermute | solution.py:250
  13.3 1.0 %copy-done = f32[4,128,256]{2,1,0:T(8,128)S(1)} copy-done((f32[4,128,256]{2,1,0:T(8,128)S(1)}, f32[4,128,256]{2,1,0:T(8,128)}, u32[]{:S(2)}) %copy-start) | copy-done | bytes 524312
  14.4 0.3 setup.1
  14.7 0.0 collective-permute-done.1.near
  14.7 1.3 %collective-permute-start.2 = (f32[2,128,256]{2,1,0:T(8,128)S(1)}, f32[2,128,256]{2,1,0:T(8,128)S(1)}, u32[]{:S(2)}, u32[]{:S(2)}) collective-permute-start(f32[2,128,256]{2,1,0:T(8,128)S(1)} %slice.8), channel_id=1, source_target_pairs={{0,4},{1,5},{4,8},{5,9},{8,12},{9,13},{6,2},{7,3},{10,6},{11,7},{1... | collective-permute-start | bytes 786440 | tf_op jit(solution)/shard_map/ppermute | solution.py:262
  16.0 0.0 collective-permute-done.5.two_a
  16.0 0.0 collective-permute-done.6.two_b
  16.0 0.0 copy-start.1
  16.1 0.0 copy-start.2
  16.1 0.2 collective-permute-start.10
  16.3 0.4 %collective-permute-start.8 = (f32[4,128,256]{2,1,0:T(8,128)S(1)}, f32[4,128,256]{2,1,0:T(8,128)S(1)}, u32[]{:S(2)}, u32[]{:S(2)}) collective-permute-start(f32[4,128,256]{2,1,0:T(8,128)S(1)} %collective-permute-done.1.near), channel_id=1, source_target_pairs={{0,1},{1,0},{2,3},{3,2},{4,5},{5,4},{6,7},{7,6},{8,9},{9,8},{10,11... | collective-permute-start | bytes 1572872 | tf_op jit(solution)/shard_map/ppermute | solution.py:250
  16.6 2.8 %collective-permute-done.far_hi = f32[2,128,256]{2,1,0:T(8,128)S(1)} collective-permute-done((f32[2,128,256]{2,1,0:T(8,128)S(1)}, f32[2,128,256]{2,1,0:T(8,128)S(1)}, u32[]{:S(2)}, u32[]{:S(2)}) %collective-permute-start) | collective-permute-done | bytes 262176 | tf_op jit(solution)/shard_map/ppermute | solution.py:250
  19.5 1.9 %collective-permute-start.9 = (f32[4,128,256]{2,1,0:T(8,128)S(1)}, f32[4,128,256]{2,1,0:T(8,128)S(1)}, u32[]{:S(2)}, u32[]{:S(2)}) collective-permute-start(f32[4,128,256]{2,1,0:T(8,128)S(1)} %collective-permute-done.5.two_a), channel_id=1, source_target_pairs={{0,1},{1,0},{2,3},{3,2},{4,5},{5,4},{6,7},{7,6},{8,9},{9,8},{10,11... | collective-permute-start | bytes 1572872 | tf_op jit(solution)/shard_map/ppermute | solution.py:250
  21.4 3.0 %collective-permute-done.2.far_lo = f32[2,128,256]{2,1,0:T(8,128)S(1)} collective-permute-done((f32[2,128,256]{2,1,0:T(8,128)S(1)}, f32[2,128,256]{2,1,0:T(8,128)S(1)}, u32[]{:S(2)}, u32[]{:S(2)}) %collective-permute-start.2) | collective-permute-done | bytes 262176 | tf_op jit(solution)/shard_map/ppermute | solution.py:262
  24.4 0.9 %collective-permute-start.3 = (f32[2,128,256]{2,1,0:T(8,128)S(1)}, f32[2,128,256]{2,1,0:T(8,128)S(1)}, u32[]{:S(2)}, u32[]{:S(2)}) collective-permute-start(f32[2,128,256]{2,1,0:T(8,128)S(1)} %collective-permute-done.far_hi), channel_id=1, source_target_pairs={{0,1},{1,0},{2,3},{3,2},{4,5},{5,4},{6,7},{7,6},{8,9},{9,8},{10,11... | collective-permute-start | bytes 786440 | tf_op jit(solution)/shard_map/ppermute | solution.py:250
  25.3 0.0 collective-permute-done.7.here2
  25.3 0.0 collective-permute-start.4
  25.3 0.0 collective-permute-done.10.two_b2
  25.3 0.0 collective-permute-done.8.near2
  25.4 0.0 collective-permute-done.9.two_a2
  25.4 1.0 %spectral.1.partial = f32[4,4,2,128,128]{4,3,2,1,0:T(8,128)S(1)} custom-call(f32[4,128,256]{2,1,0:T(8,128)S(1)} %get-tuple-element.23.here, f32[4,128,256]{2,1,0:T(8,128)S(1)} %collective-permute-done.1.near, f32[4,128,256]{2,1,0:T(8,128)S(1)} %collective-permute-done.5.two_a, f32[4,128,256]{2,1,0:T(8,128)S(1)} %collective-permute-done.6.two_b, ...), custom_call_target="tpu_custom_call" | custom-call | flops 1 | bytes 1 | tf_op jit(solution)/shard_map/spectral/pallas_call | solution.py:279
  26.4 0.1 collective-permute-done.3.far_hi2
  26.5 0.4 %collective-permute-done.4.far_lo2 = f32[2,128,256]{2,1,0:T(8,128)S(1)} collective-permute-done((f32[2,128,256]{2,1,0:T(8,128)S(1)}, f32[2,128,256]{2,1,0:T(8,128)S(1)}, u32[]{:S(2)}, u32[]{:S(2)}) %collective-permute-start.4) | collective-permute-done | bytes 262176 | tf_op jit(solution)/shard_map/ppermute | solution.py:250
  26.9 0.0 copy-done.1
  26.9 8.0 %denoise.1 = f32[4,128,256]{2,1,0:T(8,128)} custom-call(s32[4,6]{1,0:T(4,128)S(1)} %bitcast.7, s32[4,4,6]{2,1,0:T(4,128)S(1)} %bitcast.6, f32[2,128,256]{2,1,0:T(8,128)S(1)} %collective-permute-done.3.far_hi2, f32[2,128,256]{2,1,0:T(8,128)S(1)} %collective-permute-done.4.far_lo2, bf16[128,32]{1,0:T(8,128)(2,1)S(1)} %dynamic-slice_bitcast_fusion.1.table, ...), custom_call_target="tpu_custom_call" | custom-call | tf_op jit(solution)/shard_map/denoise/pallas_call | solution.py:288
  (3 shorter events, 0.0 us)
Async XLA Ops:
  0.0 14.7 %collective-permute-start.1 = (f32[4,128,256]{2,1,0:T(8,128)}, f32[4,128,256]{2,1,0:T(8,128)S(1)}, u32[]{:S(2)}, u32[]{:S(2)}) collective-permute-start(f32[4,128,256]{2,1,0:T(8,128)} %cube.1), channel_id=1, source_target_pairs={{0,2},{1,3},{2,0},{3,1},{4,6},{5,7},{6,4},{7,5},{8,10},{9,11},{10,... | collective-permute-start | bytes 1572872 | tf_op jit(solution)/shard_map/ppermute | solution.py:250
  0.0 16.0 %collective-permute-start.5 = (f32[4,128,256]{2,1,0:T(8,128)}, f32[4,128,256]{2,1,0:T(8,128)S(1)}, u32[]{:S(2)}, u32[]{:S(2)}) collective-permute-start(f32[4,128,256]{2,1,0:T(8,128)} %cube.1), channel_id=1, source_target_pairs={{0,4},{1,5},{2,6},{3,7},{4,0},{5,1},{6,2},{7,3},{8,12},{9,13},{10,... | collective-permute-start | bytes 1572872 | tf_op jit(solution)/shard_map/ppermute | solution.py:250
  1.5 14.5 %collective-permute-start.6 = (f32[4,128,256]{2,1,0:T(8,128)}, f32[4,128,256]{2,1,0:T(8,128)S(1)}, u32[]{:S(2)}, u32[]{:S(2)}) collective-permute-start(f32[4,128,256]{2,1,0:T(8,128)} %cube.1), channel_id=1, source_target_pairs={{4,8},{5,9},{6,10},{7,11},{8,4},{9,5},{10,6},{11,7},{20,24},{21,25... | collective-permute-start | bytes 1572872 | tf_op jit(solution)/shard_map/ppermute | solution.py:250
  4.8 14.7 %collective-permute-start = (f32[2,128,256]{2,1,0:T(8,128)S(1)}, f32[2,128,256]{2,1,0:T(8,128)S(1)}, u32[]{:S(2)}, u32[]{:S(2)}) collective-permute-start(f32[2,128,256]{2,1,0:T(8,128)S(1)} %slice.6), channel_id=1, source_target_pairs={{2,4},{3,5},{4,2},{5,3},{6,8},{7,9},{8,6},{9,7},{10,12},{11,13},{1... | collective-permute-start | bytes 786440 | tf_op jit(solution)/shard_map/ppermute | solution.py:250
  11.5 13.9 %collective-permute-start.7 = (f32[4,128,256]{2,1,0:T(8,128)}, f32[4,128,256]{2,1,0:T(8,128)S(1)}, u32[]{:S(2)}, u32[]{:S(2)}) collective-permute-start(f32[4,128,256]{2,1,0:T(8,128)} %cube.1), channel_id=1, source_target_pairs={{0,1},{1,0},{2,3},{3,2},{4,5},{5,4},{6,7},{7,6},{8,9},{9,8},{10,11... | collective-permute-start | bytes 1572872 | tf_op jit(solution)/shard_map/ppermute | solution.py:250
  13.3 1.0 %copy-start = (f32[4,128,256]{2,1,0:T(8,128)S(1)}, f32[4,128,256]{2,1,0:T(8,128)}, u32[]{:S(2)}) copy-start(f32[4,128,256]{2,1,0:T(8,128)} %cube.1) | copy-start | bytes 1572868
  14.7 9.7 %collective-permute-start.2 = (f32[2,128,256]{2,1,0:T(8,128)S(1)}, f32[2,128,256]{2,1,0:T(8,128)S(1)}, u32[]{:S(2)}, u32[]{:S(2)}) collective-permute-start(f32[2,128,256]{2,1,0:T(8,128)S(1)} %slice.8), channel_id=1, source_target_pairs={{0,4},{1,5},{4,8},{5,9},{8,12},{9,13},{6,2},{7,3},{10,6},{11,7},{1... | collective-permute-start | bytes 786440 | tf_op jit(solution)/shard_map/ppermute | solution.py:262
  16.0 10.8 %copy-start.1 = (s32[4,6,4]{1,2,0:T(4,128)S(1)}, s32[4,6,4]{1,2,0:T(4,128)}, u32[]{:S(2)}) copy-start(s32[4,6,4]{1,2,0:T(4,128)} %param.7) | copy-start | bytes 1156
  16.1 10.8 %copy-start.2 = (s32[6,4]{0,1:T(4,128)S(1)}, s32[6,4]{0,1:T(4,128)}, u32[]{:S(2)}) copy-start(s32[6,4]{0,1:T(4,128)} %param.6) | copy-start | bytes 292
  16.1 9.3 %collective-permute-start.10 = (f32[4,128,256]{2,1,0:T(8,128)S(1)}, f32[4,128,256]{2,1,0:T(8,128)S(1)}, u32[]{:S(2)}, u32[]{:S(2)}) collective-permute-start(f32[4,128,256]{2,1,0:T(8,128)S(1)} %collective-permute-done.6.two_b), channel_id=1, source_target_pairs={{0,1},{1,0},{2,3},{3,2},{4,5},{5,4},{6,7},{7,6},{8,9},{9,8},{10,11... | collective-permute-start | bytes 1572872 | tf_op jit(solution)/shard_map/ppermute | solution.py:250
  16.3 9.1 %collective-permute-start.8 = (f32[4,128,256]{2,1,0:T(8,128)S(1)}, f32[4,128,256]{2,1,0:T(8,128)S(1)}, u32[]{:S(2)}, u32[]{:S(2)}) collective-permute-start(f32[4,128,256]{2,1,0:T(8,128)S(1)} %collective-permute-done.1.near), channel_id=1, source_target_pairs={{0,1},{1,0},{2,3},{3,2},{4,5},{5,4},{6,7},{7,6},{8,9},{9,8},{10,11... | collective-permute-start | bytes 1572872 | tf_op jit(solution)/shard_map/ppermute | solution.py:250
  19.5 5.9 %collective-permute-start.9 = (f32[4,128,256]{2,1,0:T(8,128)S(1)}, f32[4,128,256]{2,1,0:T(8,128)S(1)}, u32[]{:S(2)}, u32[]{:S(2)}) collective-permute-start(f32[4,128,256]{2,1,0:T(8,128)S(1)} %collective-permute-done.5.two_a), channel_id=1, source_target_pairs={{0,1},{1,0},{2,3},{3,2},{4,5},{5,4},{6,7},{7,6},{8,9},{9,8},{10,11... | collective-permute-start | bytes 1572872 | tf_op jit(solution)/shard_map/ppermute | solution.py:250
  24.4 2.1 %collective-permute-start.3 = (f32[2,128,256]{2,1,0:T(8,128)S(1)}, f32[2,128,256]{2,1,0:T(8,128)S(1)}, u32[]{:S(2)}, u32[]{:S(2)}) collective-permute-start(f32[2,128,256]{2,1,0:T(8,128)S(1)} %collective-permute-done.far_hi), channel_id=1, source_target_pairs={{0,1},{1,0},{2,3},{3,2},{4,5},{5,4},{6,7},{7,6},{8,9},{9,8},{10,11... | collective-permute-start | bytes 786440 | tf_op jit(solution)/shard_map/ppermute | solution.py:250
  25.3 1.5 %collective-permute-start.4 = (f32[2,128,256]{2,1,0:T(8,128)S(1)}, f32[2,128,256]{2,1,0:T(8,128)S(1)}, u32[]{:S(2)}, u32[]{:S(2)}) collective-permute-start(f32[2,128,256]{2,1,0:T(8,128)S(1)} %collective-permute-done.2.far_lo), channel_id=1, source_target_pairs={{0,1},{1,0},{2,3},{3,2},{4,5},{5,4},{6,7},{7,6},{8,9},{9,8},{10,11... | collective-permute-start | bytes 786440 | tf_op jit(solution)/shard_map/ppermute | solution.py:250

commit v6 on v5

--- a/solution.py
+++ b/solution.py
@@ -82,7 +82,13 @@
 
 
 def denoise_kernel(rows, cols, local, mult, noise, far_hi2, far_lo2, table, partial, mats, out, *scratch):
-    detail, a, p, acc, done, out_sem = scratch
+    mult_s, noise_s, detail, a, p, acc, done, code_sem, out_sem = scratch
+    codes = [
+        pltpu.make_async_copy(mult, mult_s, code_sem.at[0]),
+        pltpu.make_async_copy(noise, noise_s, code_sem.at[1]),
+    ]
+    for c in codes:
+        c.start()
     halves = cols // LANES
     groups = rows // 8
     half = local // 2
@@ -104,7 +110,7 @@
 
     def spatial(i, carry):
         def limits(j, s):
-            level = jnp.full((8, LANES), (mult[s, j] * noise[i, s, j]).astype(F32) * (1.0 / 1024.0))
+            level = jnp.full((8, LANES), (mult_s[s, j] * noise_s[i, s, j]).astype(F32) * (1.0 / 1024.0))
             return -level, level
 
         def shrink(v, ends):
@@ -178,6 +184,8 @@
         pltpu.make_async_copy(done.at[i], out.at[i], out_sem.at[i]).start()
         return carry
 
+    for c in codes:
+        c.wait()
     lax.fori_loop(0, local, spatial, 0)
     for i in range(local):
         pltpu.make_async_copy(done.at[i], out.at[i], out_sem.at[i]).wait()
@@ -241,7 +249,6 @@
 def per_device(count, cube, multipliers, noise_code):
     local, rows, cols = cube.shape
     assert local == 4 and count % 8 == 0 and rows % 8 == 0 and cols % LANES == 0
-    smem = pl.BlockSpec(memory_space=pltpu.SMEM)
     hbm = pl.BlockSpec(memory_space=pltpu.HBM)
     vmem = pl.BlockSpec(memory_space=pltpu.VMEM)
     anyspace = pl.BlockSpec(memory_space=pl.ANY)
@@ -287,15 +294,18 @@
     )(*pieces, *passed[:4], early)
     return pl.pallas_call(
         functools.partial(denoise_kernel, rows, cols, local),
-        in_specs=[smem] * 2 + [vmem] * 5,
+        in_specs=[anyspace] * 2 + [vmem] * 5,
         out_specs=hbm,
         out_shape=jax.ShapeDtypeStruct(cube.shape, F32),
         scratch_shapes=[
+            pltpu.SMEM((scales, SCALES_XY + 1), jnp.int32),
+            pltpu.SMEM((local, scales, SCALES_XY + 1), jnp.int32),
             pltpu.VMEM((local, scales) + plane, F32),
             pltpu.VMEM((scales,) + plane, F32),
             pltpu.VMEM((scales, cols // LANES, rows + 2 * EDGE, LANES), F32),
             pltpu.VMEM(plane, F32),
             pltpu.VMEM((local, rows, cols), F32),
+            pltpu.SemaphoreType.DMA((2,)),
             pltpu.SemaphoreType.DMA((local,)),
         ],
         compiler_params=pltpu.CompilerParams(vmem_limit_bytes=11 * 2**20),

time: 35.4 us -> 34.8 us (0.983)
  Pallas kernels: 9.28 us -> 8.64 us
    pallas_call x1, Pallas kernels: 8 us -> 7.36 us  [per_device(): pl.pallas_call(functools.partial(denoise_kernel, rows, cols, local), in_s...]
  transfers between devices with their start and end apart: 11 -> 11, of which waited for: 4 -> 4; matrix products, arithmetic and copies ran while one was open for 7% -> 8% of each run, Pallas kernels for 4% -> 4%
where the time goes in v6:
time: 34.8 us; the launch traced here: 34.2 us
  starting transfers between devices  15.4 us (44%)
  Pallas kernels  8.64 us (25%)
  waiting for transfers between devices  6.4 us (18%)
  local copies, waits for them, and re-layouts  3.66 us (11%)
    ppermute x10, starting transfers between devices, permute(): return lax.ppermute(v, 'chan', pairs(count, distance, phase))  14.1 us
    pallas_call x1, Pallas kernels, per_device(): pl.pallas_call(functools.partial(denoise_kernel, rows, cols, local), in_s...  7.36 us
    ppermute x10, waiting for transfers between devices, permute(): return lax.ppermute(v, 'chan', pairs(count, distance, phase))  3.37 us
    ppermute x1, waiting for transfers between devices, per_device(): far_lo = lax.ppermute(near[:cut], 'chan', relay)  3.03 us
    squeeze x2, local copies, waits for them, and re-layouts, per_device(): lax.dynamic_index_in_dim(t, me, 0, False)  1.61 us
    ppermute x1, starting transfers between devices, per_device(): far_lo = lax.ppermute(near[:cut], 'chan', relay)  1.29 us
    unnamed x6, local copies, waits for them, and re-layouts  1.05 us
    pallas_call x1, Pallas kernels, per_device(): pl.pallas_call(functools.partial(spectral_kernel, rows, cols, local), in_...  0.99 us
  transfers between devices with their start and end apart: 11, of which 4 were waited for; matrix products, arithmetic and copies ran while one was open for 8% of the time, Pallas kernels for 4%

profile of v6, /device:TPU:5, one launch (start us, length us, event | category | flops | bytes accessed | tf_op | source)
XLA Modules:
  0.0 34.2 jit_solution(4041453507673999531)
XLA Ops:
  0.0 0.0 collective-permute-start.1
  0.0 1.5 %collective-permute-start.5 = (f32[4,128,256]{2,1,0:T(8,128)}, f32[4,128,256]{2,1,0:T(8,128)S(1)}, u32[]{:S(2)}, u32[]{:S(2)}) collective-permute-start(f32[4,128,256]{2,1,0:T(8,128)} %cube.1), channel_id=1, source_target_pairs={{0,4},{1,5},{2,6},{3,7},{4,0},{5,1},{6,2},{7,3},{8,12},{9,13},{10,... | collective-permute-start | bytes 1572872 | tf_op jit(solution)/shard_map/ppermute | solution.py:257
  1.5 0.7 %collective-permute-start.6 = (f32[4,128,256]{2,1,0:T(8,128)}, f32[4,128,256]{2,1,0:T(8,128)S(1)}, u32[]{:S(2)}, u32[]{:S(2)}) collective-permute-start(f32[4,128,256]{2,1,0:T(8,128)} %cube.1), channel_id=1, source_target_pairs={{4,8},{5,9},{6,10},{7,11},{8,4},{9,5},{10,6},{11,7},{20,24},{21,25... | collective-permute-start | bytes 1572872 | tf_op jit(solution)/shard_map/ppermute | solution.py:257
  2.2 1.0 %slice.6 = f32[2,128,256]{2,1,0:T(8,128)S(1)} slice(f32[4,128,256]{2,1,0:T(8,128)} %cube.1), slice={[2:4], [0:128], [0:256]} | slice | bytes 524288 | tf_op jit(solution)/shard_map/slice | solution.py:267
  3.2 0.8 %dynamic-slice_bitcast_fusion.1.table = bf16[128,32]{1,0:T(8,128)(2,1)S(1)} fusion(bf16[16,128,32]{2,1,0:T(8,128)(2,1)} %constant.19.clone, s32[]{:T(128)S(6)} %select_n.6), kind=kLoop, calls=%fused_computation.1 | loop fusion | bytes 16388 | tf_op jit(solution)/shard_map/jit(dynamic_index_in_dim)/squeeze | solution.py:266
  4.0 0.8 %dynamic-slice_bitcast_fusion.table = bf16[128,256]{1,0:T(8,128)(2,1)S(1)} fusion(bf16[16,128,256]{2,1,0:T(8,128)(2,1)} %constant.18.clone, s32[]{:T(128)S(6)} %select_n.6), kind=kLoop, calls=%fused_computation | loop fusion | bytes 131076 | tf_op jit(solution)/shard_map/jit(dynamic_index_in_dim)/squeeze | solution.py:266
  4.8 6.7 %collective-permute-start = (f32[2,128,256]{2,1,0:T(8,128)S(1)}, f32[2,128,256]{2,1,0:T(8,128)S(1)}, u32[]{:S(2)}, u32[]{:S(2)}) collective-permute-start(f32[2,128,256]{2,1,0:T(8,128)S(1)} %slice.6), channel_id=1, source_target_pairs={{2,4},{3,5},{4,2},{5,3},{6,8},{7,9},{8,6},{9,7},{10,12},{11,13},{1... | collective-permute-start | bytes 786440 | tf_op jit(solution)/shard_map/ppermute | solution.py:257
  11.5 1.9 %collective-permute-start.7 = (f32[4,128,256]{2,1,0:T(8,128)}, f32[4,128,256]{2,1,0:T(8,128)S(1)}, u32[]{:S(2)}, u32[]{:S(2)}) collective-permute-start(f32[4,128,256]{2,1,0:T(8,128)} %cube.1), channel_id=1, source_target_pairs={{0,1},{1,0},{2,3},{3,2},{4,5},{5,4},{6,7},{7,6},{8,9},{9,8},{10,11... | collective-permute-start | bytes 1572872 | tf_op jit(solution)/shard_map/ppermute | solution.py:257
  13.3 1.0 %copy-done = f32[4,128,256]{2,1,0:T(8,128)S(1)} copy-done((f32[4,128,256]{2,1,0:T(8,128)S(1)}, f32[4,128,256]{2,1,0:T(8,128)}, u32[]{:S(2)}) %copy-start) | copy-done | bytes 524312
  14.4 0.3 setup.1
  14.7 0.0 collective-permute-done.1.near
  14.7 1.3 %collective-permute-start.2 = (f32[2,128,256]{2,1,0:T(8,128)S(1)}, f32[2,128,256]{2,1,0:T(8,128)S(1)}, u32[]{:S(2)}, u32[]{:S(2)}) collective-permute-start(f32[2,128,256]{2,1,0:T(8,128)S(1)} %slice.8), channel_id=1, source_target_pairs={{0,4},{1,5},{4,8},{5,9},{8,12},{9,13},{6,2},{7,3},{10,6},{11,7},{1... | collective-permute-start | bytes 786440 | tf_op jit(solution)/shard_map/ppermute | solution.py:269
  16.0 0.0 collective-permute-done.5.two_a
  16.0 0.0 collective-permute-done.6.two_b
  16.0 0.0 copy-start.1
  16.1 0.0 copy-start.2
  16.1 0.2 collective-permute-start.10
  16.3 0.4 %collective-permute-start.8 = (f32[4,128,256]{2,1,0:T(8,128)S(1)}, f32[4,128,256]{2,1,0:T(8,128)S(1)}, u32[]{:S(2)}, u32[]{:S(2)}) collective-permute-start(f32[4,128,256]{2,1,0:T(8,128)S(1)} %collective-permute-done.1.near), channel_id=1, source_target_pairs={{0,1},{1,0},{2,3},{3,2},{4,5},{5,4},{6,7},{7,6},{8,9},{9,8},{10,11... | collective-permute-start | bytes 1572872 | tf_op jit(solution)/shard_map/ppermute | solution.py:257
  16.6 2.8 %collective-permute-done.far_hi = f32[2,128,256]{2,1,0:T(8,128)S(1)} collective-permute-done((f32[2,128,256]{2,1,0:T(8,128)S(1)}, f32[2,128,256]{2,1,0:T(8,128)S(1)}, u32[]{:S(2)}, u32[]{:S(2)}) %collective-permute-start) | collective-permute-done | bytes 262176 | tf_op jit(solution)/shard_map/ppermute | solution.py:257
  19.5 1.9 %collective-permute-start.9 = (f32[4,128,256]{2,1,0:T(8,128)S(1)}, f32[4,128,256]{2,1,0:T(8,128)S(1)}, u32[]{:S(2)}, u32[]{:S(2)}) collective-permute-start(f32[4,128,256]{2,1,0:T(8,128)S(1)} %collective-permute-done.5.two_a), channel_id=1, source_target_pairs={{0,1},{1,0},{2,3},{3,2},{4,5},{5,4},{6,7},{7,6},{8,9},{9,8},{10,11... | collective-permute-start | bytes 1572872 | tf_op jit(solution)/shard_map/ppermute | solution.py:257
  21.4 3.0 %collective-permute-done.2.far_lo = f32[2,128,256]{2,1,0:T(8,128)S(1)} collective-permute-done((f32[2,128,256]{2,1,0:T(8,128)S(1)}, f32[2,128,256]{2,1,0:T(8,128)S(1)}, u32[]{:S(2)}, u32[]{:S(2)}) %collective-permute-start.2) | collective-permute-done | bytes 262176 | tf_op jit(solution)/shard_map/ppermute | solution.py:269
  24.4 0.9 %collective-permute-start.3 = (f32[2,128,256]{2,1,0:T(8,128)S(1)}, f32[2,128,256]{2,1,0:T(8,128)S(1)}, u32[]{:S(2)}, u32[]{:S(2)}) collective-permute-start(f32[2,128,256]{2,1,0:T(8,128)S(1)} %collective-permute-done.far_hi), channel_id=1, source_target_pairs={{0,1},{1,0},{2,3},{3,2},{4,5},{5,4},{6,7},{7,6},{8,9},{9,8},{10,11... | collective-permute-start | bytes 786440 | tf_op jit(solution)/shard_map/ppermute | solution.py:257
  25.3 0.0 collective-permute-done.7.here2
  25.3 0.0 collective-permute-start.4
  25.3 0.0 collective-permute-done.10.two_b2
  25.3 0.0 collective-permute-done.8.near2
  25.4 0.0 collective-permute-done.9.two_a2
  25.4 1.0 %spectral.1.partial = f32[4,4,2,128,128]{4,3,2,1,0:T(8,128)S(1)} custom-call(f32[4,128,256]{2,1,0:T(8,128)S(1)} %get-tuple-element.23.here, f32[4,128,256]{2,1,0:T(8,128)S(1)} %collective-permute-done.1.near, f32[4,128,256]{2,1,0:T(8,128)S(1)} %collective-permute-done.5.two_a, f32[4,128,256]{2,1,0:T(8,128)S(1)} %collective-permute-done.6.two_b, ...), custom_call_target="tpu_custom_call" | custom-call | flops 1 | bytes 1 | tf_op jit(solution)/shard_map/spectral/pallas_call | solution.py:286
  26.4 0.1 collective-permute-done.3.far_hi2
  26.5 0.4 %collective-permute-done.4.far_lo2 = f32[2,128,256]{2,1,0:T(8,128)S(1)} collective-permute-done((f32[2,128,256]{2,1,0:T(8,128)S(1)}, f32[2,128,256]{2,1,0:T(8,128)S(1)}, u32[]{:S(2)}, u32[]{:S(2)}) %collective-permute-start.4) | collective-permute-done | bytes 262176 | tf_op jit(solution)/shard_map/ppermute | solution.py:257
  26.9 0.0 copy-done.1
  26.9 7.4 %denoise.1 = f32[4,128,256]{2,1,0:T(8,128)} custom-call(s32[4,6]{1,0:T(4,128)S(1)} %bitcast.7, s32[4,4,6]{2,1,0:T(4,128)S(1)} %bitcast.6, f32[2,128,256]{2,1,0:T(8,128)S(1)} %collective-permute-done.3.far_hi2, f32[2,128,256]{2,1,0:T(8,128)S(1)} %collective-permute-done.4.far_lo2, bf16[128,32]{1,0:T(8,128)(2,1)S(1)} %dynamic-slice_bitcast_fusion.1.table, ...), custom_call_target="tpu_custom_call" | custom-call | tf_op jit(solution)/shard_map/denoise/pallas_call | solution.py:295
  (3 shorter events, 0.0 us)
Async XLA Ops:
  0.0 14.7 %collective-permute-start.1 = (f32[4,128,256]{2,1,0:T(8,128)}, f32[4,128,256]{2,1,0:T(8,128)S(1)}, u32[]{:S(2)}, u32[]{:S(2)}) collective-permute-start(f32[4,128,256]{2,1,0:T(8,128)} %cube.1), channel_id=1, source_target_pairs={{0,2},{1,3},{2,0},{3,1},{4,6},{5,7},{6,4},{7,5},{8,10},{9,11},{10,... | collective-permute-start | bytes 1572872 | tf_op jit(solution)/shard_map/ppermute | solution.py:257
  0.0 16.0 %collective-permute-start.5 = (f32[4,128,256]{2,1,0:T(8,128)}, f32[4,128,256]{2,1,0:T(8,128)S(1)}, u32[]{:S(2)}, u32[]{:S(2)}) collective-permute-start(f32[4,128,256]{2,1,0:T(8,128)} %cube.1), channel_id=1, source_target_pairs={{0,4},{1,5},{2,6},{3,7},{4,0},{5,1},{6,2},{7,3},{8,12},{9,13},{10,... | collective-permute-start | bytes 1572872 | tf_op jit(solution)/shard_map/ppermute | solution.py:257
  1.5 14.5 %collective-permute-start.6 = (f32[4,128,256]{2,1,0:T(8,128)}, f32[4,128,256]{2,1,0:T(8,128)S(1)}, u32[]{:S(2)}, u32[]{:S(2)}) collective-permute-start(f32[4,128,256]{2,1,0:T(8,128)} %cube.1), channel_id=1, source_target_pairs={{4,8},{5,9},{6,10},{7,11},{8,4},{9,5},{10,6},{11,7},{20,24},{21,25... | collective-permute-start | bytes 1572872 | tf_op jit(solution)/shard_map/ppermute | solution.py:257
  4.8 14.7 %collective-permute-start = (f32[2,128,256]{2,1,0:T(8,128)S(1)}, f32[2,128,256]{2,1,0:T(8,128)S(1)}, u32[]{:S(2)}, u32[]{:S(2)}) collective-permute-start(f32[2,128,256]{2,1,0:T(8,128)S(1)} %slice.6), channel_id=1, source_target_pairs={{2,4},{3,5},{4,2},{5,3},{6,8},{7,9},{8,6},{9,7},{10,12},{11,13},{1... | collective-permute-start | bytes 786440 | tf_op jit(solution)/shard_map/ppermute | solution.py:257
  11.5 13.9 %collective-permute-start.7 = (f32[4,128,256]{2,1,0:T(8,128)}, f32[4,128,256]{2,1,0:T(8,128)S(1)}, u32[]{:S(2)}, u32[]{:S(2)}) collective-permute-start(f32[4,128,256]{2,1,0:T(8,128)} %cube.1), channel_id=1, source_target_pairs={{0,1},{1,0},{2,3},{3,2},{4,5},{5,4},{6,7},{7,6},{8,9},{9,8},{10,11... | collective-permute-start | bytes 1572872 | tf_op jit(solution)/shard_map/ppermute | solution.py:257
  13.3 1.0 %copy-start = (f32[4,128,256]{2,1,0:T(8,128)S(1)}, f32[4,128,256]{2,1,0:T(8,128)}, u32[]{:S(2)}) copy-start(f32[4,128,256]{2,1,0:T(8,128)} %cube.1) | copy-start | bytes 1572868
  14.7 9.7 %collective-permute-start.2 = (f32[2,128,256]{2,1,0:T(8,128)S(1)}, f32[2,128,256]{2,1,0:T(8,128)S(1)}, u32[]{:S(2)}, u32[]{:S(2)}) collective-permute-start(f32[2,128,256]{2,1,0:T(8,128)S(1)} %slice.8), channel_id=1, source_target_pairs={{0,4},{1,5},{4,8},{5,9},{8,12},{9,13},{6,2},{7,3},{10,6},{11,7},{1... | collective-permute-start | bytes 786440 | tf_op jit(solution)/shard_map/ppermute | solution.py:269
  16.0 10.8 %copy-start.1 = (s32[4,6,4]{1,2,0:T(4,128)S(1)}, s32[4,6,4]{1,2,0:T(4,128)}, u32[]{:S(2)}) copy-start(s32[4,6,4]{1,2,0:T(4,128)} %param.7) | copy-start | bytes 1156
  16.1 10.8 %copy-start.2 = (s32[6,4]{0,1:T(4,128)S(1)}, s32[6,4]{0,1:T(4,128)}, u32[]{:S(2)}) copy-start(s32[6,4]{0,1:T(4,128)} %param.6) | copy-start | bytes 292
  16.1 9.3 %collective-permute-start.10 = (f32[4,128,256]{2,1,0:T(8,128)S(1)}, f32[4,128,256]{2,1,0:T(8,128)S(1)}, u32[]{:S(2)}, u32[]{:S(2)}) collective-permute-start(f32[4,128,256]{2,1,0:T(8,128)S(1)} %collective-permute-done.6.two_b), channel_id=1, source_target_pairs={{0,1},{1,0},{2,3},{3,2},{4,5},{5,4},{6,7},{7,6},{8,9},{9,8},{10,11... | collective-permute-start | bytes 1572872 | tf_op jit(solution)/shard_map/ppermute | solution.py:257
  16.3 9.1 %collective-permute-start.8 = (f32[4,128,256]{2,1,0:T(8,128)S(1)}, f32[4,128,256]{2,1,0:T(8,128)S(1)}, u32[]{:S(2)}, u32[]{:S(2)}) collective-permute-start(f32[4,128,256]{2,1,0:T(8,128)S(1)} %collective-permute-done.1.near), channel_id=1, source_target_pairs={{0,1},{1,0},{2,3},{3,2},{4,5},{5,4},{6,7},{7,6},{8,9},{9,8},{10,11... | collective-permute-start | bytes 1572872 | tf_op jit(solution)/shard_map/ppermute | solution.py:257
  19.5 5.9 %collective-permute-start.9 = (f32[4,128,256]{2,1,0:T(8,128)S(1)}, f32[4,128,256]{2,1,0:T(8,128)S(1)}, u32[]{:S(2)}, u32[]{:S(2)}) collective-permute-start(f32[4,128,256]{2,1,0:T(8,128)S(1)} %collective-permute-done.5.two_a), channel_id=1, source_target_pairs={{0,1},{1,0},{2,3},{3,2},{4,5},{5,4},{6,7},{7,6},{8,9},{9,8},{10,11... | collective-permute-start | bytes 1572872 | tf_op jit(solution)/shard_map/ppermute | solution.py:257
  24.4 2.1 %collective-permute-start.3 = (f32[2,128,256]{2,1,0:T(8,128)S(1)}, f32[2,128,256]{2,1,0:T(8,128)S(1)}, u32[]{:S(2)}, u32[]{:S(2)}) collective-permute-start(f32[2,128,256]{2,1,0:T(8,128)S(1)} %collective-permute-done.far_hi), channel_id=1, source_target_pairs={{0,1},{1,0},{2,3},{3,2},{4,5},{5,4},{6,7},{7,6},{8,9},{9,8},{10,11... | collective-permute-start | bytes 786440 | tf_op jit(solution)/shard_map/ppermute | solution.py:257
  25.3 1.5 %collective-permute-start.4 = (f32[2,128,256]{2,1,0:T(8,128)S(1)}, f32[2,128,256]{2,1,0:T(8,128)S(1)}, u32[]{:S(2)}, u32[]{:S(2)}) collective-permute-start(f32[2,128,256]{2,1,0:T(8,128)S(1)} %collective-permute-done.2.far_lo), channel_id=1, source_target_pairs={{0,1},{1,0},{2,3},{3,2},{4,5},{5,4},{6,7},{7,6},{8,9},{9,8},{10,11... | collective-permute-start | bytes 786440 | tf_op jit(solution)/shard_map/ppermute | solution.py:257

commit v7 on v5

v7 whole, which is shorter than its diff:
```python
import functools

import jax
import jax.numpy as jnp
import numpy as np
from jax import lax
from jax.experimental import pallas as pl
from jax.experimental.pallas import tpu as pltpu
from jax.sharding import PartitionSpec as P

SCALES_XY = 5
SCALES_NU = 3
TAPS = (1, 4, 6, 4, 1)
REACH = 14
LANES = 128
EDGE = 8
F32 = jnp.float32
BF16 = jnp.bfloat16


def pairs(count, distance, phase):
    out = []
    for i in range(count):
        j = i + distance if (i // distance) % 2 == phase else i - distance
        if 0 <= j < count:
            out.append((i, j))
    return out


def plus(*terms):
    terms = [t for t in terms if t is not None]
    out = terms[0]
    for t in terms[1:]:
        out = out + t
    return out


def pick(values, k):
    return values[k] if 0 <= k < len(values) else None


def split(x):
    hi = x.astype(BF16)
    return hi, (x - hi.astype(F32)).astype(BF16)


def smooths(local, count, table, planes):
    hi, lo = split(jnp.concatenate(planes, 0))
    y = jnp.dot(table[...], hi, preferred_element_type=F32)
    z = jnp.dot(table[: 8 * count * local], lo, preferred_element_type=F32)
    out = []
    for s in range(count):
        row = []
        for k in range(local):
            at = 8 * (s * local + k)
            v = y[at : at + 8] + z[at : at + 8]
            if s == SCALES_NU - 1:
                v = v + y[at + 8 * local : at + 8 * local + 8]
            row.append(v)
        out.append(row)
    return out


def spectral_kernel(rows, cols, local, here, near, two_a, two_b, far, relayed, here2, near2, two_a2, two_b2, table, detail):
    me = lax.axis_index("chan").astype(jnp.int32)
    half = local // 2
    edge_a = half * ((me // 4) % 2)
    edge_b = half - edge_a
    for g in range(rows // 8):
        r = pl.ds(8 * g, 8)
        planes = [here[k, r] for k in range(local)] + [near[k, r] for k in range(local)]
        planes += [two_a[edge_a + k, r] for k in range(half)] + [two_b[edge_b + k, r] for k in range(half)]
        planes += [far[k, r] for k in range(half)] + [relayed[k, r] for k in range(half)]
        for ref in (here2, near2, two_a2, two_b2):
            planes += [ref[k, r] for k in range(local)]
        e = [planes[:local]] + smooths(local, SCALES_NU, table, planes)
        for k in range(local):
            for s in range(SCALES_NU + 1):
                d = e[s][k] - e[s + 1][k] if s < SCALES_NU else e[s][k]
                for h in range(cols // LANES):
                    detail[k, s, h, r] = d[:, h * LANES : (h + 1) * LANES]


def fetch_codes(mult, noise, mult_s, noise_s, sem):
    copies = [pltpu.make_async_copy(mult, mult_s, sem.at[0]), pltpu.make_async_copy(noise, noise_s, sem.at[1])]
    for c in copies:
        c.start()
    return copies


def limits(mult_s, noise_s, i, j, s):
    level = jnp.full((8, LANES), (mult_s[s, j] * noise_s[i, s, j]).astype(F32) * (1.0 / 1024.0))
    return -level, level


def shrink(v, ends):
    return v - jnp.minimum(jnp.maximum(v, ends[0]), ends[1])


def clear_edges(rows, p):
    for n in range(p.shape[0]):
        for h in range(p.shape[1]):
            p[n, h, :EDGE] = jnp.zeros((EDGE, LANES), F32)
            p[n, h, EDGE + rows :] = jnp.zeros((EDGE, LANES), F32)


def smooth_rows(groups, d, p):
    def load(o):
        return [p[pl.ds(EDGE + 8 * k + o, 8)] for k in range(groups)]

    x = load(0)
    if d >= 8:
        q = d // 8
        cur = x
        for _ in range(4):
            cur = [plus(pick(cur, k), pick(cur, k - q)) for k in range(len(cur) + q)]
        return cur[2 * q : 2 * q + groups]
    if d == 4:
        u = [p[pl.ds(EDGE + 8 * k - 4, 8)] for k in range(groups + 1)]
        near = [u[k] + u[k + 1] for k in range(groups)]
        far = [plus(pick(x, k - 1), pick(x, k + 1)) for k in range(groups)]
    elif d == 2:
        u = [p[pl.ds(EDGE + 8 * k - 4, 8)] for k in range(groups + 1)]
        near = [m + n for m, n in zip(load(-2), load(2))]
        far = [u[k] + u[k + 1] for k in range(groups)]
    else:
        near = [m + n for m, n in zip(load(-1), load(1))]
        far = [m + n for m, n in zip(load(-2), load(2))]
    return [6.0 * x[k] + 4.0 * near[k] + far[k] for k in range(groups)]


def spatial(rows, cols, mats, a, p, sources, ends_of, sums, add):
    halves = cols // LANES
    groups = rows // 8
    for j in range(SCALES_XY):
        ends = [ends_of(n, j) for n in range(len(sources))]
        source = [src if j == 0 else a.at[n] for n, src in enumerate(sources)]
        for n, src in enumerate(source):
            hi, lo = split(jnp.concatenate([src[h] for h in range(halves)], 1))
            y = jnp.dot(jnp.concatenate([hi, lo], 0), mats[j], preferred_element_type=F32)
            y = y[:rows] + y[rows:]
            for h in range(halves):
                p[n, h, pl.ds(EDGE, rows)] = y[:, h * LANES : (h + 1) * LANES]
        for t, members in enumerate(sums):
            for h in range(halves):
                total = [None] * groups
                for n in members:
                    y = smooth_rows(groups, 2**j, p.at[n, h])
                    for k in range(groups):
                        r = pl.ds(8 * k, 8)
                        v = shrink(source[n][h, r] - y[k], ends[n])
                        a[n, h, r] = y[k]
                        total[k] = plus(total[k], v)
                for k in range(groups):
                    add(j, t, h, pl.ds(8 * k, 8), total[k])


def first_kernel(rows, cols, local, mult, noise, here, here2, table, mats, out, mult_s, noise_s, detail, a, p, sem):
    codes = fetch_codes(mult, noise, mult_s, noise_s, sem)
    clear_edges(rows, p)
    half = local // 2
    begin = half * (1 - lax.axis_index("chan").astype(jnp.int32) % 2)
    for g in range(rows // 8):
        r = pl.ds(8 * g, 8)
        e = smooths(half, 1, table, [ref[k, r] for ref in (here, here2) for k in range(local)])[0]
        for k in range(half):
            d = here[begin + k, r] - e[k]
            for h in range(cols // LANES):
                detail[k, h, r] = d[:, h * LANES : (h + 1) * LANES]
    for c in codes:
        c.wait()

    def add(j, t, h, r, v):
        if j == 0:
            out[t, h, r] = v
        else:
            out[t, h, r] += v

    def ends_of(n, j):
        return limits(mult_s, noise_s, begin + n, j, 0)

    spatial(rows, cols, mats, a, p, [detail.at[k] for k in range(half)], ends_of, [[k] for k in range(half)], add)
    for k in range(half):
        ends = ends_of(k, SCALES_XY)
        for h in range(cols // LANES):
            for g in range(rows // 8):
                r = pl.ds(8 * g, 8)
                out[k, h, r] += shrink(a[k, h, r], ends)


def denoise_kernel(rows, cols, local, mult, noise, far2, relayed2, table, partial, begun, mats, out, *scratch):
    mult_s, noise_s, detail, a, p, acc, done, sem, out_sem = scratch
    halves = cols // LANES
    half = local // 2
    core = lax.axis_index("chan").astype(jnp.int32) % 2
    codes = fetch_codes(mult, noise, mult_s, noise_s, sem)
    clear_edges(rows, p)
    for g in range(rows // 8):
        r = pl.ds(8 * g, 8)
        e = smooths(local, SCALES_NU, table, [ref[k, r] for ref in (far2, relayed2) for k in range(ref.shape[0])])
        for k in range(local):
            for s in range(SCALES_NU + 1):
                if s == 0:
                    d = -e[0][k]
                else:
                    d = e[s - 1][k] - e[s][k] if s < SCALES_NU else e[s - 1][k]
                for h in range(halves):
                    detail[k, s, h, r] = partial[k, s, h, r] + d[:, h * LANES : (h + 1) * LANES]
    for c in codes:
        c.wait()

    copies = []
    for begin, scales in ((half * core, range(SCALES_NU + 1)), (half * (1 - core), range(1, SCALES_NU + 1))):
        streams = [(k, s) for k in range(half) for s in scales]
        sums = [[n for n, (k, _) in enumerate(streams) if k == t] for t in range(half)]

        def add(j, t, h, r, v, partly=scales[0] > 0):
            if j > 0:
                acc[t, h, r] += v
            else:
                acc[t, h, r] = v + begun[t, h, r] if partly else v

        def ends_of(n, j, begin=begin, streams=streams):
            k, s = streams[n]
            return limits(mult_s, noise_s, begin + k, j, s)

        spatial(rows, cols, mats, a, p, [detail.at[begin + k, s] for k, s in streams], ends_of, sums, add)
        for t, members in enumerate(sums):
            ends = [ends_of(n, SCALES_XY) for n in members[:-1]]
            for h in range(halves):
                for g in range(rows // 8):
                    r = pl.ds(8 * g, 8)
                    total = acc[t, h, r] + a[members[-1], h, r]
                    for n, lim in zip(members, ends):
                        total = total + shrink(a[n, h, r], lim)
                    done[begin + t, r, h * LANES : (h + 1) * LANES] = total
            copy = pltpu.make_async_copy(done.at[begin + t], out.at[begin + t], out_sem.at[len(copies)])
            copy.start()
            copies.append(copy)
    for copy in copies:
        copy.wait()


def places(i, local):
    beside = 1 - 2 * (i % 2)
    up2 = 2 - 4 * (i // 2 % 2)
    up4 = 4 - 8 * (i // 4 % 2)
    half = local // 2

    def block(at):
        return [at * local + o for o in range(local)]

    def edge(at):
        return block(at)[half:] if at < 0 else block(at)[:half]

    def passed(held):
        return [c + beside * local for c in held]

    early = block(0) + block(up2) + edge(up4) + edge(-up4) + block(-up2)[half:] + block(-up2)[:half]
    for at in (0, up2, up4, -up4):
        early += passed(block(at))
    last = passed(block(-up2)[half:] + block(-up2)[:half])
    return early, last, block(0) + passed(block(0))


def spectral_tables(count, local):
    n = count * local
    whole = np.eye(n)
    parts = []
    for s in range(SCALES_NU):
        whole = sum(w / 16.0 * np.eye(n, k=(k - 2) * 2**s) for k, w in enumerate(TAPS)) @ whole
        parts.append(whole)
    hi = parts[-1].astype(BF16).astype(np.float64)
    parts[-1:] = [hi, parts[-1] - hi]
    tables = [], [], []
    for i in range(count):
        own = np.concatenate([p[i * local : (i + 1) * local] for p in parts])
        both = places(i, local)
        seen = [at for at in both[0] + both[1] if -REACH <= at < local + REACH]
        assert sorted(seen) == list(range(-REACH, local + REACH))
        for table, held in zip(tables, both):
            begin = local // 2 * (1 - i % 2) if table is tables[2] else 0
            taps = np.zeros((local // 2 if table is tables[2] else own.shape[0], len(held)))
            for c, at in enumerate(held):
                if 0 <= i * local + at < n:
                    taps[:, c] = own[begin : begin + taps.shape[0], i * local + at]
            table.append(np.kron(taps, np.eye(8)))
    return [jnp.asarray(np.stack(t), BF16) for t in tables]


def setup_kernel(cols, cube, here, mats, sem):
    fetch = pltpu.make_async_copy(cube, here, sem)
    fetch.start()
    row = lax.broadcasted_iota(jnp.int32, (cols, cols), 0)
    offset = lax.broadcasted_iota(jnp.int32, (cols, cols), 1) - row
    for j in range(SCALES_XY):
        m = jnp.zeros((cols, cols), F32)
        for k, w in enumerate(TAPS):
            m = jnp.where(offset == (k - 2) * 2**j, w / 256.0, m)
        mats[j] = m.astype(BF16)
    fetch.wait()


def per_device(count, cube, multipliers, noise_code):
    local, rows, cols = cube.shape
    assert local == 4 and count % 8 == 0 and rows % 8 == 0 and cols % LANES == 0
    hbm = pl.BlockSpec(memory_space=pltpu.HBM)
    vmem = pl.BlockSpec(memory_space=pltpu.VMEM)
    anyspace = pl.BlockSpec(memory_space=pl.ANY)

    def permute(v, distance, phase):
        return lax.ppermute(v, "chan", pairs(count, distance, phase))

    relay = [(i, i + 4) for i in range(count - 4) if (i // 2) % 2 == 0]
    relay += [(i, i - 4) for i in range(4, count) if (i // 2) % 2 == 1]
    half = local // 2
    me = lax.axis_index("chan")
    near = permute(cube, 2, 0)
    two_a = permute(cube, 4, 0)
    two_b = permute(cube, 4, 1)
    early, late, one = [lax.dynamic_index_in_dim(t, me, 0, False) for t in spectral_tables(count, local)]
    upper, early, late, one = lax.optimization_barrier((cube[half:], early, late, one))
    far = permute(upper, 2, 1)
    here, mats = pl.pallas_call(
        functools.partial(setup_kernel, cols),
        in_specs=[anyspace],
        out_specs=[vmem] * 2,
        out_shape=[jax.ShapeDtypeStruct(cube.shape, F32), jax.ShapeDtypeStruct((SCALES_XY, cols, cols), BF16)],
        scratch_shapes=[pltpu.SemaphoreType.DMA],
        compiler_params=pltpu.CompilerParams(vmem_limit_bytes=4 * 2**20),
        cost_estimate=pl.CostEstimate(flops=10**7, bytes_accessed=2 * 10**6, transcendentals=0),
        name="setup",
    )(cube)
    plane = (cols // LANES, rows, LANES)
    scales = SCALES_NU + 1
    codes = (multipliers.T, noise_code.transpose(0, 2, 1))
    code_scratch = [
        pltpu.SMEM((scales, SCALES_XY + 1), jnp.int32),
        pltpu.SMEM((local, scales, SCALES_XY + 1), jnp.int32),
    ]

    def planes(n):
        return [
            pltpu.VMEM((n,) + plane, F32),
            pltpu.VMEM((n, cols // LANES, rows + 2 * EDGE, LANES), F32),
        ]

    here2 = permute(cube, 1, 0)
    begun = pl.pallas_call(
        functools.partial(first_kernel, rows, cols, local),
        in_specs=[anyspace] * 2 + [vmem] * 4,
        out_specs=vmem,
        out_shape=jax.ShapeDtypeStruct((half,) + plane, F32),
        scratch_shapes=code_scratch
        + [pltpu.VMEM((half,) + plane, F32)]
        + planes(half)
        + [pltpu.SemaphoreType.DMA((2,))],
        compiler_params=pltpu.CompilerParams(vmem_limit_bytes=4 * 2**20),
        cost_estimate=pl.CostEstimate(flops=10**7, bytes_accessed=2 * 10**6, transcendentals=0),
        name="first",
    )(*codes, here, here2, one, mats)
    relayed = lax.ppermute(near[:half], "chan", relay)
    two_a, two_b, near, here, mats = lax.optimization_barrier((two_a, two_b, near, here, mats))
    far, relayed, begun = lax.optimization_barrier((far, relayed, begun))
    near2, two_a2, two_b2, far2, relayed2 = [permute(v, 1, 0) for v in (near, two_a, two_b, far, relayed)]
    partial = pl.pallas_call(
        functools.partial(spectral_kernel, rows, cols, local),
        in_specs=[vmem] * 11,
        out_specs=vmem,
        out_shape=jax.ShapeDtypeStruct((local, scales) + plane, F32),
        compiler_params=pltpu.CompilerParams(vmem_limit_bytes=6 * 2**20),
        cost_estimate=pl.CostEstimate(flops=1, bytes_accessed=1, transcendentals=0),
        name="spectral",
    )(here, near, two_a, two_b, far, relayed, here2, near2, two_a2, two_b2, early)
    return pl.pallas_call(
        functools.partial(denoise_kernel, rows, cols, local),
        in_specs=[anyspace] * 2 + [vmem] * 6,
        out_specs=hbm,
        out_shape=jax.ShapeDtypeStruct(cube.shape, F32),
        scratch_shapes=code_scratch
        + [pltpu.VMEM((local, scales) + plane, F32)]
        + planes(half * scales)
        + [
            pltpu.VMEM((half,) + plane, F32),
            pltpu.VMEM((local, rows, cols), F32),
            pltpu.SemaphoreType.DMA((2,)),
            pltpu.SemaphoreType.DMA((local,)),
        ],
        compiler_params=pltpu.CompilerParams(vmem_limit_bytes=11 * 2**20),
        name="denoise",
    )(*codes, far2, relayed2, late, partial, begun, mats)


def solution(mesh):
    placed = (P(("slab", "chan"), None, None), P(), P(("slab", "chan"), None, None))
    return jax.shard_map(
        functools.partial(per_device, mesh.shape["chan"]),
        mesh=mesh,
        in_specs=placed,
        out_specs=P(("slab", "chan"), None, None),
        check_vma=False,
    )
```

time: 35.4 us -> 34.8 us (0.983)
  local copies, waits for them, and re-layouts: 3.66 us -> 5.71 us
  waiting for transfers between devices: 6.4 us -> 4.48 us
  starting transfers between devices: 15.4 us -> 13.7 us
  Pallas kernels: 9.28 us -> 10.3 us
    ppermute x10, waiting for transfers between devices: 3.37 us -> 0.53 us  [permute(): return lax.ppermute(v, 'chan', pairs(count, distance, phase))]
    pallas_call x0 -> x1, Pallas kernels: none -> 1.92 us  [per_device(): pl.pallas_call(functools.partial(first_kernel, rows, cols, local), in_spe...]
    ppermute x10, starting transfers between devices: 14.1 us -> 12.4 us  [permute(): return lax.ppermute(v, 'chan', pairs(count, distance, phase))]
    unnamed x6 -> x10, local copies, waits for them, and re-layouts: 1.05 us -> 2.43 us
    pallas_call x1, Pallas kernels: 8 us -> 7.06 us  [per_device(): pl.pallas_call(functools.partial(denoise_kernel, rows, cols, local), in_s...]
    ppermute x1, waiting for transfers between devices: 3.03 us -> 3.95 us  [per_device(): relayed = lax.ppermute(near[:half], 'chan', relay)]
    squeeze x2 -> x3, local copies, waits for them, and re-layouts: 1.61 us -> 2.3 us  [per_device(): lax.dynamic_index_in_dim(t, me, 0, False)]
  transfers between devices with their start and end apart: 11 -> 11, of which waited for: 4 -> 3; matrix products, arithmetic and copies ran while one was open for 7% -> 10% of each run, Pallas kernels for 4% -> 9%
where the time goes in v7:
time: 34.8 us; the launch traced here: 34.3 us
  starting transfers between devices  13.7 us (39%)
  Pallas kernels  10.3 us (30%)
  local copies, waits for them, and re-layouts  5.71 us (16%)
  waiting for transfers between devices  4.48 us (13%)
    ppermute x10, starting transfers between devices, permute(): return lax.ppermute(v, 'chan', pairs(count, distance, phase))  12.4 us
    pallas_call x1, Pallas kernels, per_device(): pl.pallas_call(functools.partial(denoise_kernel, rows, cols, local), in_s...  7.06 us
    ppermute x1, waiting for transfers between devices, per_device(): relayed = lax.ppermute(near[:half], 'chan', relay)  3.95 us
    unnamed x10, local copies, waits for them, and re-layouts  2.43 us
    squeeze x3, local copies, waits for them, and re-layouts, per_device(): lax.dynamic_index_in_dim(t, me, 0, False)  2.3 us
    pallas_call x1, Pallas kernels, per_device(): pl.pallas_call(functools.partial(first_kernel, rows, cols, local), in_spe...  1.92 us
    ppermute x1, starting transfers between devices, per_device(): relayed = lax.ppermute(near[:half], 'chan', relay)  1.29 us
    pallas_call x1, Pallas kernels, per_device(): pl.pallas_call(functools.partial(spectral_kernel, rows, cols, local), in_...  1 us
  transfers between devices with their start and end apart: 11, of which 3 were waited for; matrix products, arithmetic and copies ran while one was open for 10% of the time, Pallas kernels for 9%

profile of v7, /device:TPU:5, one launch (start us, length us, event | category | flops | bytes accessed | tf_op | source)
XLA Modules:
  0.0 34.3 jit_solution(6569078721764211689)
XLA Ops:
  0.0 0.0 collective-permute-start.1
  0.0 1.5 %collective-permute-start.6 = (f32[4,128,256]{2,1,0:T(8,128)}, f32[4,128,256]{2,1,0:T(8,128)S(1)}, u32[]{:S(2)}, u32[]{:S(2)}) collective-permute-start(f32[4,128,256]{2,1,0:T(8,128)} %cube.1), channel_id=1, source_target_pairs={{0,4},{1,5},{2,6},{3,7},{4,0},{5,1},{6,2},{7,3},{8,12},{9,13},{10,... | collective-permute-start | bytes 1572872 | tf_op jit(solution)/shard_map/ppermute | solution.py:312
  1.5 0.7 %collective-permute-start.7 = (f32[4,128,256]{2,1,0:T(8,128)}, f32[4,128,256]{2,1,0:T(8,128)S(1)}, u32[]{:S(2)}, u32[]{:S(2)}) collective-permute-start(f32[4,128,256]{2,1,0:T(8,128)} %cube.1), channel_id=1, source_target_pairs={{4,8},{5,9},{6,10},{7,11},{8,4},{9,5},{10,6},{11,7},{20,24},{21,25... | collective-permute-start | bytes 1572872 | tf_op jit(solution)/shard_map/ppermute | solution.py:312
  2.2 1.3 %collective-permute-start.3 = (f32[4,128,256]{2,1,0:T(8,128)}, f32[4,128,256]{2,1,0:T(8,128)S(1)}, u32[]{:S(2)}, u32[]{:S(2)}) collective-permute-start(f32[4,128,256]{2,1,0:T(8,128)} %cube.1), channel_id=1, source_target_pairs={{0,1},{1,0},{2,3},{3,2},{4,5},{5,4},{6,7},{7,6},{8,9},{9,8},{10,11... | collective-permute-start | bytes 1572872 | tf_op jit(solution)/shard_map/ppermute | solution.py:312
  3.5 1.0 %slice.6 = f32[2,128,256]{2,1,0:T(8,128)S(1)} slice(f32[4,128,256]{2,1,0:T(8,128)} %cube.1), slice={[2:4], [0:128], [0:256]} | slice | bytes 524288 | tf_op jit(solution)/shard_map/slice | solution.py:322
  4.5 0.7 %dynamic-slice_bitcast_fusion.2.table = bf16[16,64]{1,0:T(8,128)(2,1)S(1)} fusion(bf16[16,16,64]{2,1,0:T(8,128)(2,1)} %constant.26.clone, s32[]{:T(128)S(6)} %select_n.8), kind=kLoop, calls=%fused_computation.2 | loop fusion | bytes 4100 | tf_op jit(solution)/shard_map/jit(dynamic_index_in_dim)/squeeze | solution.py:321
  5.2 0.8 %dynamic-slice_bitcast_fusion.1.table = bf16[128,32]{1,0:T(8,128)(2,1)S(1)} fusion(bf16[16,128,32]{2,1,0:T(8,128)(2,1)} %constant.25.clone, s32[]{:T(128)S(6)} %select_n.8), kind=kLoop, calls=%fused_computation.1 | loop fusion | bytes 16388 | tf_op jit(solution)/shard_map/jit(dynamic_index_in_dim)/squeeze | solution.py:321
  5.9 0.8 %dynamic-slice_bitcast_fusion.table = bf16[128,256]{1,0:T(8,128)(2,1)S(1)} fusion(bf16[16,128,256]{2,1,0:T(8,128)(2,1)} %constant.24.clone, s32[]{:T(128)S(6)} %select_n.8), kind=kLoop, calls=%fused_computation | loop fusion | bytes 131076 | tf_op jit(solution)/shard_map/jit(dynamic_index_in_dim)/squeeze | solution.py:321
  6.8 6.9 %collective-permute-start = (f32[2,128,256]{2,1,0:T(8,128)S(1)}, f32[2,128,256]{2,1,0:T(8,128)S(1)}, u32[]{:S(2)}, u32[]{:S(2)}) collective-permute-start(f32[2,128,256]{2,1,0:T(8,128)S(1)} %slice.6), channel_id=1, source_target_pairs={{2,4},{3,5},{4,2},{5,3},{6,8},{7,9},{8,6},{9,7},{10,12},{11,13},{1... | collective-permute-start | bytes 786440 | tf_op jit(solution)/shard_map/ppermute | solution.py:312
  13.7 0.0 copy-start
  13.8 1.0 %copy-done = f32[4,128,256]{2,1,0:T(8,128)S(1)} copy-done((f32[4,128,256]{2,1,0:T(8,128)S(1)}, f32[4,128,256]{2,1,0:T(8,128)}, u32[]{:S(2)}) %copy-start) | copy-done | bytes 524312
  14.8 0.3 setup.1
  15.1 1.3 %collective-permute-start.2 = (f32[2,128,256]{2,1,0:T(8,128)S(1)}, f32[2,128,256]{2,1,0:T(8,128)S(1)}, u32[]{:S(2)}, u32[]{:S(2)}) collective-permute-start(f32[2,128,256]{2,1,0:T(8,128)S(1)} %slice.8), channel_id=1, source_target_pairs={{0,4},{1,5},{4,8},{5,9},{8,12},{9,13},{6,2},{7,3},{10,6},{11,7},{1... | collective-permute-start | bytes 786440 | tf_op jit(solution)/shard_map/ppermute | solution.py:362
  16.4 0.0 collective-permute-done.6.two_a
  16.4 0.4 %collective-permute-start.10 = (f32[4,128,256]{2,1,0:T(8,128)S(1)}, f32[4,128,256]{2,1,0:T(8,128)S(1)}, u32[]{:S(2)}, u32[]{:S(2)}) collective-permute-start(f32[4,128,256]{2,1,0:T(8,128)S(1)} %collective-permute-done.7.two_b), channel_id=1, source_target_pairs={{0,1},{1,0},{2,3},{3,2},{4,5},{5,4},{6,7},{7,6},{8,9},{9,8},{10,11... | collective-permute-start | bytes 1572872 | tf_op jit(solution)/shard_map/ppermute | solution.py:312
  16.8 0.2 collective-permute-start.8
  17.0 0.3 collective-permute-start.9
  17.3 0.7 %copy-done.1 = s32[4,6,4]{1,2,0:T(4,128)S(1)} copy-done((s32[4,6,4]{1,2,0:T(4,128)S(1)}, s32[4,6,4]{1,2,0:T(4,128)}, u32[]{:S(2)}) %copy-start.1) | copy-done | bytes 408
  18.0 0.7 %copy-done.3 = s32[6,4]{0,1:T(4,128)S(1)} copy-done((s32[6,4]{0,1:T(4,128)S(1)}, s32[6,4]{0,1:T(4,128)}, u32[]{:S(2)}) %copy-start.3) | copy-done | bytes 120
  18.7 1.9 %first.1.begun = f32[2,2,128,128]{3,2,1,0:T(8,128)S(1)} custom-call(s32[4,6]{1,0:T(4,128)S(1)} %bitcast.10, s32[4,4,6]{2,1,0:T(4,128)S(1)} %bitcast.8, f32[4,128,256]{2,1,0:T(8,128)S(1)} %get-tuple-element.26.here, f32[4,128,256]{2,1,0:T(8,128)S(1)} %collective-permute-done.3.here2, bf16[16,64]{1,0:T(8,128)(2,1)S(1)} %dynamic-slice_bitcast_fusion.2.table, ...), custom_call_target="tpu_custom_call" | custom-call | flops 10000000 | bytes 2000000 | tf_op jit(solution)/shard_map/first/pallas_call | solution.py:349
  20.6 0.0 copy-start.2
  20.6 0.0 copy-start.4
  20.7 0.0 collective-permute-done.far
  20.7 4.0 %collective-permute-done.2.relayed = f32[2,128,256]{2,1,0:T(8,128)S(1)} collective-permute-done((f32[2,128,256]{2,1,0:T(8,128)S(1)}, f32[2,128,256]{2,1,0:T(8,128)S(1)}, u32[]{:S(2)}, u32[]{:S(2)}) %collective-permute-start.2) | collective-permute-done | bytes 262176 | tf_op jit(solution)/shard_map/ppermute | solution.py:362
  24.6 1.1 %collective-permute-start.4 = (f32[2,128,256]{2,1,0:T(8,128)S(1)}, f32[2,128,256]{2,1,0:T(8,128)S(1)}, u32[]{:S(2)}, u32[]{:S(2)}) collective-permute-start(f32[2,128,256]{2,1,0:T(8,128)S(1)} %collective-permute-done.far), channel_id=1, source_target_pairs={{0,1},{1,0},{2,3},{3,2},{4,5},{5,4},{6,7},{7,6},{8,9},{9,8},{10,11... | collective-permute-start | bytes 786440 | tf_op jit(solution)/shard_map/ppermute | solution.py:312
  25.7 0.0 collective-permute-start.5
  25.7 0.0 collective-permute-done.10.two_b2
  25.8 0.0 collective-permute-done.9.two_a2
  25.8 1.0 %spectral.1.partial = f32[4,4,2,128,128]{4,3,2,1,0:T(8,128)S(1)} custom-call(f32[4,128,256]{2,1,0:T(8,128)S(1)} %get-tuple-element.26.here, f32[4,128,256]{2,1,0:T(8,128)S(1)} %collective-permute-done.1.near, f32[4,128,256]{2,1,0:T(8,128)S(1)} %collective-permute-done.6.two_a, f32[4,128,256]{2,1,0:T(8,128)S(1)} %collective-permute-done.7.two_b, ...), custom_call_target="tpu_custom_call" | custom-call | flops 1 | bytes 1 | tf_op jit(solution)/shard_map/spectral/pallas_call | solution.py:366
  26.8 0.1 collective-permute-done.4.far2
  26.9 0.4 %collective-permute-done.5.relayed2 = f32[2,128,256]{2,1,0:T(8,128)S(1)} collective-permute-done((f32[2,128,256]{2,1,0:T(8,128)S(1)}, f32[2,128,256]{2,1,0:T(8,128)S(1)}, u32[]{:S(2)}, u32[]{:S(2)}) %collective-permute-start.5) | collective-permute-done | bytes 262176 | tf_op jit(solution)/shard_map/ppermute | solution.py:312
  27.3 7.1 %denoise.1 = f32[4,128,256]{2,1,0:T(8,128)} custom-call(s32[4,6]{1,0:T(4,128)S(1)} %bitcast.11, s32[4,4,6]{2,1,0:T(4,128)S(1)} %bitcast.9, f32[2,128,256]{2,1,0:T(8,128)S(1)} %collective-permute-done.4.far2, f32[2,128,256]{2,1,0:T(8,128)S(1)} %collective-permute-done.5.relayed2, bf16[128,32]{1,0:T(8,128)(2,1)S(1)} %dynamic-slice_bitcast_fusion.1.table, ...), custom_call_target="tpu_custom_call" | custom-call | tf_op jit(solution)/shard_map/denoise/pallas_call | solution.py:375
  (9 shorter events, 0.0 us)
Async XLA Ops:
  0.0 15.1 %collective-permute-start.1 = (f32[4,128,256]{2,1,0:T(8,128)}, f32[4,128,256]{2,1,0:T(8,128)S(1)}, u32[]{:S(2)}, u32[]{:S(2)}) collective-permute-start(f32[4,128,256]{2,1,0:T(8,128)} %cube.1), channel_id=1, source_target_pairs={{0,2},{1,3},{2,0},{3,1},{4,6},{5,7},{6,4},{7,5},{8,10},{9,11},{10,... | collective-permute-start | bytes 1572872 | tf_op jit(solution)/shard_map/ppermute | solution.py:312
  0.0 16.4 %collective-permute-start.6 = (f32[4,128,256]{2,1,0:T(8,128)}, f32[4,128,256]{2,1,0:T(8,128)S(1)}, u32[]{:S(2)}, u32[]{:S(2)}) collective-permute-start(f32[4,128,256]{2,1,0:T(8,128)} %cube.1), channel_id=1, source_target_pairs={{0,4},{1,5},{2,6},{3,7},{4,0},{5,1},{6,2},{7,3},{8,12},{9,13},{10,... | collective-permute-start | bytes 1572872 | tf_op jit(solution)/shard_map/ppermute | solution.py:312
  1.5 14.9 %collective-permute-start.7 = (f32[4,128,256]{2,1,0:T(8,128)}, f32[4,128,256]{2,1,0:T(8,128)S(1)}, u32[]{:S(2)}, u32[]{:S(2)}) collective-permute-start(f32[4,128,256]{2,1,0:T(8,128)} %cube.1), channel_id=1, source_target_pairs={{4,8},{5,9},{6,10},{7,11},{8,4},{9,5},{10,6},{11,7},{20,24},{21,25... | collective-permute-start | bytes 1572872 | tf_op jit(solution)/shard_map/ppermute | solution.py:312
  2.2 14.8 %collective-permute-start.3 = (f32[4,128,256]{2,1,0:T(8,128)}, f32[4,128,256]{2,1,0:T(8,128)S(1)}, u32[]{:S(2)}, u32[]{:S(2)}) collective-permute-start(f32[4,128,256]{2,1,0:T(8,128)} %cube.1), channel_id=1, source_target_pairs={{0,1},{1,0},{2,3},{3,2},{4,5},{5,4},{6,7},{7,6},{8,9},{9,8},{10,11... | collective-permute-start | bytes 1572872 | tf_op jit(solution)/shard_map/ppermute | solution.py:312
  6.8 13.9 %collective-permute-start = (f32[2,128,256]{2,1,0:T(8,128)S(1)}, f32[2,128,256]{2,1,0:T(8,128)S(1)}, u32[]{:S(2)}, u32[]{:S(2)}) collective-permute-start(f32[2,128,256]{2,1,0:T(8,128)S(1)} %slice.6), channel_id=1, source_target_pairs={{2,4},{3,5},{4,2},{5,3},{6,8},{7,9},{8,6},{9,7},{10,12},{11,13},{1... | collective-permute-start | bytes 786440 | tf_op jit(solution)/shard_map/ppermute | solution.py:312
  13.7 1.0 %copy-start = (f32[4,128,256]{2,1,0:T(8,128)S(1)}, f32[4,128,256]{2,1,0:T(8,128)}, u32[]{:S(2)}) copy-start(f32[4,128,256]{2,1,0:T(8,128)} %cube.1) | copy-start | bytes 1572868
  15.1 9.5 %collective-permute-start.2 = (f32[2,128,256]{2,1,0:T(8,128)S(1)}, f32[2,128,256]{2,1,0:T(8,128)S(1)}, u32[]{:S(2)}, u32[]{:S(2)}) collective-permute-start(f32[2,128,256]{2,1,0:T(8,128)S(1)} %slice.8), channel_id=1, source_target_pairs={{0,4},{1,5},{4,8},{5,9},{8,12},{9,13},{6,2},{7,3},{10,6},{11,7},{1... | collective-permute-start | bytes 786440 | tf_op jit(solution)/shard_map/ppermute | solution.py:362
  16.4 9.3 %collective-permute-start.10 = (f32[4,128,256]{2,1,0:T(8,128)S(1)}, f32[4,128,256]{2,1,0:T(8,128)S(1)}, u32[]{:S(2)}, u32[]{:S(2)}) collective-permute-start(f32[4,128,256]{2,1,0:T(8,128)S(1)} %collective-permute-done.7.two_b), channel_id=1, source_target_pairs={{0,1},{1,0},{2,3},{3,2},{4,5},{5,4},{6,7},{7,6},{8,9},{9,8},{10,11... | collective-permute-start | bytes 1572872 | tf_op jit(solution)/shard_map/ppermute | solution.py:312
  16.8 8.9 %collective-permute-start.8 = (f32[4,128,256]{2,1,0:T(8,128)S(1)}, f32[4,128,256]{2,1,0:T(8,128)S(1)}, u32[]{:S(2)}, u32[]{:S(2)}) collective-permute-start(f32[4,128,256]{2,1,0:T(8,128)S(1)} %collective-permute-done.1.near), channel_id=1, source_target_pairs={{0,1},{1,0},{2,3},{3,2},{4,5},{5,4},{6,7},{7,6},{8,9},{9,8},{10,11... | collective-permute-start | bytes 1572872 | tf_op jit(solution)/shard_map/ppermute | solution.py:312
  17.0 8.7 %collective-permute-start.9 = (f32[4,128,256]{2,1,0:T(8,128)S(1)}, f32[4,128,256]{2,1,0:T(8,128)S(1)}, u32[]{:S(2)}, u32[]{:S(2)}) collective-permute-start(f32[4,128,256]{2,1,0:T(8,128)S(1)} %collective-permute-done.6.two_a), channel_id=1, source_target_pairs={{0,1},{1,0},{2,3},{3,2},{4,5},{5,4},{6,7},{7,6},{8,9},{9,8},{10,11... | collective-permute-start | bytes 1572872 | tf_op jit(solution)/shard_map/ppermute | solution.py:312
  17.3 0.7 %copy-start.1 = (s32[4,6,4]{1,2,0:T(4,128)S(1)}, s32[4,6,4]{1,2,0:T(4,128)}, u32[]{:S(2)}) copy-start(s32[4,6,4]{1,2,0:T(4,128)} %param.8) | copy-start | bytes 1156
  18.0 0.7 %copy-start.3 = (s32[6,4]{0,1:T(4,128)S(1)}, s32[6,4]{0,1:T(4,128)}, u32[]{:S(2)}) copy-start(s32[6,4]{0,1:T(4,128)} %param.7) | copy-start | bytes 292
  20.6 6.6 %copy-start.2 = (s32[4,6,4]{1,2,0:T(4,128)S(1)}, s32[4,6,4]{1,2,0:T(4,128)}, u32[]{:S(2)}) copy-start(s32[4,6,4]{1,2,0:T(4,128)} %param.8) | copy-start | bytes 1156
  20.6 6.6 %copy-start.4 = (s32[6,4]{0,1:T(4,128)S(1)}, s32[6,4]{0,1:T(4,128)}, u32[]{:S(2)}) copy-start(s32[6,4]{0,1:T(4,128)} %param.7) | copy-start | bytes 292
  24.6 2.3 %collective-permute-start.4 = (f32[2,128,256]{2,1,0:T(8,128)S(1)}, f32[2,128,256]{2,1,0:T(8,128)S(1)}, u32[]{:S(2)}, u32[]{:S(2)}) collective-permute-start(f32[2,128,256]{2,1,0:T(8,128)S(1)} %collective-permute-done.far), channel_id=1, source_target_pairs={{0,1},{1,0},{2,3},{3,2},{4,5},{5,4},{6,7},{7,6},{8,9},{9,8},{10,11... | collective-permute-start | bytes 786440 | tf_op jit(solution)/shard_map/ppermute | solution.py:312
  25.7 1.5 %collective-permute-start.5 = (f32[2,128,256]{2,1,0:T(8,128)S(1)}, f32[2,128,256]{2,1,0:T(8,128)S(1)}, u32[]{:S(2)}, u32[]{:S(2)}) collective-permute-start(f32[2,128,256]{2,1,0:T(8,128)S(1)} %collective-permute-done.2.relayed), channel_id=1, source_target_pairs={{0,1},{1,0},{2,3},{3,2},{4,5},{5,4},{6,7},{7,6},{8,9},{9,8},{10,11... | collective-permute-start | bytes 786440 | tf_op jit(solution)/shard_map/ppermute | solution.py:312
